TPU v7x, 512 devices: a whole 4x8x8 slice. The times are simulated.
512 devices in a mesh: row: 16 (over x_lo, y), col: 32 (over x_hi, z, core).
Axes of the slice: x: 4 (x_hi: 2, x_lo: 2; x = x_hi * 2 + x_lo), y: 8, z: 8, core: 2. Of those that a mesh axis runs over, the one named last changes fastest.
Arguments:
- sensitivity: bfloat16 [24576, 16384], P('row', 'col'), may hold values from -1.5 to 1.5
- stencil_weights: float32 [4], replicated, may hold values from 0.1 to 0.6
- cell_offsets: int32 [3], replicated, may hold values from 1 to 64, as said below
- step_start: int32 [1], replicated, may hold values from 0 to 1023
Outputs:
- gram_columns: bfloat16 [32, 24576, 768], P('col', 'row')
Inputs may be any that keep to these rules, and one draw needn't show every extreme that they name: `cell_offsets`: every offset lies between 1 and 64, and one of them equals 64.
All inputs are finite; a program needn't handle non-finite values.
Results may differ from a plain program's by a relative error of at most 0.0049.
Values may be sent and summed in bfloat16 or wider, within the bound.
No kernel may reach another device: no remote copies, remote signals or barrier semaphores. Data moves between devices by JAX's collectives and lax.ppermute only.
A program may use at most 64 MiB of HBM per device.

v0:
```python
import jax
import jax.numpy as jnp
from jax import lax
from jax.sharding import PartitionSpec as P

HALO = 64
NOFF = 3
STEPS = 2


def extended(cells, sides, width):
    for axis, dim in sides:
        count = lax.axis_size(axis)
        ends = count - 1
        head = lax.slice_in_dim(cells, 0, width, axis=dim)
        tail = lax.slice_in_dim(cells, cells.shape[dim] - width, cells.shape[dim], axis=dim)
        cells = jnp.concatenate(
            [
                lax.ppermute(tail, axis, [(i, (i + 1) % count) for i in range(ends)]),
                cells,
                lax.ppermute(head, axis, [((i + 1) % count, i) for i in range(ends)]),
            ],
            axis=dim,
        )
    return cells


def from_root(shard, axis, root):
    mine = lax.axis_index(axis) == root
    return lax.psum(jnp.where(mine, shard, jnp.zeros_like(shard)), axis)


def smooth_block(window, cell_offsets, stencil_weights, width):
    widened = window.astype(jnp.float32)
    center = lax.slice_in_dim(widened, HALO, HALO + width, axis=1)
    total = stencil_weights[0] * center
    for term in range(NOFF):
        forward = lax.dynamic_slice_in_dim(widened, HALO + cell_offsets[term], width, 1)
        backward = lax.dynamic_slice_in_dim(widened, HALO - cell_offsets[term], width, 1)
        total = total + stencil_weights[term + 1] * (forward + backward)
    return total.astype(jnp.bfloat16)


def local(sensitivity, stencil_weights, cell_offsets, step_start):
    rows_dev, cells_dev = sensitivity.shape
    row_count = lax.axis_size("row")
    col_count = lax.axis_size("col")
    piece_rows = rows_dev // col_count
    row_index = lax.axis_index("row")
    first_owner = (STEPS * row_index + step_start[0]) % col_count
    padded = extended(sensitivity, (("col", 1),), HALO)
    smoothed = smooth_block(padded, cell_offsets, stencil_weights, cells_dev)
    own_rows = lax.all_to_all(sensitivity, "col", split_axis=0, concat_axis=1, tiled=True)
    cell_groups = own_rows.reshape(piece_rows, col_count, cells_dev)
    row_targets = jnp.arange(row_count, dtype=jnp.int32)
    right_blocks = []
    for step in range(STEPS):
        block_index = (STEPS * row_targets + step_start[0] + step) % col_count
        chosen = jnp.take(cell_groups, block_index, axis=1).reshape(
            piece_rows, row_count * cells_dev
        )
        right_blocks.append(lax.all_to_all(chosen, "row", split_axis=1, concat_axis=0, tiled=True))
    left_blocks = [
        from_root(smoothed, "col", (first_owner + step) % col_count) for step in range(STEPS)
    ]
    total = jnp.zeros((rows_dev, right_blocks[0].shape[0]), jnp.float32)
    for step in range(STEPS):
        total = total + lax.dot_general(
            left_blocks[step],
            right_blocks[step],
            (((1,), (1,)), ((), ())),
            preferred_element_type=jnp.float32,
        )
    return total.astype(jnp.bfloat16)[None]


def solution(mesh):
    in_specs = (P("row", "col"), P(), P(), P())
    out_specs = P("col", "row", None)
    return jax.shard_map(local, mesh=mesh, in_specs=in_specs, out_specs=out_specs, check_vma=False)
```

profile of v0, /device:TPU:1, one launch (start us, length us, event | category | flops | bytes accessed | tf_op | source)
XLA Modules:
  0.0 375.2 jit_solution(4585420477194535088)
XLA Ops:
  6.5 0.0 copy-start
  6.5 0.0 copy-start.3
  6.5 14.6 %all-to-all-start = ((bf16[32,48,512]{2,1,0:T(8,128)(2,1)}), bf16[32,48,512]{2,1,0:T(8,128)(2,1)S(1)}, u32[]{:S(2)}, u32[]{:S(2)}) async-start(bf16[32,48,512]{2,1,0:T(8,128)(2,1)} %bitcast.40), calls=%async_computation | async-start | bytes 3145728 | tf_op jit(solution)/shard_map/all_to_all | solution.py:53
  21.1 0.0 all-reduce.3.cloned.1.call-start
  21.2 0.0 copy-done
  21.2 1.1 fusion.8
  22.2 3.5 collective-permute-start
  25.8 1.9 collective-permute-start.1
  28.4 0.0 copy-done.3
  28.4 0.6 fusion.10
  36.1 0.0 copy-done.2
  36.1 0.7 fusion.9
  36.8 23.0 %collective-permute-done = bf16[1536,64]{1,0:T(8,128)(2,1)S(1)} collective-permute-done((bf16[1536,64]{1,0:T(8,128)(2,1)}, bf16[1536,64]{1,0:T(8,128)(2,1)S(1)}, u32[]{:S(2)}, u32[]{:S(2)}) %collective-permute-start) | collective-permute-done | bytes 196640 | tf_op jit(solution)/shard_map/ppermute | solution.py:19
  59.8 1.9 collective-permute-done.1
  61.7 2.0 maximum_convert_fusion
  63.7 9.4 %broadcast_select_fusion = (bf16[1536,512]{1,0:T(8,128)(2,1)}, bf16[1536,512]{1,0:T(8,128)(2,1)S(1)}) fusion(pred[]{:T(512)S(6)} %eq.14, f32[1536,640]{1,0:T(8,128)S(1)} %maximum_convert_fusion, s32[]{:T(128)S(6)} %select_n.72, s32[]{:T(128)S(6)} %select_n.71, f32[]{:T(128)} %bitcast.12, s32[]{:T(128)S(6)} %select_n.70, s32[]{:T(128)S(6)} %select_n.69, ...), kind=kLoop, calls=%fused_computation.10 | loop fusion | flops 9437184 | bytes 25165864 | tf_op jit(solution)/shard_map/jit(_where)/select_n | solution.py:30
  73.1 1.3 broadcast_select_fusion.1
  74.4 0.0 all-reduce.3.cloned.1.call-update
  74.4 0.0 all-to-all-done
  74.4 0.6 gather_fusion
  75.0 1.0 select_bitcast_fusion.1
  76.1 7.0 %all-to-all-start.1 = ((bf16[48,16,512]{2,0,1:T(8,128)(2,1)}), bf16[48,16,512]{2,0,1:T(8,128)(2,1)S(1)}, u32[]{:S(2)}, u32[]{:S(2)}) async-start(bf16[48,16,512]{2,0,1:T(8,128)(2,1)} %select_bitcast_fusion.1), calls=%async_computation.1 | async-start | bytes 1572864 | tf_op jit(solution)/shard_map/all_to_all | solution.py:62
  83.1 0.6 gather_fusion.1
  83.7 1.1 select_bitcast_fusion
  84.8 11.6 %all-to-all-done.1 = bf16[48,16,512]{2,0,1:T(8,128)(2,1)S(1)} async-done(((bf16[48,16,512]{2,0,1:T(8,128)(2,1)}), bf16[48,16,512]{2,0,1:T(8,128)(2,1)S(1)}, u32[]{:S(2)}, u32[]{:S(2)}) %all-to-all-start.1) | async-done | bytes 786464 | tf_op jit(solution)/shard_map/all_to_all | solution.py:62
  96.4 8.8 %all-to-all-start.2 = ((bf16[48,16,512]{2,0,1:T(8,128)(2,1)}), bf16[48,16,512]{2,0,1:T(8,128)(2,1)S(1)}, u32[]{:S(2)}, u32[]{:S(2)}) async-start(bf16[48,16,512]{2,0,1:T(8,128)(2,1)} %select_bitcast_fusion), calls=%async_computation.2 | async-start | bytes 1572864 | tf_op jit(solution)/shard_map/all_to_all | solution.py:62
  105.2 252.9 %all-reduce.3.cloned.1.call-done = (bf16[1536,512]{1,0:T(8,128)(2,1)}, bf16[1536,512]{1,0:T(8,128)(2,1)}) async-done(((bf16[1536,512]{1,0:T(8,128)(2,1)}, bf16[1536,512]{1,0:T(8,128)(2,1)}), (bf16[1536,512]{1,0:T(8,128)(2,1)}, bf16[1536,512]{1,0:T(8,128)(2,1)})) %all-reduce.3.cloned.1.call-update) | async-done | bytes 3145744 | tf_op jit(solution)/shard_map/psum | solution.py:30
  358.1 0.0 copy-start.1
  358.1 5.1 %fusion.11 = f32[1536,768]{1,0:T(8,128)} fusion(bf16[1536,512]{1,0:T(8,128)(2,1)} %get-tuple-element.6, bf16[768,512]{1,0:T(8,128)(2,1)S(1)} %bitcast.43), kind=kOutput, calls=%fused_computation.32 | convolution fusion | flops 1207959552 | bytes 7077888 | tf_op jit(solution)/shard_map/dot_general | solution.py:68
  363.2 0.0 all-to-all-done.2
  363.2 0.0 copy-done.1
  363.2 5.2 %fusion.4 = bf16[1,1536,768]{2,1,0:T(8,128)(2,1)} fusion(f32[1536,768]{1,0:T(8,128)} %fusion.11, bf16[1536,512]{1,0:T(8,128)(2,1)S(1)} %copy-done.1, bf16[768,512]{1,0:T(8,128)(2,1)S(1)} %bitcast.44), kind=kOutput, calls=%fused_computation.8 | convolution fusion | flops 1210318848 | bytes 9437184 | tf_op jit(solution)/shard_map/dot_general | solution.py:68
  (7 shorter events, 0.1 us)
Async XLA Ops:
  6.5 14.6 %copy-start = (bf16[1536,512]{1,0:T(8,128)(2,1)S(1)}, bf16[1536,512]{1,0:T(8,128)(2,1)}, u32[]{:S(2)}) copy-start(bf16[1536,512]{1,0:T(8,128)(2,1)} %param.6) | copy-start | bytes 4718596
  6.5 21.9 %copy-start.3 = (s32[3]{0:T(128)S(1)}, s32[3]{0:T(128)}, u32[]{:S(2)}) copy-start(s32[3]{0:T(128)} %param.8) | copy-start | bytes 40
  6.5 29.6 %copy-start.2 = (f32[4]{0:T(128)S(1)}, f32[4]{0:T(128)}, u32[]{:S(2)}) copy-start(f32[4]{0:T(128)} %param.7) | copy-start | bytes 52
  6.5 67.9 %all-to-all-start = ((bf16[32,48,512]{2,1,0:T(8,128)(2,1)}), bf16[32,48,512]{2,1,0:T(8,128)(2,1)S(1)}, u32[]{:S(2)}, u32[]{:S(2)}) async-start(bf16[32,48,512]{2,1,0:T(8,128)(2,1)} %bitcast.40), calls=%async_computation | async-start | bytes 3145728 | tf_op jit(solution)/shard_map/all_to_all | solution.py:53
  21.1 337.0 %all-reduce.3.cloned.1.call-start = ((), (), s32[]{:S(2)}) async-start(), calls=%async_computation.3 | async-start | bytes 6291456 | tf_op jit(solution)/shard_map/psum | solution.py:30
  22.2 37.6 %collective-permute-start = (bf16[1536,64]{1,0:T(8,128)(2,1)}, bf16[1536,64]{1,0:T(8,128)(2,1)S(1)}, u32[]{:S(2)}, u32[]{:S(2)}) collective-permute-start(bf16[1536,64]{1,0:T(8,128)(2,1)} %get-tuple-element.10), channel_id=1, source_target_pairs={{0,1},{1,2},{2,3},{3,4},{4,5},{5,6},{6,7},{7,8},{8,9},{9,10},{10,1... | collective-permute-start | bytes 589832 | tf_op jit(solution)/shard_map/ppermute | solution.py:19
  25.8 35.9 %collective-permute-start.1 = (bf16[1536,64]{1,0:T(8,128)(2,1)}, bf16[1536,64]{1,0:T(8,128)(2,1)}, u32[]{:S(2)}, u32[]{:S(2)}) collective-permute-start(bf16[1536,64]{1,0:T(8,128)(2,1)} %get-tuple-element.11), channel_id=1, source_target_pairs={{1,0},{2,1},{3,2},{4,3},{5,4},{6,5},{7,6},{8,7},{9,8},{10,9},{11,1... | collective-permute-start | bytes 589832 | tf_op jit(solution)/shard_map/ppermute | solution.py:21
  76.1 20.3 %all-to-all-start.1 = ((bf16[48,16,512]{2,0,1:T(8,128)(2,1)}), bf16[48,16,512]{2,0,1:T(8,128)(2,1)S(1)}, u32[]{:S(2)}, u32[]{:S(2)}) async-start(bf16[48,16,512]{2,0,1:T(8,128)(2,1)} %select_bitcast_fusion.1), calls=%async_computation.1 | async-start | bytes 1572864 | tf_op jit(solution)/shard_map/all_to_all | solution.py:62
  96.4 266.8 %all-to-all-start.2 = ((bf16[48,16,512]{2,0,1:T(8,128)(2,1)}), bf16[48,16,512]{2,0,1:T(8,128)(2,1)S(1)}, u32[]{:S(2)}, u32[]{:S(2)}) async-start(bf16[48,16,512]{2,0,1:T(8,128)(2,1)} %select_bitcast_fusion), calls=%async_computation.2 | async-start | bytes 1572864 | tf_op jit(solution)/shard_map/all_to_all | solution.py:62
  358.1 5.1 %copy-start.1 = (bf16[1536,512]{1,0:T(8,128)(2,1)S(1)}, bf16[1536,512]{1,0:T(8,128)(2,1)}, u32[]{:S(2)}) copy-start(bf16[1536,512]{1,0:T(8,128)(2,1)} %get-tuple-element.7) | copy-start | bytes 4718596
Sparse Core Ops, SparseCore 0:
  74.5 283.5 all-reduce.2
where the time goes:
time: 376 us; the launch traced here: 375 us
  waiting for transfers between devices  289 us (77%)
  starting transfers between devices  35.8 us (10%)
  between operations  21.3 us (6%)
  other arithmetic  14.8 us (4%)
  matrix products  10.2 us (3%)
    psum x1, waiting for transfers between devices, from_root(): return lax.psum(jnp.where(mine, shard, jnp.zeros_like(shard)), axis)  253 us
    ppermute x1, waiting for transfers between devices, extended(): lax.ppermute(tail, axis, [(i, (i + 1) % count) for i in range(ends)])  23 us
    all_to_all x2, starting transfers between devices, local(): lax.all_to_all(chosen, 'row', split_axis=1, concat_axis=0, tiled=True)  15.8 us
    all_to_all x1, starting transfers between devices, local(): lax.all_to_all(sensitivity, 'col', split_axis=0, concat_axis=1, tiled=True)  14.6 us
    all_to_all x2, waiting for transfers between devices, local(): lax.all_to_all(chosen, 'row', split_axis=1, concat_axis=0, tiled=True)  11.6 us
    select_n x2, other arithmetic, from_root(): return lax.psum(jnp.where(mine, shard, jnp.zeros_like(shard)), axis)  10.7 us
    dot_general x2, matrix products, local(): lax.dot_general(left_blocks[step], right_blocks[step], (((1,), (1,)), (()...  10.2 us
  transfers between devices with their start and end apart: 6, of which 4 were waited for; matrix products, arithmetic and copies ran while one was open for 6% of the time, Pallas kernels for 0%

commit v1 on v0

v1 whole, which is shorter than its diff:
```python
import jax
import jax.numpy as jnp
from jax import lax
from jax.experimental import pallas as pl
from jax.experimental.pallas import tpu as pltpu
from jax.sharding import PartitionSpec as P

HALO = 64
NOFF = 3
STEPS = 2
N_XH = 2
N_Z = 8
N_C = 2
LANE = 128
VMEM_LIMIT = 20 * 1024 * 1024


def select_kernel(start_ref, offsets_ref, weights_ref, own_ref, chosen_ref, piece_ref, window, sem, wsem):
    count, rows, cells = own_ref.shape
    start = lax.rem(start_ref[0], count)
    copies = []
    first = lax.rem(STEPS * lax.axis_index("row") + start, count)
    for j in range(4):
        block = lax.rem(first + (j - 1 + count), count)
        copy = pltpu.make_async_copy(own_ref.at[block], window.at[j], wsem.at[j])
        copy.start()
        copies.append(copy)
    moves = []
    for t in range(count):
        block = lax.rem(t + start, count)
        move = pltpu.make_async_copy(own_ref.at[block], chosen_ref.at[t // STEPS, t % STEPS], sem.at[t])
        move.start()
        moves.append(move)
    for copy in copies:
        copy.wait()
    for s in range(STEPS):
        here = lax.rem(first + s, count)
        before = jnp.where(here > 0, window[s][:, cells - LANE:].astype(jnp.float32), 0.0)
        after = jnp.where(here < count - 1, window[s + 2][:, :LANE].astype(jnp.float32), 0.0)
        center = window[s + 1].astype(jnp.float32)
        wide = jnp.concatenate([before, center, after], axis=1)
        width = cells + 2 * LANE
        total = weights_ref[0] * center
        for m in range(NOFF):
            offset = offsets_ref[m]
            forward = pltpu.roll(wide, width - offset, 1)[:, LANE:LANE + cells]
            backward = pltpu.roll(wide, offset, 1)[:, LANE:LANE + cells]
            total = total + weights_ref[m + 1] * (forward + backward)
        piece_ref[:, s * cells:(s + 1) * cells] = total.astype(jnp.bfloat16)
    for move in moves:
        move.wait()


def select(own, stencil_weights, cell_offsets, step_start):
    count, rows, cells = own.shape
    smem = pl.BlockSpec(memory_space=pltpu.SMEM)
    return pl.pallas_call(
        select_kernel,
        out_shape=(
            jax.ShapeDtypeStruct((count // STEPS, STEPS, rows, cells), own.dtype),
            jax.ShapeDtypeStruct((rows, STEPS * cells), own.dtype),
        ),
        in_specs=[smem, smem, smem, pl.BlockSpec(memory_space=pl.ANY)],
        out_specs=(pl.BlockSpec(memory_space=pl.ANY), pl.BlockSpec(memory_space=pltpu.VMEM)),
        scratch_shapes=[
            pltpu.VMEM((4, rows, cells), own.dtype),
            pltpu.SemaphoreType.DMA((count,)),
            pltpu.SemaphoreType.DMA((4,)),
        ],
    )(step_start, cell_offsets, stencil_weights, own)


def gram_kernel(*refs):
    pieces, right_ref, out_ref, left, right, sem, rsem = refs[:9], refs[9], refs[10], *refs[11:]
    tile = pl.program_id(0)
    tile_rows = out_ref.shape[0]
    cells = right.shape[3]
    piece = pieces[0].shape[-2]

    def copies():
        column = lax.axis_index("col")
        xh = column // (N_Z * N_C)
        z = lax.rem(column // N_C, N_Z)
        core = lax.rem(column, N_C)
        up = 1 - 2 * core
        made = []
        n = 0
        for index, ref in enumerate(pieces):
            hop = index if index < 5 else index - 4
            side = 0 if index < 5 else 1
            toward = up if side == 0 else -up
            source_z = lax.rem(z - hop * toward + N_Z, N_Z)
            source_core = core if side == 0 else 1 - core
            for rc in range(N_C if hop < 4 else 1):
                for rx in range(N_XH):
                    from_core = source_core if rc == 0 else 1 - source_core
                    from_xh = xh if rx == 0 else 1 - xh
                    place = (from_xh * N_Z + source_z) * N_C + from_core
                    source = ref.at[rc, rx] if hop < 4 else ref.at[rx]
                    target = left.at[pl.ds(pl.multiple_of(place * piece, piece), piece)]
                    made.append(pltpu.make_async_copy(source, target, sem.at[n]))
                    n += 1
        for s in range(STEPS):
            made.append(pltpu.make_async_copy(right_ref.at[:, s], right.at[s], rsem.at[s]))
        return made

    @pl.when(tile == 0)
    def _():
        made = copies()
        for copy in made:
            copy.start()
        for copy in made:
            copy.wait()

    rows = left[pl.ds(pl.multiple_of(tile * tile_rows, tile_rows), tile_rows), :]
    total = None
    for s in range(STEPS):
        columns = right[s].reshape(-1, cells)
        part = lax.dot_general(
            rows[:, s * cells:(s + 1) * cells], columns,
            (((1,), (1,)), ((), ())), preferred_element_type=jnp.float32,
        )
        total = part if total is None else total + part
    out_ref[...] = total.astype(out_ref.dtype)


def gram(pieces, right, rows_dev):
    row_count, steps, piece, cells = right.shape
    width = row_count * piece
    tiles = 4
    return pl.pallas_call(
        gram_kernel,
        out_shape=jax.ShapeDtypeStruct((rows_dev, width), jnp.bfloat16),
        grid=(tiles,),
        in_specs=[pl.BlockSpec(memory_space=pl.ANY)] * 10,
        out_specs=pl.BlockSpec((rows_dev // tiles, width), lambda t: (t, 0)),
        scratch_shapes=[
            pltpu.VMEM((rows_dev, steps * cells), jnp.bfloat16),
            pltpu.VMEM((steps, row_count, piece, cells), jnp.bfloat16),
            pltpu.SemaphoreType.DMA((32,)),
            pltpu.SemaphoreType.DMA((steps,)),
        ],
        compiler_params=pltpu.CompilerParams(vmem_limit_bytes=VMEM_LIMIT),
    )(*pieces, right)


def place(xh, z, core):
    return ((xh % N_XH) * N_Z + z % N_Z) * N_C + core % N_C


PLACES = [(xh, z, core) for xh in range(N_XH) for z in range(N_Z) for core in range(N_C)]
SWAP_X = [(place(x, z, c), place(x + 1, z, c)) for x, z, c in PLACES]
SWAP_CORE = [(place(x, z, c), place(x, z, c + 1)) for x, z, c in PLACES]
RING = [(place(x, z, c), place(x, z + 1 - 2 * c, c)) for x, z, c in PLACES]


def gather_left(piece):
    both_x = jnp.stack([piece, lax.ppermute(piece, "col", SWAP_X)])
    base = jnp.stack([both_x, lax.ppermute(both_x, "col", SWAP_CORE)])
    held, other = [], []
    block = base
    for hop in range(1, 5):
        block = lax.ppermute(block if hop < 4 else block[0], "col", RING)
        held.append(block)
        other.append(lax.ppermute(block, "col", SWAP_CORE))
    return [base] + held + other


def local(sensitivity, stencil_weights, cell_offsets, step_start):
    rows_dev, cells_dev = sensitivity.shape
    col_count = lax.axis_size("col")
    piece_rows = rows_dev // col_count
    blocks = sensitivity.reshape(col_count, piece_rows, cells_dev)
    own = lax.all_to_all(blocks, "col", split_axis=0, concat_axis=0, tiled=True)
    chosen, piece = select(own, stencil_weights, cell_offsets, step_start)
    right = lax.all_to_all(chosen, "row", split_axis=0, concat_axis=0, tiled=True)
    pieces = gather_left(piece)
    return gram(pieces, right, rows_dev)[None]


def solution(mesh):
    in_specs = (P("row", "col"), P(), P(), P())
    out_specs = P("col", "row", None)
    return jax.shard_map(local, mesh=mesh, in_specs=in_specs, out_specs=out_specs, check_vma=False)
```

time: 376 us -> 190 us (0.51)
  waiting for transfers between devices: 289 us -> 56.1 us
  Pallas kernels: 0 us -> 59.8 us
  starting transfers between devices: 35.8 us -> 63.3 us
  between operations: 21.3 us -> 0.82 us
  other arithmetic: 14.8 us -> 0.07 us
  matrix products: 10.2 us -> 0 us
  local copies, waits for them, and re-layouts: 3.53 us -> 7.86 us
    psum x1 -> x0, waiting for transfers between devices: 253 us -> none  [from_root(): return lax.psum(jnp.where(mine, shard, jnp.zeros_like(shard)), axis)]
    pallas_call x0 -> x2, Pallas kernels: none -> 59.8 us  [the longest x1 50.4 us: select(): pl.pallas_call(select_kernel, out_shape=(jax.ShapeDtypeStruct((count // S...]
    ppermute x2 -> x10, starting transfers between devices: 5.45 us -> 41.8 us  [the longest x4 16.1 us: gather_left(): other.append(lax.ppermute(block, 'col', SWAP_CORE))]
    all_to_all x3 -> x2, waiting for transfers between devices: 11.6 us -> 39.2 us  [the longest x1 39.2 us: local(): own = lax.all_to_all(blocks, 'col', split_axis=0, concat_axis=0, tiled=True)]
    select_n x6 -> x0, other arithmetic: 12.8 us -> none  [the longest x2 10.7 us: from_root(): return lax.psum(jnp.where(mine, shard, jnp.zeros_like(shard)), axis)]
    dot_general x2 -> x0, matrix products: 10.2 us -> none  [local(): lax.dot_general(left_blocks[step], right_blocks[step], (((1,), (1,)), (()...]
    all_to_all x3 -> x2, starting transfers between devices: 30.3 us -> 21.5 us  [the longest x1 14.4 us: local(): own = lax.all_to_all(blocks, 'col', split_axis=0, concat_axis=0, tiled=True)]
    ppermute x2 -> x10, waiting for transfers between devices: 24.9 us -> 16.9 us  [the longest x4 12.5 us: gather_left(): block = lax.ppermute(block if hop < 4 else block[0], 'col', RING)]
  transfers between devices with their start and end apart: 6 -> 12, of which waited for: 4 -> 5; matrix products, arithmetic and copies ran while one was open for 6% -> 0% of each run, Pallas kernels for 0% -> 0%
where the time goes in v1:
time: 190 us; the launch traced here: 188 us
  starting transfers between devices  63.3 us (33%)
  Pallas kernels  59.8 us (31%)
  waiting for transfers between devices  56.1 us (30%)
  local copies, waits for them, and re-layouts  7.86 us (4%)
    pallas_call x1, Pallas kernels, select(): pl.pallas_call(select_kernel, out_shape=(jax.ShapeDtypeStruct((count // S...  50.4 us
    all_to_all x1, waiting for transfers between devices, local(): own = lax.all_to_all(blocks, 'col', split_axis=0, concat_axis=0, tiled=True)  39.2 us
    ppermute x4, starting transfers between devices, gather_left(): other.append(lax.ppermute(block, 'col', SWAP_CORE))  16.1 us
    ppermute x4, starting transfers between devices, gather_left(): block = lax.ppermute(block if hop < 4 else block[0], 'col', RING)  15 us
    all_to_all x1, starting transfers between devices, local(): own = lax.all_to_all(blocks, 'col', split_axis=0, concat_axis=0, tiled=True)  14.4 us
    ppermute x4, waiting for transfers between devices, gather_left(): block = lax.ppermute(block if hop < 4 else block[0], 'col', RING)  12.5 us
    pallas_call x1, Pallas kernels, gram(): pl.pallas_call(gram_kernel, out_shape=jax.ShapeDtypeStruct((rows_dev, wid...  9.39 us
    unnamed x20, local copies, waits for them, and re-layouts  7.85 us
  transfers between devices with their start and end apart: 12, of which 5 were waited for; matrix products, arithmetic and copies ran while one was open for 0% of the time, Pallas kernels for 0%

profile of v1, /device:TPU:1, one launch (start us, length us, event | category | flops | bytes accessed | tf_op | source)
XLA Modules:
  0.0 188.0 jit_solution(4902239532209149541)
XLA Ops:
  0.0 14.4 %all-to-all-start = ((bf16[32,48,512]{2,1,0:T(8,128)(2,1)}), bf16[32,48,512]{2,1,0:T(8,128)(2,1)S(1)}, u32[]{:S(2)}, u32[]{:S(2)}) async-start(bf16[32,48,512]{2,1,0:T(8,128)(2,1)} %bitcast.9), calls=%async_computation | async-start | bytes 3145728 | tf_op jit(solution)/shard_map/all_to_all | solution.py:174
  15.1 39.2 %all-to-all-done.own_ref = bf16[32,48,512]{2,1,0:T(8,128)(2,1)S(1)} async-done(((bf16[32,48,512]{2,1,0:T(8,128)(2,1)}), bf16[32,48,512]{2,1,0:T(8,128)(2,1)S(1)}, u32[]{:S(2)}, u32[]{:S(2)}) %all-to-all-start) | async-done | bytes 1572896 | tf_op jit(solution)/shard_map/all_to_all | solution.py:174
  54.3 1.1 copy-done.8
  55.4 50.4 %shard_map.46 = (bf16[16,2,48,512]{3,2,1,0:T(8,128)(2,1)}, bf16[48,1024]{1,0:T(8,128)(2,1)}) custom-call(s32[1]{0:T(128)S(6)} %copy.5.start_ref, s32[3]{0:T(128)} %offsets_ref.1, f32[4]{0:T(128)} %weights_ref.1, bf16[32,48,512]{2,1,0:T(8,128)(2,1)} %copy-done.8), custom_call_target="tpu_custom_call" | custom-call | tf_op jit(solution)/shard_map/pallas_call | solution.py:57
  105.8 7.1 %all-to-all-start.1 = ((bf16[16,2,48,512]{3,2,1,0:T(8,128)(2,1)}), bf16[16,2,48,512]{3,2,1,0:T(8,128)(2,1)S(1)}, u32[]{:S(2)}, u32[]{:S(2)}) async-start(bf16[16,2,48,512]{3,2,1,0:T(8,128)(2,1)} %get-tuple-element.8), calls=%async_computation.1 | async-start | bytes 3145728 | tf_op jit(solution)/shard_map/all_to_all | solution.py:176
  112.9 3.5 %collective-permute-start = (bf16[48,1024]{1,0:T(8,128)(2,1)S(1)}, bf16[48,1024]{1,0:T(8,128)(2,1)S(1)}, u32[]{:S(2)}, u32[]{:S(2)}) collective-permute-start(bf16[48,1024]{1,0:T(8,128)(2,1)S(1)} %copy-done.9), channel_id=1, source_target_pairs={{0,16},{1,17},{2,18},{3,19},{4,20},{5,21},{6,22},{7,23},{8,24},{9,... | collective-permute-start | bytes 294920 | tf_op jit(solution)/shard_map/ppermute | solution.py:158
  116.4 3.4 %collective-permute-done = bf16[48,1024]{1,0:T(8,128)(2,1)S(1)} collective-permute-done((bf16[48,1024]{1,0:T(8,128)(2,1)S(1)}, bf16[48,1024]{1,0:T(8,128)(2,1)S(1)}, u32[]{:S(2)}, u32[]{:S(2)}) %collective-permute-start) | collective-permute-done | bytes 98336 | tf_op jit(solution)/shard_map/ppermute | solution.py:158
  119.8 7.2 %collective-permute-start.1 = (bf16[2,48,1024]{2,1,0:T(8,128)(2,1)S(1)}, bf16[2,48,1024]{2,1,0:T(8,128)(2,1)S(1)}, u32[]{:S(2)}, u32[]{:S(2)}) collective-permute-start(bf16[2,48,1024]{2,1,0:T(8,128)(2,1)S(1)} %get-tuple-element.10), channel_id=1, source_target_pairs={{0,1},{1,0},{2,3},{3,2},{4,5},{5,4},{6,7},{7,6},{8,9},{9,8},{10,11... | collective-permute-start | bytes 589832 | tf_op jit(solution)/shard_map/ppermute | solution.py:159
  127.1 1.0 collective-permute-done.1
  128.2 2.6 %collective-permute-start.2 = (bf16[2,2,48,1024]{3,2,1,0:T(8,128)(2,1)S(1)}, bf16[2,2,48,1024]{3,2,1,0:T(8,128)(2,1)S(1)}, u32[]{:S(2)}, u32[]{:S(2)}) collective-permute-start(bf16[2,2,48,1024]{3,2,1,0:T(8,128)(2,1)S(1)} %pad_maximum_fusion.refs_0_), channel_id=1, source_target_pairs={{0,2},{1,15},{2,4},{3,1},{4,6},{5,3},{6,8},{7,5},{8,10},{9,7},{10,... | collective-permute-start | bytes 1179656 | tf_op jit(solution)/shard_map/ppermute | solution.py:163
  130.8 6.8 %collective-permute-done.2.refs_1_ = bf16[2,2,48,1024]{3,2,1,0:T(8,128)(2,1)S(1)} collective-permute-done((bf16[2,2,48,1024]{3,2,1,0:T(8,128)(2,1)S(1)}, bf16[2,2,48,1024]{3,2,1,0:T(8,128)(2,1)S(1)}, u32[]{:S(2)}, u32[]{:S(2)}) %collective-permute-start.2) | collective-permute-done | bytes 393248 | tf_op jit(solution)/shard_map/ppermute | solution.py:163
  137.6 3.2 %collective-permute-start.3 = (bf16[2,2,48,1024]{3,2,1,0:T(8,128)(2,1)S(1)}, bf16[2,2,48,1024]{3,2,1,0:T(8,128)(2,1)S(1)}, u32[]{:S(2)}, u32[]{:S(2)}) collective-permute-start(bf16[2,2,48,1024]{3,2,1,0:T(8,128)(2,1)S(1)} %collective-permute-done.2.refs_1_), channel_id=1, source_target_pairs={{0,2},{1,15},{2,4},{3,1},{4,6},{5,3},{6,8},{7,5},{8,10},{9,7},{10,... | collective-permute-start | bytes 1179656 | tf_op jit(solution)/shard_map/ppermute | solution.py:163
  140.8 5.6 %collective-permute-done.3.refs_2_ = bf16[2,2,48,1024]{3,2,1,0:T(8,128)(2,1)S(1)} collective-permute-done((bf16[2,2,48,1024]{3,2,1,0:T(8,128)(2,1)S(1)}, bf16[2,2,48,1024]{3,2,1,0:T(8,128)(2,1)S(1)}, u32[]{:S(2)}, u32[]{:S(2)}) %collective-permute-start.3) | collective-permute-done | bytes 393248 | tf_op jit(solution)/shard_map/ppermute | solution.py:163
  146.4 4.4 %collective-permute-start.4 = (bf16[2,2,48,1024]{3,2,1,0:T(8,128)(2,1)S(1)}, bf16[2,2,48,1024]{3,2,1,0:T(8,128)(2,1)S(1)}, u32[]{:S(2)}, u32[]{:S(2)}) collective-permute-start(bf16[2,2,48,1024]{3,2,1,0:T(8,128)(2,1)S(1)} %collective-permute-done.3.refs_2_), channel_id=1, source_target_pairs={{0,2},{1,15},{2,4},{3,1},{4,6},{5,3},{6,8},{7,5},{8,10},{9,7},{10,... | collective-permute-start | bytes 1179656 | tf_op jit(solution)/shard_map/ppermute | solution.py:163
  150.8 3.3 %collective-permute-start.6 = (bf16[2,2,48,1024]{3,2,1,0:T(8,128)(2,1)S(1)}, bf16[2,2,48,1024]{3,2,1,0:T(8,128)(2,1)S(1)}, u32[]{:S(2)}, u32[]{:S(2)}) collective-permute-start(bf16[2,2,48,1024]{3,2,1,0:T(8,128)(2,1)S(1)} %collective-permute-done.2.refs_1_), channel_id=1, source_target_pairs={{0,1},{1,0},{2,3},{3,2},{4,5},{5,4},{6,7},{7,6},{8,9},{9,8},{10,11... | collective-permute-start | bytes 1179656 | tf_op jit(solution)/shard_map/ppermute | solution.py:165
  154.1 1.9 %collective-permute-start.7 = (bf16[2,2,48,1024]{3,2,1,0:T(8,128)(2,1)S(1)}, bf16[2,2,48,1024]{3,2,1,0:T(8,128)(2,1)S(1)}, u32[]{:S(2)}, u32[]{:S(2)}) collective-permute-start(bf16[2,2,48,1024]{3,2,1,0:T(8,128)(2,1)S(1)} %collective-permute-done.3.refs_2_), channel_id=1, source_target_pairs={{0,1},{1,0},{2,3},{3,2},{4,5},{5,4},{6,7},{7,6},{8,9},{9,8},{10,11... | collective-permute-start | bytes 1179656 | tf_op jit(solution)/shard_map/ppermute | solution.py:165
  156.1 0.0 collective-permute-done.4.refs_3_
  156.1 4.9 %collective-permute-start.5 = (bf16[2,48,1024]{2,1,0:T(8,128)(2,1)S(1)}, bf16[2,48,1024]{2,1,0:T(8,128)(2,1)S(1)}, u32[]{:S(2)}, u32[]{:S(2)}) collective-permute-start(bf16[2,48,1024]{2,1,0:T(8,128)(2,1)S(1)} %slice_bitcast_fusion), channel_id=1, source_target_pairs={{0,2},{1,15},{2,4},{3,1},{4,6},{5,3},{6,8},{7,5},{8,10},{9,7},{10,... | collective-permute-start | bytes 589832 | tf_op jit(solution)/shard_map/ppermute | solution.py:163
  160.9 4.1 %collective-permute-start.8 = (bf16[2,2,48,1024]{3,2,1,0:T(8,128)(2,1)S(1)}, bf16[2,2,48,1024]{3,2,1,0:T(8,128)(2,1)S(1)}, u32[]{:S(2)}, u32[]{:S(2)}) collective-permute-start(bf16[2,2,48,1024]{3,2,1,0:T(8,128)(2,1)S(1)} %collective-permute-done.4.refs_3_), channel_id=1, source_target_pairs={{0,1},{1,0},{2,3},{3,2},{4,5},{5,4},{6,7},{7,6},{8,9},{9,8},{10,11... | collective-permute-start | bytes 1179656 | tf_op jit(solution)/shard_map/ppermute | solution.py:165
  165.0 0.0 collective-permute-done.5.refs_4_
  165.0 6.8 %collective-permute-start.9 = (bf16[2,48,1024]{2,1,0:T(8,128)(2,1)S(1)}, bf16[2,48,1024]{2,1,0:T(8,128)(2,1)S(1)}, u32[]{:S(2)}, u32[]{:S(2)}) collective-permute-start(bf16[2,48,1024]{2,1,0:T(8,128)(2,1)S(1)} %collective-permute-done.5.refs_4_), channel_id=1, source_target_pairs={{0,1},{1,0},{2,3},{3,2},{4,5},{5,4},{6,7},{7,6},{8,9},{9,8},{10,11... | collective-permute-start | bytes 589832 | tf_op jit(solution)/shard_map/ppermute | solution.py:165
  171.9 0.7 copy-done.4
  172.5 0.0 collective-permute-done.6.refs_5_
  172.5 0.0 collective-permute-done.7.refs_6_
  172.5 0.7 copy-done
  173.3 0.7 copy-done.6
  174.0 0.8 copy-done.2
  174.7 1.0 copy-done.1
  175.7 1.0 copy-done.3
  176.7 0.9 copy-done.5
  177.7 0.9 copy-done.7
  178.6 9.4 %shard_map.47 = bf16[1536,768]{1,0:T(8,128)(2,1)} custom-call(bf16[2,2,48,1024]{3,2,1,0:T(8,128)(2,1)S(1)} %pad_maximum_fusion.refs_0_, bf16[2,2,48,1024]{3,2,1,0:T(8,128)(2,1)S(1)} %collective-permute-done.2.refs_1_, bf16[2,2,48,1024]{3,2,1,0:T(8,128)(2,1)S(1)} %collective-permute-done.3.refs_2_, ...), custom_call_target="tpu_custom_call" | custom-call | tf_op jit(solution)/shard_map/pallas_call | solution.py:131
  (17 shorter events, 0.1 us)
Async XLA Ops:
  0.0 54.3 %all-to-all-start = ((bf16[32,48,512]{2,1,0:T(8,128)(2,1)}), bf16[32,48,512]{2,1,0:T(8,128)(2,1)S(1)}, u32[]{:S(2)}, u32[]{:S(2)}) async-start(bf16[32,48,512]{2,1,0:T(8,128)(2,1)} %bitcast.9), calls=%async_computation | async-start | bytes 3145728 | tf_op jit(solution)/shard_map/all_to_all | solution.py:174
  54.3 1.1 copy-start.8
  105.8 7.1 %copy-start.9 = (bf16[48,1024]{1,0:T(8,128)(2,1)S(1)}, bf16[48,1024]{1,0:T(8,128)(2,1)}, u32[]{:S(2)}) copy-start(bf16[48,1024]{1,0:T(8,128)(2,1)} %get-tuple-element.7) | copy-start | bytes 294916
  105.8 68.9 %all-to-all-start.1 = ((bf16[16,2,48,512]{3,2,1,0:T(8,128)(2,1)}), bf16[16,2,48,512]{3,2,1,0:T(8,128)(2,1)S(1)}, u32[]{:S(2)}, u32[]{:S(2)}) async-start(bf16[16,2,48,512]{3,2,1,0:T(8,128)(2,1)} %get-tuple-element.8), calls=%async_computation.1 | async-start | bytes 3145728 | tf_op jit(solution)/shard_map/all_to_all | solution.py:176
  112.9 6.9 %collective-permute-start = (bf16[48,1024]{1,0:T(8,128)(2,1)S(1)}, bf16[48,1024]{1,0:T(8,128)(2,1)S(1)}, u32[]{:S(2)}, u32[]{:S(2)}) collective-permute-start(bf16[48,1024]{1,0:T(8,128)(2,1)S(1)} %copy-done.9), channel_id=1, source_target_pairs={{0,16},{1,17},{2,18},{3,19},{4,20},{5,21},{6,22},{7,23},{8,24},{9,... | collective-permute-start | bytes 294920 | tf_op jit(solution)/shard_map/ppermute | solution.py:158
  119.8 8.3 %collective-permute-start.1 = (bf16[2,48,1024]{2,1,0:T(8,128)(2,1)S(1)}, bf16[2,48,1024]{2,1,0:T(8,128)(2,1)S(1)}, u32[]{:S(2)}, u32[]{:S(2)}) collective-permute-start(bf16[2,48,1024]{2,1,0:T(8,128)(2,1)S(1)} %get-tuple-element.10), channel_id=1, source_target_pairs={{0,1},{1,0},{2,3},{3,2},{4,5},{5,4},{6,7},{7,6},{8,9},{9,8},{10,11... | collective-permute-start | bytes 589832 | tf_op jit(solution)/shard_map/ppermute | solution.py:159
  128.2 9.4 %collective-permute-start.2 = (bf16[2,2,48,1024]{3,2,1,0:T(8,128)(2,1)S(1)}, bf16[2,2,48,1024]{3,2,1,0:T(8,128)(2,1)S(1)}, u32[]{:S(2)}, u32[]{:S(2)}) collective-permute-start(bf16[2,2,48,1024]{3,2,1,0:T(8,128)(2,1)S(1)} %pad_maximum_fusion.refs_0_), channel_id=1, source_target_pairs={{0,2},{1,15},{2,4},{3,1},{4,6},{5,3},{6,8},{7,5},{8,10},{9,7},{10,... | collective-permute-start | bytes 1179656 | tf_op jit(solution)/shard_map/ppermute | solution.py:163
  137.6 8.8 %collective-permute-start.3 = (bf16[2,2,48,1024]{3,2,1,0:T(8,128)(2,1)S(1)}, bf16[2,2,48,1024]{3,2,1,0:T(8,128)(2,1)S(1)}, u32[]{:S(2)}, u32[]{:S(2)}) collective-permute-start(bf16[2,2,48,1024]{3,2,1,0:T(8,128)(2,1)S(1)} %collective-permute-done.2.refs_1_), channel_id=1, source_target_pairs={{0,2},{1,15},{2,4},{3,1},{4,6},{5,3},{6,8},{7,5},{8,10},{9,7},{10,... | collective-permute-start | bytes 1179656 | tf_op jit(solution)/shard_map/ppermute | solution.py:163
  146.4 9.7 %collective-permute-start.4 = (bf16[2,2,48,1024]{3,2,1,0:T(8,128)(2,1)S(1)}, bf16[2,2,48,1024]{3,2,1,0:T(8,128)(2,1)S(1)}, u32[]{:S(2)}, u32[]{:S(2)}) collective-permute-start(bf16[2,2,48,1024]{3,2,1,0:T(8,128)(2,1)S(1)} %collective-permute-done.3.refs_2_), channel_id=1, source_target_pairs={{0,2},{1,15},{2,4},{3,1},{4,6},{5,3},{6,8},{7,5},{8,10},{9,7},{10,... | collective-permute-start | bytes 1179656 | tf_op jit(solution)/shard_map/ppermute | solution.py:163
  150.8 21.7 %collective-permute-start.6 = (bf16[2,2,48,1024]{3,2,1,0:T(8,128)(2,1)S(1)}, bf16[2,2,48,1024]{3,2,1,0:T(8,128)(2,1)S(1)}, u32[]{:S(2)}, u32[]{:S(2)}) collective-permute-start(bf16[2,2,48,1024]{3,2,1,0:T(8,128)(2,1)S(1)} %collective-permute-done.2.refs_1_), channel_id=1, source_target_pairs={{0,1},{1,0},{2,3},{3,2},{4,5},{5,4},{6,7},{7,6},{8,9},{9,8},{10,11... | collective-permute-start | bytes 1179656 | tf_op jit(solution)/shard_map/ppermute | solution.py:165
  154.1 18.4 %collective-permute-start.7 = (bf16[2,2,48,1024]{3,2,1,0:T(8,128)(2,1)S(1)}, bf16[2,2,48,1024]{3,2,1,0:T(8,128)(2,1)S(1)}, u32[]{:S(2)}, u32[]{:S(2)}) collective-permute-start(bf16[2,2,48,1024]{3,2,1,0:T(8,128)(2,1)S(1)} %collective-permute-done.3.refs_2_), channel_id=1, source_target_pairs={{0,1},{1,0},{2,3},{3,2},{4,5},{5,4},{6,7},{7,6},{8,9},{9,8},{10,11... | collective-permute-start | bytes 1179656 | tf_op jit(solution)/shard_map/ppermute | solution.py:165
  156.1 8.9 %collective-permute-start.5 = (bf16[2,48,1024]{2,1,0:T(8,128)(2,1)S(1)}, bf16[2,48,1024]{2,1,0:T(8,128)(2,1)S(1)}, u32[]{:S(2)}, u32[]{:S(2)}) collective-permute-start(bf16[2,48,1024]{2,1,0:T(8,128)(2,1)S(1)} %slice_bitcast_fusion), channel_id=1, source_target_pairs={{0,2},{1,15},{2,4},{3,1},{4,6},{5,3},{6,8},{7,5},{8,10},{9,7},{10,... | collective-permute-start | bytes 589832 | tf_op jit(solution)/shard_map/ppermute | solution.py:163
  160.9 13.0 %collective-permute-start.8 = (bf16[2,2,48,1024]{3,2,1,0:T(8,128)(2,1)S(1)}, bf16[2,2,48,1024]{3,2,1,0:T(8,128)(2,1)S(1)}, u32[]{:S(2)}, u32[]{:S(2)}) collective-permute-start(bf16[2,2,48,1024]{3,2,1,0:T(8,128)(2,1)S(1)} %collective-permute-done.4.refs_3_), channel_id=1, source_target_pairs={{0,1},{1,0},{2,3},{3,2},{4,5},{5,4},{6,7},{7,6},{8,9},{9,8},{10,11... | collective-permute-start | bytes 1179656 | tf_op jit(solution)/shard_map/ppermute | solution.py:165
  165.0 8.3 %collective-permute-start.9 = (bf16[2,48,1024]{2,1,0:T(8,128)(2,1)S(1)}, bf16[2,48,1024]{2,1,0:T(8,128)(2,1)S(1)}, u32[]{:S(2)}, u32[]{:S(2)}) collective-permute-start(bf16[2,48,1024]{2,1,0:T(8,128)(2,1)S(1)} %collective-permute-done.5.refs_4_), channel_id=1, source_target_pairs={{0,1},{1,0},{2,3},{3,2},{4,5},{5,4},{6,7},{7,6},{8,9},{9,8},{10,11... | collective-permute-start | bytes 589832 | tf_op jit(solution)/shard_map/ppermute | solution.py:165
  171.9 0.7 copy-start.4
  172.5 0.7 copy-start
  173.3 0.7 copy-start.6
  174.0 0.8 copy-start.2
  174.7 1.0 copy-start.1
  175.7 1.0 copy-start.3
  176.7 0.9 copy-start.5
  177.7 0.9 copy-start.7

commit v2 on v1

v2 whole, which is shorter than its diff:
```python
import jax
import jax.numpy as jnp
from jax import lax
from jax.experimental import pallas as pl
from jax.experimental.pallas import tpu as pltpu
from jax.sharding import PartitionSpec as P

HALO = 64
NOFF = 3
STEPS = 2
N_XH = 2
N_Z = 8
N_C = 2
LANE = 128
VMEM_LIMIT = 16 * 1024 * 1024
SELECT_LIMIT = 10 * 1024 * 1024


def select_kernel(start_ref, offsets_ref, weights_ref, own_ref, chosen_ref, piece_ref):
    count, rows, cells = own_ref.shape
    start = lax.rem(start_ref[0], count)
    first = lax.rem(STEPS * lax.axis_index("row") + start, count)
    for s in range(STEPS):
        here = lax.rem(first + s, count)
        left = own_ref[lax.rem(here + count - 1, count)][:, cells - LANE:].astype(jnp.float32)
        right = own_ref[lax.rem(here + 1, count)][:, :LANE].astype(jnp.float32)
        before = jnp.where(here > 0, left, 0.0)
        after = jnp.where(here < count - 1, right, 0.0)
        center = own_ref[here].astype(jnp.float32)
        wide = jnp.concatenate([before, center, after], axis=1)
        width = cells + 2 * LANE
        total = weights_ref[0] * center
        for m in range(NOFF):
            offset = offsets_ref[m]
            forward = pltpu.roll(wide, width - offset, 1)[:, LANE:LANE + cells]
            backward = pltpu.roll(wide, offset, 1)[:, LANE:LANE + cells]
            total = total + weights_ref[m + 1] * (forward + backward)
        piece_ref[:, s * cells:(s + 1) * cells] = total.astype(jnp.bfloat16)

    @pl.loop(0, count)
    def _(t):
        chosen_ref[t // STEPS, lax.rem(t, STEPS)] = own_ref[lax.rem(t + start, count)]


def select(own, stencil_weights, cell_offsets, step_start):
    count, rows, cells = own.shape
    smem = pl.BlockSpec(memory_space=pltpu.SMEM)
    vmem = pl.BlockSpec(memory_space=pltpu.VMEM)
    return pl.pallas_call(
        select_kernel,
        out_shape=(
            jax.ShapeDtypeStruct((count // STEPS, STEPS, rows, cells), own.dtype),
            jax.ShapeDtypeStruct((rows, STEPS * cells), own.dtype),
        ),
        in_specs=[smem, smem, smem, vmem],
        out_specs=(vmem, vmem),
        compiler_params=pltpu.CompilerParams(vmem_limit_bytes=SELECT_LIMIT),
    )(step_start, cell_offsets, stencil_weights, own)


PAIR = [[(hop, 0, 0), (hop, 0, 1)] for hop in range(4)]
PAIR_X = [[(hop, 1, 0), (hop, 1, 1)] for hop in range(4)]
LAST = [(4, 0, 0), (4, 1, 0), (0, 1, 0)]


def gram_kernel(*refs):
    count = len(LAYOUT)
    pieces, right_ref, out_ref, left, right, sem, rsem = refs[:count], refs[count], refs[count + 1], *refs[count + 2:]
    tile = pl.program_id(0)
    tile_rows = out_ref.shape[0]
    cells = right.shape[3]
    piece = right.shape[2]

    def copies():
        column = lax.axis_index("col")
        xh = column // (N_Z * N_C)
        z = lax.rem(column // N_C, N_Z)
        core = lax.rem(column, N_C)
        made = []
        n = 0
        for ref, (side, holds) in zip(pieces, LAYOUT):
            side_core = core if side == 0 else 1 - core
            up = 1 - 2 * side_core
            for index, (hop, other_x, other_core) in enumerate(holds):
                from_z = lax.rem(z - hop * up + N_Z, N_Z)
                from_core = 1 - side_core if other_core else side_core
                from_xh = 1 - xh if other_x else xh
                at = ((from_xh * N_Z + from_z) * N_C + from_core) * piece
                target = left.at[pl.ds(pl.multiple_of(at, piece), piece)]
                made.append(pltpu.make_async_copy(ref.at[index], target, sem.at[n]))
                n += 1
        for s in range(STEPS):
            made.append(pltpu.make_async_copy(right_ref.at[:, s], right.at[s], rsem.at[s]))
        return made

    @pl.when(tile == 0)
    def _():
        made = copies()
        for copy in made:
            copy.start()
        for copy in made:
            copy.wait()

    rows = left[pl.ds(pl.multiple_of(tile * tile_rows, tile_rows), tile_rows), :]
    total = None
    for s in range(STEPS):
        columns = right[s].reshape(-1, cells)
        part = lax.dot_general(
            rows[:, s * cells:(s + 1) * cells], columns,
            (((1,), (1,)), ((), ())), preferred_element_type=jnp.float32,
        )
        total = part if total is None else total + part
    out_ref[...] = total.astype(out_ref.dtype)


def gram(pieces, right, rows_dev):
    row_count, steps, piece, cells = right.shape
    width = row_count * piece
    tiles = 4
    return pl.pallas_call(
        gram_kernel,
        out_shape=jax.ShapeDtypeStruct((rows_dev, width), jnp.bfloat16),
        grid=(tiles,),
        in_specs=[pl.BlockSpec(memory_space=pl.ANY)] * (len(LAYOUT) + 1),
        out_specs=pl.BlockSpec((rows_dev // tiles, width), lambda t: (t, 0)),
        scratch_shapes=[
            pltpu.VMEM((rows_dev, steps * cells), jnp.bfloat16),
            pltpu.VMEM((steps, row_count, piece, cells), jnp.bfloat16),
            pltpu.SemaphoreType.DMA((32,)),
            pltpu.SemaphoreType.DMA((steps,)),
        ],
        compiler_params=pltpu.CompilerParams(vmem_limit_bytes=VMEM_LIMIT),
    )(*pieces, right)


def place(xh, z, core):
    return ((xh % N_XH) * N_Z + z % N_Z) * N_C + core % N_C


PLACES = [(xh, z, core) for xh in range(N_XH) for z in range(N_Z) for core in range(N_C)]
SWAP_X = [(place(x, z, c), place(x + 1, z, c)) for x, z, c in PLACES]
SWAP_CORE = [(place(x, z, c), place(x, z, c + 1)) for x, z, c in PLACES]
RING = [[(place(x, z, c), place(x, z + hop * (1 - 2 * c), c)) for x, z, c in PLACES] for hop in range(5)]
LAYOUT = (
    [(0, PAIR[0])]
    + [(0, PAIR[hop]) for hop in (1, 2, 3)]
    + [(0, PAIR_X[hop]) for hop in (1, 2, 3)]
    + [(0, LAST)]
    + [(1, PAIR[hop] + PAIR_X[hop]) for hop in (1, 2, 3)]
    + [(1, LAST)]
)


def gather_left(piece):
    def swap_x(block):
        return lax.ppermute(block, "col", SWAP_X)

    def swap_core(block):
        return lax.ppermute(block, "col", SWAP_CORE)

    pair = jnp.stack([piece, swap_core(piece)])
    far = lax.ppermute(piece, "col", RING[4])
    near = [lax.ppermute(pair, "col", RING[hop]) for hop in (3, 2, 1)][::-1]
    across = [swap_x(block) for block in near]
    last = jnp.stack([far, swap_x(far), swap_x(piece)])
    other = [swap_core(jnp.concatenate([here, there])) for here, there in zip(near, across)]
    return [pair] + near + across + [last] + other + [swap_core(last)]


def local(sensitivity, stencil_weights, cell_offsets, step_start):
    rows_dev, cells_dev = sensitivity.shape
    col_count = lax.axis_size("col")
    piece_rows = rows_dev // col_count
    blocks = sensitivity.reshape(col_count, piece_rows, cells_dev)
    own = lax.all_to_all(blocks, "col", split_axis=0, concat_axis=0, tiled=True)
    chosen, piece = select(own, stencil_weights, cell_offsets, step_start)
    right = lax.all_to_all(chosen, "row", split_axis=0, concat_axis=0, tiled=True)
    pieces = gather_left(piece)
    return gram(pieces, right, rows_dev)[None]


def solution(mesh):
    in_specs = (P("row", "col"), P(), P(), P())
    out_specs = P("col", "row", None)
    return jax.shard_map(local, mesh=mesh, in_specs=in_specs, out_specs=out_specs, check_vma=False)
```

time: 190 us -> 133 us (0.70)
  Pallas kernels: 59.8 us -> 12 us
  waiting for transfers between devices: 56.1 us -> 41.7 us
  starting transfers between devices: 63.3 us -> 72.7 us
  local copies, waits for them, and re-layouts: 7.86 us -> 5.24 us
    pallas_call x1, Pallas kernels: 50.4 us -> 2.62 us  [select(): pl.pallas_call(select_kernel, out_shape=(jax.ShapeDtypeStruct((count // S...]
    ppermute x10 -> x14, waiting for transfers between devices: 16.9 us -> 2.5 us  [the longest x5 2.48 us: swap_core(): return lax.ppermute(block, 'col', SWAP_CORE)]
    ppermute x10 -> x14, starting transfers between devices: 41.8 us -> 51.2 us  [the longest x5 18 us: swap_x(): return lax.ppermute(block, 'col', SWAP_X)]
    unnamed x20 -> x16, local copies, waits for them, and re-layouts: 7.85 us -> 5.24 us
  transfers between devices with their start and end apart: 12 -> 16, of which waited for: 5 -> 3; matrix products, arithmetic and copies ran while one was open for 0% -> 0% of each run, Pallas kernels for 0% -> 0%
where the time goes in v2:
time: 133 us
  starting transfers between devices  72.7 us (55%)
  waiting for transfers between devices  41.7 us (31%)
  Pallas kernels  12 us (9%)
  local copies, waits for them, and re-layouts  5.24 us (4%)
    all_to_all x1, waiting for transfers between devices, local(): own = lax.all_to_all(blocks, 'col', split_axis=0, concat_axis=0, tiled=True)  39.2 us
    ppermute x5, starting transfers between devices, swap_x(): return lax.ppermute(block, 'col', SWAP_X)  18 us
    ppermute x5, starting transfers between devices, swap_core(): return lax.ppermute(block, 'col', SWAP_CORE)  16.5 us
    all_to_all x1, starting transfers between devices, local(): own = lax.all_to_all(blocks, 'col', split_axis=0, concat_axis=0, tiled=True)  14.6 us
    ppermute x3, starting transfers between devices, gather_left(): near = [lax.ppermute(pair, 'col', RING[hop]) for hop in (3, 2, 1)][::-1]  9.57 us
    pallas_call x1, Pallas kernels, gram(): pl.pallas_call(gram_kernel, out_shape=jax.ShapeDtypeStruct((rows_dev, wid...  9.39 us
    ppermute x1, starting transfers between devices, gather_left(): far = lax.ppermute(piece, 'col', RING[4])  7.13 us
    all_to_all x1, starting transfers between devices, local(): lax.all_to_all(chosen, 'row', split_axis=0, concat_axis=0, tiled=True)  6.95 us
  transfers between devices with their start and end apart: 16, of which 3 were waited for; matrix products, arithmetic and copies ran while one was open for 0% of the time, Pallas kernels for 0%

profile of v2, /device:TPU:1, one launch (start us, length us, event | category | flops | bytes accessed | tf_op | source)
XLA Modules:
  0.0 132.7 jit_solution(2433020912648678416)
XLA Ops:
  0.0 14.6 %all-to-all-start = ((bf16[32,48,512]{2,1,0:T(8,128)(2,1)}), bf16[32,48,512]{2,1,0:T(8,128)(2,1)S(1)}, u32[]{:S(2)}, u32[]{:S(2)}) async-start(bf16[32,48,512]{2,1,0:T(8,128)(2,1)} %bitcast.8), calls=%async_computation | async-start | bytes 3145728 | tf_op jit(solution)/shard_map/all_to_all | solution.py:175
  15.2 39.2 %all-to-all-done.own_ref = bf16[32,48,512]{2,1,0:T(8,128)(2,1)S(1)} async-done(((bf16[32,48,512]{2,1,0:T(8,128)(2,1)}), bf16[32,48,512]{2,1,0:T(8,128)(2,1)S(1)}, u32[]{:S(2)}, u32[]{:S(2)}) %all-to-all-start) | async-done | bytes 1572896 | tf_op jit(solution)/shard_map/all_to_all | solution.py:175
  54.4 2.6 %shard_map.46 = (bf16[16,2,48,512]{3,2,1,0:T(8,128)(2,1)}, bf16[48,1024]{1,0:T(8,128)(2,1)S(1)}) custom-call(s32[1]{0:T(128)S(6)} %copy.5.start_ref, s32[3]{0:T(128)S(1)} %copy-done.6, f32[4]{0:T(128)S(1)} %copy-done.7, bf16[32,48,512]{2,1,0:T(8,128)(2,1)S(1)} %all-to-all-done.own_ref), custom_call_target="tpu_custom_call" | custom-call | tf_op jit(solution)/shard_map/pallas_call | solution.py:49
  57.0 7.0 %all-to-all-start.1 = ((bf16[16,2,48,512]{3,2,1,0:T(8,128)(2,1)}), bf16[16,2,48,512]{3,2,1,0:T(8,128)(2,1)S(1)}, u32[]{:S(2)}, u32[]{:S(2)}) async-start(bf16[16,2,48,512]{3,2,1,0:T(8,128)(2,1)} %get-tuple-element.8), calls=%async_computation.1 | async-start | bytes 3145728 | tf_op jit(solution)/shard_map/all_to_all | solution.py:177
  64.0 3.4 %collective-permute-start = (bf16[48,1024]{1,0:T(8,128)(2,1)S(1)}, bf16[48,1024]{1,0:T(8,128)(2,1)S(1)}, u32[]{:S(2)}, u32[]{:S(2)}) collective-permute-start(bf16[48,1024]{1,0:T(8,128)(2,1)S(1)} %get-tuple-element.7), channel_id=1, source_target_pairs={{0,1},{1,0},{2,3},{3,2},{4,5},{5,4},{6,7},{7,6},{8,9},{9,8},{10,11... | collective-permute-start | bytes 294920 | tf_op jit(solution)/shard_map/ppermute | solution.py:159
  67.3 0.9 collective-permute-done
  68.3 2.3 %collective-permute-start.3 = (bf16[2,48,1024]{2,1,0:T(8,128)(2,1)S(1)}, bf16[2,48,1024]{2,1,0:T(8,128)(2,1)S(1)}, u32[]{:S(2)}, u32[]{:S(2)}) collective-permute-start(bf16[2,48,1024]{2,1,0:T(8,128)(2,1)S(1)} %pad_maximum_fusion.4.refs_0_), channel_id=1, source_target_pairs={{0,6},{1,11},{2,8},{3,13},{4,10},{5,15},{6,12},{7,1},{8,14},{9,3},... | collective-permute-start | bytes 589832 | tf_op jit(solution)/shard_map/ppermute | solution.py:163
  70.6 5.3 %collective-permute-start.2 = (bf16[2,48,1024]{2,1,0:T(8,128)(2,1)S(1)}, bf16[2,48,1024]{2,1,0:T(8,128)(2,1)S(1)}, u32[]{:S(2)}, u32[]{:S(2)}) collective-permute-start(bf16[2,48,1024]{2,1,0:T(8,128)(2,1)S(1)} %pad_maximum_fusion.4.refs_0_), channel_id=1, source_target_pairs={{0,4},{1,13},{2,6},{3,15},{4,8},{5,1},{6,10},{7,3},{8,12},{9,5},{1... | collective-permute-start | bytes 589832 | tf_op jit(solution)/shard_map/ppermute | solution.py:163
  76.0 1.9 %collective-permute-start.1 = (bf16[2,48,1024]{2,1,0:T(8,128)(2,1)S(1)}, bf16[2,48,1024]{2,1,0:T(8,128)(2,1)S(1)}, u32[]{:S(2)}, u32[]{:S(2)}) collective-permute-start(bf16[2,48,1024]{2,1,0:T(8,128)(2,1)S(1)} %pad_maximum_fusion.4.refs_0_), channel_id=1, source_target_pairs={{0,2},{1,15},{2,4},{3,1},{4,6},{5,3},{6,8},{7,5},{8,10},{9,7},{10,... | collective-permute-start | bytes 589832 | tf_op jit(solution)/shard_map/ppermute | solution.py:163
  77.9 0.0 collective-permute-done.3.refs_3_
  77.9 4.4 %collective-permute-start.6 = (bf16[2,48,1024]{2,1,0:T(8,128)(2,1)S(1)}, bf16[2,48,1024]{2,1,0:T(8,128)(2,1)S(1)}, u32[]{:S(2)}, u32[]{:S(2)}) collective-permute-start(bf16[2,48,1024]{2,1,0:T(8,128)(2,1)S(1)} %collective-permute-done.3.refs_3_), channel_id=1, source_target_pairs={{0,16},{1,17},{2,18},{3,19},{4,20},{5,21},{6,22},{7,23},{8,24},{9,... | collective-permute-start | bytes 589832 | tf_op jit(solution)/shard_map/ppermute | solution.py:156
  82.3 7.1 %collective-permute-start.7 = (bf16[48,1024]{1,0:T(8,128)(2,1)S(1)}, bf16[48,1024]{1,0:T(8,128)(2,1)S(1)}, u32[]{:S(2)}, u32[]{:S(2)}) collective-permute-start(bf16[48,1024]{1,0:T(8,128)(2,1)S(1)} %get-tuple-element.7), channel_id=1, source_target_pairs={{0,8},{1,9},{2,10},{3,11},{4,12},{5,13},{6,14},{7,15},{8,0},{9,1},... | collective-permute-start | bytes 294920 | tf_op jit(solution)/shard_map/ppermute | solution.py:162
  89.5 0.0 collective-permute-done.2.refs_2_
  89.5 4.0 %collective-permute-start.5 = (bf16[2,48,1024]{2,1,0:T(8,128)(2,1)S(1)}, bf16[2,48,1024]{2,1,0:T(8,128)(2,1)S(1)}, u32[]{:S(2)}, u32[]{:S(2)}) collective-permute-start(bf16[2,48,1024]{2,1,0:T(8,128)(2,1)S(1)} %collective-permute-done.2.refs_2_), channel_id=1, source_target_pairs={{0,16},{1,17},{2,18},{3,19},{4,20},{5,21},{6,22},{7,23},{8,24},{9,... | collective-permute-start | bytes 589832 | tf_op jit(solution)/shard_map/ppermute | solution.py:156
  93.5 2.8 %collective-permute-start.9 = (bf16[48,1024]{1,0:T(8,128)(2,1)S(1)}, bf16[48,1024]{1,0:T(8,128)(2,1)S(1)}, u32[]{:S(2)}, u32[]{:S(2)}) collective-permute-start(bf16[48,1024]{1,0:T(8,128)(2,1)S(1)} %get-tuple-element.7), channel_id=1, source_target_pairs={{0,16},{1,17},{2,18},{3,19},{4,20},{5,21},{6,22},{7,23},{8,24},{9,... | collective-permute-start | bytes 294920 | tf_op jit(solution)/shard_map/ppermute | solution.py:156
  96.3 4.0 %collective-permute-start.8 = (bf16[48,1024]{1,0:T(8,128)(2,1)S(1)}, bf16[48,1024]{1,0:T(8,128)(2,1)S(1)}, u32[]{:S(2)}, u32[]{:S(2)}) collective-permute-start(bf16[48,1024]{1,0:T(8,128)(2,1)S(1)} %collective-permute-done.7), channel_id=1, source_target_pairs={{0,16},{1,17},{2,18},{3,19},{4,20},{5,21},{6,22},{7,23},{8,24},{9,... | collective-permute-start | bytes 294920 | tf_op jit(solution)/shard_map/ppermute | solution.py:156
  100.3 2.8 %collective-permute-start.4 = (bf16[2,48,1024]{2,1,0:T(8,128)(2,1)S(1)}, bf16[2,48,1024]{2,1,0:T(8,128)(2,1)S(1)}, u32[]{:S(2)}, u32[]{:S(2)}) collective-permute-start(bf16[2,48,1024]{2,1,0:T(8,128)(2,1)S(1)} %collective-permute-done.1.refs_1_), channel_id=1, source_target_pairs={{0,16},{1,17},{2,18},{3,19},{4,20},{5,21},{6,22},{7,23},{8,24},{9,... | collective-permute-start | bytes 589832 | tf_op jit(solution)/shard_map/ppermute | solution.py:156
  103.1 0.0 collective-permute-done.6.refs_6_
  103.2 4.4 %collective-permute-start.12 = (bf16[4,48,1024]{2,1,0:T(8,128)(2,1)S(1)}, bf16[4,48,1024]{2,1,0:T(8,128)(2,1)S(1)}, u32[]{:S(2)}, u32[]{:S(2)}) collective-permute-start(bf16[4,48,1024]{2,1,0:T(8,128)(2,1)S(1)} %pad_maximum_fusion.2), channel_id=1, source_target_pairs={{0,1},{1,0},{2,3},{3,2},{4,5},{5,4},{6,7},{7,6},{8,9},{9,8},{10,11... | collective-permute-start | bytes 1179656 | tf_op jit(solution)/shard_map/ppermute | solution.py:159
  107.6 0.0 collective-permute-done.5.refs_5_
  107.6 1.9 %collective-permute-start.11 = (bf16[4,48,1024]{2,1,0:T(8,128)(2,1)S(1)}, bf16[4,48,1024]{2,1,0:T(8,128)(2,1)S(1)}, u32[]{:S(2)}, u32[]{:S(2)}) collective-permute-start(bf16[4,48,1024]{2,1,0:T(8,128)(2,1)S(1)} %pad_maximum_fusion.1), channel_id=1, source_target_pairs={{0,1},{1,0},{2,3},{3,2},{4,5},{5,4},{6,7},{7,6},{8,9},{9,8},{10,11... | collective-permute-start | bytes 1179656 | tf_op jit(solution)/shard_map/ppermute | solution.py:159
  109.6 4.9 %collective-permute-start.10 = (bf16[4,48,1024]{2,1,0:T(8,128)(2,1)S(1)}, bf16[4,48,1024]{2,1,0:T(8,128)(2,1)S(1)}, u32[]{:S(2)}, u32[]{:S(2)}) collective-permute-start(bf16[4,48,1024]{2,1,0:T(8,128)(2,1)S(1)} %pad_maximum_fusion), channel_id=1, source_target_pairs={{0,1},{1,0},{2,3},{3,2},{4,5},{5,4},{6,7},{7,6},{8,9},{9,8},{10,11... | collective-permute-start | bytes 1179656 | tf_op jit(solution)/shard_map/ppermute | solution.py:159
  114.5 0.0 collective-permute-done.8
  114.6 1.9 %collective-permute-start.13 = (bf16[3,48,1024]{2,1,0:T(8,128)(2,1)S(1)}, bf16[3,48,1024]{2,1,0:T(8,128)(2,1)S(1)}, u32[]{:S(2)}, u32[]{:S(2)}) collective-permute-start(bf16[3,48,1024]{2,1,0:T(8,128)(2,1)S(1)} %pad_maximum_fusion.3.refs_7_), channel_id=1, source_target_pairs={{0,1},{1,0},{2,3},{3,2},{4,5},{5,4},{6,7},{7,6},{8,9},{9,8},{10,11... | collective-permute-start | bytes 884744 | tf_op jit(solution)/shard_map/ppermute | solution.py:159
  116.5 1.5 %collective-permute-done.13.refs_11_ = bf16[3,48,1024]{2,1,0:T(8,128)(2,1)S(1)} collective-permute-done((bf16[3,48,1024]{2,1,0:T(8,128)(2,1)S(1)}, bf16[3,48,1024]{2,1,0:T(8,128)(2,1)S(1)}, u32[]{:S(2)}, u32[]{:S(2)}) %collective-permute-start.13) | collective-permute-done | bytes 294944 | tf_op jit(solution)/shard_map/ppermute | solution.py:159
  118.0 0.8 copy-done
  118.8 0.7 copy-done.2
  119.6 0.7 copy-done.4
  120.3 1.0 copy-done.1
  121.3 1.0 copy-done.3
  122.3 1.0 copy-done.5
  123.3 9.4 %shard_map.47 = bf16[1536,768]{1,0:T(8,128)(2,1)} custom-call(bf16[2,48,1024]{2,1,0:T(8,128)(2,1)S(1)} %pad_maximum_fusion.4.refs_0_, bf16[2,48,1024]{2,1,0:T(8,128)(2,1)S(1)} %collective-permute-done.1.refs_1_, bf16[2,48,1024]{2,1,0:T(8,128)(2,1)S(1)} %collective-permute-done.2.refs_2_, bf16[2,48,1024]{2,1,0:T(8,128)(2,1)S(1)} %collective-permute-done.3.refs_3_, ...), custom_call_target="tpu_custom_call" | custom-call | tf_op jit(solution)/shard_map/pallas_call | solution.py:120
  (23 shorter events, 0.2 us)
Async XLA Ops:
  0.0 54.4 %copy-start.6 = (s32[3]{0:T(128)S(1)}, s32[3]{0:T(128)}, u32[]{:S(2)}) copy-start(s32[3]{0:T(128)} %offsets_ref.1) | copy-start | bytes 40
  0.0 54.4 %copy-start.7 = (f32[4]{0:T(128)S(1)}, f32[4]{0:T(128)}, u32[]{:S(2)}) copy-start(f32[4]{0:T(128)} %weights_ref.1) | copy-start | bytes 52
  0.0 54.4 %all-to-all-start = ((bf16[32,48,512]{2,1,0:T(8,128)(2,1)}), bf16[32,48,512]{2,1,0:T(8,128)(2,1)S(1)}, u32[]{:S(2)}, u32[]{:S(2)}) async-start(bf16[32,48,512]{2,1,0:T(8,128)(2,1)} %bitcast.8), calls=%async_computation | async-start | bytes 3145728 | tf_op jit(solution)/shard_map/all_to_all | solution.py:175
  57.0 63.3 %all-to-all-start.1 = ((bf16[16,2,48,512]{3,2,1,0:T(8,128)(2,1)}), bf16[16,2,48,512]{3,2,1,0:T(8,128)(2,1)S(1)}, u32[]{:S(2)}, u32[]{:S(2)}) async-start(bf16[16,2,48,512]{3,2,1,0:T(8,128)(2,1)} %get-tuple-element.8), calls=%async_computation.1 | async-start | bytes 3145728 | tf_op jit(solution)/shard_map/all_to_all | solution.py:177
  64.0 4.3 %collective-permute-start = (bf16[48,1024]{1,0:T(8,128)(2,1)S(1)}, bf16[48,1024]{1,0:T(8,128)(2,1)S(1)}, u32[]{:S(2)}, u32[]{:S(2)}) collective-permute-start(bf16[48,1024]{1,0:T(8,128)(2,1)S(1)} %get-tuple-element.7), channel_id=1, source_target_pairs={{0,1},{1,0},{2,3},{3,2},{4,5},{5,4},{6,7},{7,6},{8,9},{9,8},{10,11... | collective-permute-start | bytes 294920 | tf_op jit(solution)/shard_map/ppermute | solution.py:159
  68.3 9.6 %collective-permute-start.3 = (bf16[2,48,1024]{2,1,0:T(8,128)(2,1)S(1)}, bf16[2,48,1024]{2,1,0:T(8,128)(2,1)S(1)}, u32[]{:S(2)}, u32[]{:S(2)}) collective-permute-start(bf16[2,48,1024]{2,1,0:T(8,128)(2,1)S(1)} %pad_maximum_fusion.4.refs_0_), channel_id=1, source_target_pairs={{0,6},{1,11},{2,8},{3,13},{4,10},{5,15},{6,12},{7,1},{8,14},{9,3},... | collective-permute-start | bytes 589832 | tf_op jit(solution)/shard_map/ppermute | solution.py:163
  70.6 18.8 %collective-permute-start.2 = (bf16[2,48,1024]{2,1,0:T(8,128)(2,1)S(1)}, bf16[2,48,1024]{2,1,0:T(8,128)(2,1)S(1)}, u32[]{:S(2)}, u32[]{:S(2)}) collective-permute-start(bf16[2,48,1024]{2,1,0:T(8,128)(2,1)S(1)} %pad_maximum_fusion.4.refs_0_), channel_id=1, source_target_pairs={{0,4},{1,13},{2,6},{3,15},{4,8},{5,1},{6,10},{7,3},{8,12},{9,5},{1... | collective-permute-start | bytes 589832 | tf_op jit(solution)/shard_map/ppermute | solution.py:163
  76.0 24.3 %collective-permute-start.1 = (bf16[2,48,1024]{2,1,0:T(8,128)(2,1)S(1)}, bf16[2,48,1024]{2,1,0:T(8,128)(2,1)S(1)}, u32[]{:S(2)}, u32[]{:S(2)}) collective-permute-start(bf16[2,48,1024]{2,1,0:T(8,128)(2,1)S(1)} %pad_maximum_fusion.4.refs_0_), channel_id=1, source_target_pairs={{0,2},{1,15},{2,4},{3,1},{4,6},{5,3},{6,8},{7,5},{8,10},{9,7},{10,... | collective-permute-start | bytes 589832 | tf_op jit(solution)/shard_map/ppermute | solution.py:163
  77.9 25.2 %collective-permute-start.6 = (bf16[2,48,1024]{2,1,0:T(8,128)(2,1)S(1)}, bf16[2,48,1024]{2,1,0:T(8,128)(2,1)S(1)}, u32[]{:S(2)}, u32[]{:S(2)}) collective-permute-start(bf16[2,48,1024]{2,1,0:T(8,128)(2,1)S(1)} %collective-permute-done.3.refs_3_), channel_id=1, source_target_pairs={{0,16},{1,17},{2,18},{3,19},{4,20},{5,21},{6,22},{7,23},{8,24},{9,... | collective-permute-start | bytes 589832 | tf_op jit(solution)/shard_map/ppermute | solution.py:156
  82.3 14.0 %collective-permute-start.7 = (bf16[48,1024]{1,0:T(8,128)(2,1)S(1)}, bf16[48,1024]{1,0:T(8,128)(2,1)S(1)}, u32[]{:S(2)}, u32[]{:S(2)}) collective-permute-start(bf16[48,1024]{1,0:T(8,128)(2,1)S(1)} %get-tuple-element.7), channel_id=1, source_target_pairs={{0,8},{1,9},{2,10},{3,11},{4,12},{5,13},{6,14},{7,15},{8,0},{9,1},... | collective-permute-start | bytes 294920 | tf_op jit(solution)/shard_map/ppermute | solution.py:162
  89.5 18.1 %collective-permute-start.5 = (bf16[2,48,1024]{2,1,0:T(8,128)(2,1)S(1)}, bf16[2,48,1024]{2,1,0:T(8,128)(2,1)S(1)}, u32[]{:S(2)}, u32[]{:S(2)}) collective-permute-start(bf16[2,48,1024]{2,1,0:T(8,128)(2,1)S(1)} %collective-permute-done.2.refs_2_), channel_id=1, source_target_pairs={{0,16},{1,17},{2,18},{3,19},{4,20},{5,21},{6,22},{7,23},{8,24},{9,... | collective-permute-start | bytes 589832 | tf_op jit(solution)/shard_map/ppermute | solution.py:156
  93.5 21.0 %collective-permute-start.9 = (bf16[48,1024]{1,0:T(8,128)(2,1)S(1)}, bf16[48,1024]{1,0:T(8,128)(2,1)S(1)}, u32[]{:S(2)}, u32[]{:S(2)}) collective-permute-start(bf16[48,1024]{1,0:T(8,128)(2,1)S(1)} %get-tuple-element.7), channel_id=1, source_target_pairs={{0,16},{1,17},{2,18},{3,19},{4,20},{5,21},{6,22},{7,23},{8,24},{9,... | collective-permute-start | bytes 294920 | tf_op jit(solution)/shard_map/ppermute | solution.py:156
  96.3 18.2 %collective-permute-start.8 = (bf16[48,1024]{1,0:T(8,128)(2,1)S(1)}, bf16[48,1024]{1,0:T(8,128)(2,1)S(1)}, u32[]{:S(2)}, u32[]{:S(2)}) collective-permute-start(bf16[48,1024]{1,0:T(8,128)(2,1)S(1)} %collective-permute-done.7), channel_id=1, source_target_pairs={{0,16},{1,17},{2,18},{3,19},{4,20},{5,21},{6,22},{7,23},{8,24},{9,... | collective-permute-start | bytes 294920 | tf_op jit(solution)/shard_map/ppermute | solution.py:156
  100.3 9.3 %collective-permute-start.4 = (bf16[2,48,1024]{2,1,0:T(8,128)(2,1)S(1)}, bf16[2,48,1024]{2,1,0:T(8,128)(2,1)S(1)}, u32[]{:S(2)}, u32[]{:S(2)}) collective-permute-start(bf16[2,48,1024]{2,1,0:T(8,128)(2,1)S(1)} %collective-permute-done.1.refs_1_), channel_id=1, source_target_pairs={{0,16},{1,17},{2,18},{3,19},{4,20},{5,21},{6,22},{7,23},{8,24},{9,... | collective-permute-start | bytes 589832 | tf_op jit(solution)/shard_map/ppermute | solution.py:156
  103.2 14.9 %collective-permute-start.12 = (bf16[4,48,1024]{2,1,0:T(8,128)(2,1)S(1)}, bf16[4,48,1024]{2,1,0:T(8,128)(2,1)S(1)}, u32[]{:S(2)}, u32[]{:S(2)}) collective-permute-start(bf16[4,48,1024]{2,1,0:T(8,128)(2,1)S(1)} %pad_maximum_fusion.2), channel_id=1, source_target_pairs={{0,1},{1,0},{2,3},{3,2},{4,5},{5,4},{6,7},{7,6},{8,9},{9,8},{10,11... | collective-permute-start | bytes 1179656 | tf_op jit(solution)/shard_map/ppermute | solution.py:159
  107.6 11.2 %collective-permute-start.11 = (bf16[4,48,1024]{2,1,0:T(8,128)(2,1)S(1)}, bf16[4,48,1024]{2,1,0:T(8,128)(2,1)S(1)}, u32[]{:S(2)}, u32[]{:S(2)}) collective-permute-start(bf16[4,48,1024]{2,1,0:T(8,128)(2,1)S(1)} %pad_maximum_fusion.1), channel_id=1, source_target_pairs={{0,1},{1,0},{2,3},{3,2},{4,5},{5,4},{6,7},{7,6},{8,9},{9,8},{10,11... | collective-permute-start | bytes 1179656 | tf_op jit(solution)/shard_map/ppermute | solution.py:159
  109.6 9.9 %collective-permute-start.10 = (bf16[4,48,1024]{2,1,0:T(8,128)(2,1)S(1)}, bf16[4,48,1024]{2,1,0:T(8,128)(2,1)S(1)}, u32[]{:S(2)}, u32[]{:S(2)}) collective-permute-start(bf16[4,48,1024]{2,1,0:T(8,128)(2,1)S(1)} %pad_maximum_fusion), channel_id=1, source_target_pairs={{0,1},{1,0},{2,3},{3,2},{4,5},{5,4},{6,7},{7,6},{8,9},{9,8},{10,11... | collective-permute-start | bytes 1179656 | tf_op jit(solution)/shard_map/ppermute | solution.py:159
  114.6 3.5 %collective-permute-start.13 = (bf16[3,48,1024]{2,1,0:T(8,128)(2,1)S(1)}, bf16[3,48,1024]{2,1,0:T(8,128)(2,1)S(1)}, u32[]{:S(2)}, u32[]{:S(2)}) collective-permute-start(bf16[3,48,1024]{2,1,0:T(8,128)(2,1)S(1)} %pad_maximum_fusion.3.refs_7_), channel_id=1, source_target_pairs={{0,1},{1,0},{2,3},{3,2},{4,5},{5,4},{6,7},{7,6},{8,9},{9,8},{10,11... | collective-permute-start | bytes 884744 | tf_op jit(solution)/shard_map/ppermute | solution.py:159
  118.0 0.8 copy-start
  118.8 0.7 copy-start.2
  119.5 0.7 copy-start.4
  120.3 1.0 copy-start.1
  121.3 1.0 copy-start.3
  122.3 1.0 copy-start.5

commit v3 on v2

--- a/solution.py
+++ b/solution.py
@@ -58,26 +58,19 @@
     )(step_start, cell_offsets, stencil_weights, own)
 
 
-PAIR = [[(hop, 0, 0), (hop, 0, 1)] for hop in range(4)]
-PAIR_X = [[(hop, 1, 0), (hop, 1, 1)] for hop in range(4)]
-LAST = [(4, 0, 0), (4, 1, 0), (0, 1, 0)]
-
-
 def gram_kernel(*refs):
     count = len(LAYOUT)
-    pieces, right_ref, out_ref, left, right, sem, rsem = refs[:count], refs[count], refs[count + 1], *refs[count + 2:]
+    pieces, right_ref, out_ref, left = refs[:count], refs[count], refs[count + 1], refs[count + 2]
     tile = pl.program_id(0)
     tile_rows = out_ref.shape[0]
-    cells = right.shape[3]
-    piece = right.shape[2]
+    row_count, steps, piece, cells = right_ref.shape
 
-    def copies():
+    @pl.when(tile == 0)
+    def _():
         column = lax.axis_index("col")
         xh = column // (N_Z * N_C)
         z = lax.rem(column // N_C, N_Z)
         core = lax.rem(column, N_C)
-        made = []
-        n = 0
         for ref, (side, holds) in zip(pieces, LAYOUT):
             side_core = core if side == 0 else 1 - core
             up = 1 - 2 * side_core
@@ -86,25 +79,12 @@
                 from_core = 1 - side_core if other_core else side_core
                 from_xh = 1 - xh if other_x else xh
                 at = ((from_xh * N_Z + from_z) * N_C + from_core) * piece
-                target = left.at[pl.ds(pl.multiple_of(at, piece), piece)]
-                made.append(pltpu.make_async_copy(ref.at[index], target, sem.at[n]))
-                n += 1
-        for s in range(STEPS):
-            made.append(pltpu.make_async_copy(right_ref.at[:, s], right.at[s], rsem.at[s]))
-        return made
-
-    @pl.when(tile == 0)
-    def _():
-        made = copies()
-        for copy in made:
-            copy.start()
-        for copy in made:
-            copy.wait()
+                left[pl.ds(pl.multiple_of(at, piece), piece), :] = ref[index]
 
     rows = left[pl.ds(pl.multiple_of(tile * tile_rows, tile_rows), tile_rows), :]
     total = None
-    for s in range(STEPS):
-        columns = right[s].reshape(-1, cells)
+    for s in range(steps):
+        columns = right_ref[:, s].reshape(row_count * piece, cells)
         part = lax.dot_general(
             rows[:, s * cells:(s + 1) * cells], columns,
             (((1,), (1,)), ((), ())), preferred_element_type=jnp.float32,
@@ -121,14 +101,9 @@
         gram_kernel,
         out_shape=jax.ShapeDtypeStruct((rows_dev, width), jnp.bfloat16),
         grid=(tiles,),
-        in_specs=[pl.BlockSpec(memory_space=pl.ANY)] * (len(LAYOUT) + 1),
+        in_specs=[pl.BlockSpec(memory_space=pltpu.VMEM)] * (len(LAYOUT) + 1),
         out_specs=pl.BlockSpec((rows_dev // tiles, width), lambda t: (t, 0)),
-        scratch_shapes=[
-            pltpu.VMEM((rows_dev, steps * cells), jnp.bfloat16),
-            pltpu.VMEM((steps, row_count, piece, cells), jnp.bfloat16),
-            pltpu.SemaphoreType.DMA((32,)),
-            pltpu.SemaphoreType.DMA((steps,)),
-        ],
+        scratch_shapes=[pltpu.VMEM((rows_dev, steps * cells), jnp.bfloat16)],
         compiler_params=pltpu.CompilerParams(vmem_limit_bytes=VMEM_LIMIT),
     )(*pieces, right)
 
@@ -141,14 +116,25 @@
 SWAP_X = [(place(x, z, c), place(x + 1, z, c)) for x, z, c in PLACES]
 SWAP_CORE = [(place(x, z, c), place(x, z, c + 1)) for x, z, c in PLACES]
 RING = [[(place(x, z, c), place(x, z + hop * (1 - 2 * c), c)) for x, z, c in PLACES] for hop in range(5)]
-LAYOUT = (
-    [(0, PAIR[0])]
-    + [(0, PAIR[hop]) for hop in (1, 2, 3)]
-    + [(0, PAIR_X[hop]) for hop in (1, 2, 3)]
-    + [(0, LAST)]
-    + [(1, PAIR[hop] + PAIR_X[hop]) for hop in (1, 2, 3)]
-    + [(1, LAST)]
-)
+OWN, FIRST, FAR = [(0, 0, 0)], [(1, 0, 0), (1, 0, 1)], [(4, 0, 0)]
+SECOND = [(2, 0, 0), (2, 0, 1), (3, 0, 0), (3, 0, 1)]
+
+
+def across(holds):
+    return [(hop, 1, core) for hop, _, core in holds]
+
+
+LAYOUT = [
+    (0, [(0, 0, 0), (0, 0, 1)]),
+    (0, FIRST),
+    (0, FAR),
+    (0, SECOND),
+    (0, across(OWN + FIRST + FAR)),
+    (0, across(SECOND)),
+    (1, FIRST + FAR + across(OWN + FIRST + FAR)),
+    (1, SECOND),
+    (1, across(SECOND)),
+]
 
 
 def gather_left(piece):
@@ -158,13 +144,18 @@
     def swap_core(block):
         return lax.ppermute(block, "col", SWAP_CORE)
 
-    pair = jnp.stack([piece, swap_core(piece)])
-    far = lax.ppermute(piece, "col", RING[4])
-    near = [lax.ppermute(pair, "col", RING[hop]) for hop in (3, 2, 1)][::-1]
-    across = [swap_x(block) for block in near]
-    last = jnp.stack([far, swap_x(far), swap_x(piece)])
-    other = [swap_core(jnp.concatenate([here, there])) for here, there in zip(near, across)]
-    return [pair] + near + across + [last] + other + [swap_core(last)]
+    own = piece[None]
+    pair = jnp.concatenate([own, swap_core(own)])
+    far = lax.ppermute(own, "col", RING[4])
+    first = lax.ppermute(pair, "col", RING[1])
+    second = lax.ppermute(jnp.concatenate([pair, first]), "col", RING[2])
+    near = jnp.concatenate([first, far])
+    near_x = swap_x(jnp.concatenate([own, near]))
+    second_x = swap_x(second)
+    return [
+        pair, first, far, second, near_x, second_x,
+        swap_core(jnp.concatenate([near, near_x])), swap_core(second), swap_core(second_x),
+    ]
 
 
 def local(sensitivity, stencil_weights, cell_offsets, step_start):

time: 133 us -> 126 us (0.947)
  starting transfers between devices: 72.7 us -> 56.8 us
  waiting for transfers between devices: 41.7 us -> 54.5 us
  Pallas kernels: 12 us -> 6.98 us
    ppermute x4 -> x3, waiting for transfers between devices: 0.01 us -> 7.52 us  [the longest x1 3.77 us: gather_left(): second = lax.ppermute(jnp.concatenate([pair, first]), 'col', RING[2])]
    ppermute x5 -> x2, waiting for transfers between devices: 0.01 us -> 6.89 us  [swap_x(): return lax.ppermute(block, 'col', SWAP_X)]
    ppermute x5 -> x2, starting transfers between devices: 18 us -> 11.2 us  [swap_x(): return lax.ppermute(block, 'col', SWAP_X)]
    ppermute x4 -> x3, starting transfers between devices: 16.7 us -> 11.5 us  [the longest x1 5.56 us: gather_left(): far = lax.ppermute(own, 'col', RING[4])]
    pallas_call x1, Pallas kernels: 9.39 us -> 4.36 us  [gram(): pl.pallas_call(gram_kernel, out_shape=jax.ShapeDtypeStruct((rows_dev, wid...]
    ppermute x5 -> x4, starting transfers between devices: 16.5 us -> 12.5 us  [swap_core(): return lax.ppermute(block, 'col', SWAP_CORE)]
    ppermute x5 -> x4, waiting for transfers between devices: 2.48 us -> 0.93 us  [swap_core(): return lax.ppermute(block, 'col', SWAP_CORE)]
  transfers between devices with their start and end apart: 16 -> 11, of which waited for: 3 -> 6; matrix products, arithmetic and copies ran while one was open for 0% -> 0% of each run, Pallas kernels for 0% -> 0%
where the time goes in v3:
time: 126 us; the launch traced here: 124 us
  starting transfers between devices  56.8 us (45%)
  waiting for transfers between devices  54.5 us (43%)
  Pallas kernels  6.98 us (6%)
  local copies, waits for them, and re-layouts  5.25 us (4%)
    all_to_all x1, waiting for transfers between devices, local(): own = lax.all_to_all(blocks, 'col', split_axis=0, concat_axis=0, tiled=True)  39.2 us
    all_to_all x1, starting transfers between devices, local(): own = lax.all_to_all(blocks, 'col', split_axis=0, concat_axis=0, tiled=True)  14.6 us
    ppermute x4, starting transfers between devices, swap_core(): return lax.ppermute(block, 'col', SWAP_CORE)  12.5 us
    ppermute x2, starting transfers between devices, swap_x(): return lax.ppermute(block, 'col', SWAP_X)  11.2 us
    all_to_all x1, starting transfers between devices, local(): lax.all_to_all(chosen, 'row', split_axis=0, concat_axis=0, tiled=True)  6.95 us
    ppermute x2, waiting for transfers between devices, swap_x(): return lax.ppermute(block, 'col', SWAP_X)  6.89 us
    ppermute x1, starting transfers between devices, gather_left(): far = lax.ppermute(own, 'col', RING[4])  5.56 us
    unnamed x16, local copies, waits for them, and re-layouts  5.25 us
  transfers between devices with their start and end apart: 11, of which 6 were waited for; matrix products, arithmetic and copies ran while one was open for 0% of the time, Pallas kernels for 0%

profile of v3, /device:TPU:1, one launch (start us, length us, event | category | flops | bytes accessed | tf_op | source)
XLA Modules:
  0.0 124.4 jit_solution(1830855414687014712)
XLA Ops:
  0.0 14.6 %all-to-all-start = ((bf16[32,48,512]{2,1,0:T(8,128)(2,1)}), bf16[32,48,512]{2,1,0:T(8,128)(2,1)S(1)}, u32[]{:S(2)}, u32[]{:S(2)}) async-start(bf16[32,48,512]{2,1,0:T(8,128)(2,1)} %bitcast.7), calls=%async_computation | async-start | bytes 3145728 | tf_op jit(solution)/shard_map/all_to_all | solution.py:166
  15.2 39.2 %all-to-all-done.own_ref = bf16[32,48,512]{2,1,0:T(8,128)(2,1)S(1)} async-done(((bf16[32,48,512]{2,1,0:T(8,128)(2,1)}), bf16[32,48,512]{2,1,0:T(8,128)(2,1)S(1)}, u32[]{:S(2)}, u32[]{:S(2)}) %all-to-all-start) | async-done | bytes 1572896 | tf_op jit(solution)/shard_map/all_to_all | solution.py:166
  54.4 2.6 %shard_map.46 = (bf16[16,2,48,512]{3,2,1,0:T(8,128)(2,1)}, bf16[48,1024]{1,0:T(8,128)(2,1)S(1)}) custom-call(s32[1]{0:T(128)S(6)} %copy.5.start_ref, s32[3]{0:T(128)S(1)} %copy-done.6, f32[4]{0:T(128)S(1)} %copy-done.7, bf16[32,48,512]{2,1,0:T(8,128)(2,1)S(1)} %all-to-all-done.own_ref), custom_call_target="tpu_custom_call" | custom-call | tf_op jit(solution)/shard_map/pallas_call | solution.py:49
  57.0 7.0 %all-to-all-start.1 = ((bf16[16,2,48,512]{3,2,1,0:T(8,128)(2,1)}), bf16[16,2,48,512]{3,2,1,0:T(8,128)(2,1)S(1)}, u32[]{:S(2)}, u32[]{:S(2)}) async-start(bf16[16,2,48,512]{3,2,1,0:T(8,128)(2,1)} %get-tuple-element.8), calls=%async_computation.1 | async-start | bytes 3145728 | tf_op jit(solution)/shard_map/all_to_all | solution.py:168
  64.0 3.4 %collective-permute-start = (bf16[1,48,1024]{2,1,0:T(8,128)(2,1)S(1)}, bf16[1,48,1024]{2,1,0:T(8,128)(2,1)S(1)}, u32[]{:S(2)}, u32[]{:S(2)}) collective-permute-start(bf16[1,48,1024]{2,1,0:T(8,128)(2,1)S(1)} %bitcast.3), channel_id=1, source_target_pairs={{0,1},{1,0},{2,3},{3,2},{4,5},{5,4},{6,7},{7,6},{8,9},{9,8},{10,11... | collective-permute-start | bytes 294920 | tf_op jit(solution)/shard_map/ppermute | solution.py:145
  67.3 0.9 collective-permute-done
  68.3 2.1 %collective-permute-start.1 = (bf16[2,48,1024]{2,1,0:T(8,128)(2,1)S(1)}, bf16[2,48,1024]{2,1,0:T(8,128)(2,1)S(1)}, u32[]{:S(2)}, u32[]{:S(2)}) collective-permute-start(bf16[2,48,1024]{2,1,0:T(8,128)(2,1)S(1)} %pad_maximum_fusion.3.refs_0_), channel_id=1, source_target_pairs={{0,2},{1,15},{2,4},{3,1},{4,6},{5,3},{6,8},{7,5},{8,10},{9,7},{10,... | collective-permute-start | bytes 589832 | tf_op jit(solution)/shard_map/ppermute | solution.py:150
  70.4 5.6 %collective-permute-start.2 = (bf16[1,48,1024]{2,1,0:T(8,128)(2,1)S(1)}, bf16[1,48,1024]{2,1,0:T(8,128)(2,1)S(1)}, u32[]{:S(2)}, u32[]{:S(2)}) collective-permute-start(bf16[1,48,1024]{2,1,0:T(8,128)(2,1)S(1)} %bitcast.5), channel_id=1, source_target_pairs={{0,8},{1,9},{2,10},{3,11},{4,12},{5,13},{6,14},{7,15},{8,0},{9,1},... | collective-permute-start | bytes 294920 | tf_op jit(solution)/shard_map/ppermute | solution.py:149
  76.0 3.7 %collective-permute-done.2.refs_2_ = bf16[1,48,1024]{2,1,0:T(8,128)(2,1)S(1)} collective-permute-done((bf16[1,48,1024]{2,1,0:T(8,128)(2,1)S(1)}, bf16[1,48,1024]{2,1,0:T(8,128)(2,1)S(1)}, u32[]{:S(2)}, u32[]{:S(2)}) %collective-permute-start.2) | collective-permute-done | bytes 98336 | tf_op jit(solution)/shard_map/ppermute | solution.py:149
  79.7 0.0 collective-permute-done.1.refs_1_
  79.7 0.1 fusion.1
  79.8 3.8 %collective-permute-start.3 = (bf16[4,48,1024]{2,1,0:T(8,128)(2,1)S(1)}, bf16[4,48,1024]{2,1,0:T(8,128)(2,1)S(1)}, u32[]{:S(2)}, u32[]{:S(2)}) collective-permute-start(bf16[4,48,1024]{2,1,0:T(8,128)(2,1)S(1)} %get-tuple-element.10), channel_id=1, source_target_pairs={{0,4},{1,13},{2,6},{3,15},{4,8},{5,1},{6,10},{7,3},{8,12},{9,5},{1... | collective-permute-start | bytes 1179656 | tf_op jit(solution)/shard_map/ppermute | solution.py:151
  83.6 6.8 %collective-permute-start.4 = (bf16[4,48,1024]{2,1,0:T(8,128)(2,1)S(1)}, bf16[4,48,1024]{2,1,0:T(8,128)(2,1)S(1)}, u32[]{:S(2)}, u32[]{:S(2)}) collective-permute-start(bf16[4,48,1024]{2,1,0:T(8,128)(2,1)S(1)} %get-tuple-element.9), channel_id=1, source_target_pairs={{0,16},{1,17},{2,18},{3,19},{4,20},{5,21},{6,22},{7,23},{8,24},{9,... | collective-permute-start | bytes 1179656 | tf_op jit(solution)/shard_map/ppermute | solution.py:142
  90.4 3.8 %collective-permute-done.3.refs_3_ = bf16[4,48,1024]{2,1,0:T(8,128)(2,1)S(1)} collective-permute-done((bf16[4,48,1024]{2,1,0:T(8,128)(2,1)S(1)}, bf16[4,48,1024]{2,1,0:T(8,128)(2,1)S(1)}, u32[]{:S(2)}, u32[]{:S(2)}) %collective-permute-start.3) | collective-permute-done | bytes 393248 | tf_op jit(solution)/shard_map/ppermute | solution.py:151
  94.1 4.5 %collective-permute-start.5 = (bf16[4,48,1024]{2,1,0:T(8,128)(2,1)S(1)}, bf16[4,48,1024]{2,1,0:T(8,128)(2,1)S(1)}, u32[]{:S(2)}, u32[]{:S(2)}) collective-permute-start(bf16[4,48,1024]{2,1,0:T(8,128)(2,1)S(1)} %collective-permute-done.3.refs_3_), channel_id=1, source_target_pairs={{0,16},{1,17},{2,18},{3,19},{4,20},{5,21},{6,22},{7,23},{8,24},{9,... | collective-permute-start | bytes 1179656 | tf_op jit(solution)/shard_map/ppermute | solution.py:142
  98.6 5.0 %collective-permute-done.4.refs_4_ = bf16[4,48,1024]{2,1,0:T(8,128)(2,1)S(1)} collective-permute-done((bf16[4,48,1024]{2,1,0:T(8,128)(2,1)S(1)}, bf16[4,48,1024]{2,1,0:T(8,128)(2,1)S(1)}, u32[]{:S(2)}, u32[]{:S(2)}) %collective-permute-start.4) | collective-permute-done | bytes 393248 | tf_op jit(solution)/shard_map/ppermute | solution.py:142
  103.6 0.1 pad_maximum_fusion
  103.7 3.2 %collective-permute-start.6 = (bf16[7,48,1024]{2,1,0:T(8,128)(2,1)S(1)}, bf16[7,48,1024]{2,1,0:T(8,128)(2,1)S(1)}, u32[]{:S(2)}, u32[]{:S(2)}) collective-permute-start(bf16[7,48,1024]{2,1,0:T(8,128)(2,1)S(1)} %pad_maximum_fusion), channel_id=1, source_target_pairs={{0,1},{1,0},{2,3},{3,2},{4,5},{5,4},{6,7},{7,6},{8,9},{9,8},{10,11... | collective-permute-start | bytes 2064392 | tf_op jit(solution)/shard_map/ppermute | solution.py:145
  106.9 1.9 %collective-permute-start.7 = (bf16[4,48,1024]{2,1,0:T(8,128)(2,1)S(1)}, bf16[4,48,1024]{2,1,0:T(8,128)(2,1)S(1)}, u32[]{:S(2)}, u32[]{:S(2)}) collective-permute-start(bf16[4,48,1024]{2,1,0:T(8,128)(2,1)S(1)} %collective-permute-done.3.refs_3_), channel_id=1, source_target_pairs={{0,1},{1,0},{2,3},{3,2},{4,5},{5,4},{6,7},{7,6},{8,9},{9,8},{10,11... | collective-permute-start | bytes 1179656 | tf_op jit(solution)/shard_map/ppermute | solution.py:145
  108.8 1.9 %collective-permute-done.5.refs_5_ = bf16[4,48,1024]{2,1,0:T(8,128)(2,1)S(1)} collective-permute-done((bf16[4,48,1024]{2,1,0:T(8,128)(2,1)S(1)}, bf16[4,48,1024]{2,1,0:T(8,128)(2,1)S(1)}, u32[]{:S(2)}, u32[]{:S(2)}) %collective-permute-start.5) | collective-permute-done | bytes 393248 | tf_op jit(solution)/shard_map/ppermute | solution.py:142
  110.7 4.1 %collective-permute-start.8 = (bf16[4,48,1024]{2,1,0:T(8,128)(2,1)S(1)}, bf16[4,48,1024]{2,1,0:T(8,128)(2,1)S(1)}, u32[]{:S(2)}, u32[]{:S(2)}) collective-permute-start(bf16[4,48,1024]{2,1,0:T(8,128)(2,1)S(1)} %collective-permute-done.5.refs_5_), channel_id=1, source_target_pairs={{0,1},{1,0},{2,3},{3,2},{4,5},{5,4},{6,7},{7,6},{8,9},{9,8},{10,11... | collective-permute-start | bytes 1179656 | tf_op jit(solution)/shard_map/ppermute | solution.py:145
  114.8 0.7 copy-done
  115.5 0.0 collective-permute-done.7.refs_7_
  115.5 0.7 copy-done.2
  116.3 0.0 collective-permute-done.6.refs_6_
  116.3 0.0 collective-permute-done.8.refs_8_
  116.3 0.8 copy-done.4
  117.1 0.0 all-to-all-done.1.refs_9_
  117.1 1.0 copy-done.1
  118.1 1.0 copy-done.3
  119.1 1.0 copy-done.5
  120.1 4.4 %shard_map.47 = bf16[1536,768]{1,0:T(8,128)(2,1)} custom-call(bf16[2,48,1024]{2,1,0:T(8,128)(2,1)S(1)} %pad_maximum_fusion.3.refs_0_, bf16[2,48,1024]{2,1,0:T(8,128)(2,1)S(1)} %collective-permute-done.1.refs_1_, bf16[1,48,1024]{2,1,0:T(8,128)(2,1)S(1)} %collective-permute-done.2.refs_2_, bf16[4,48,1024]{2,1,0:T(8,128)(2,1)S(1)} %collective-permute-done.3.refs_3_, ...), custom_call_target="tpu_custom_call" | custom-call | tf_op jit(solution)/shard_map/pallas_call | solution.py:100
  (11 shorter events, 0.0 us)
Async XLA Ops:
  0.0 54.4 %copy-start.6 = (s32[3]{0:T(128)S(1)}, s32[3]{0:T(128)}, u32[]{:S(2)}) copy-start(s32[3]{0:T(128)} %offsets_ref.1) | copy-start | bytes 40
  0.0 54.4 %copy-start.7 = (f32[4]{0:T(128)S(1)}, f32[4]{0:T(128)}, u32[]{:S(2)}) copy-start(f32[4]{0:T(128)} %weights_ref.1) | copy-start | bytes 52
  0.0 54.4 %all-to-all-start = ((bf16[32,48,512]{2,1,0:T(8,128)(2,1)}), bf16[32,48,512]{2,1,0:T(8,128)(2,1)S(1)}, u32[]{:S(2)}, u32[]{:S(2)}) async-start(bf16[32,48,512]{2,1,0:T(8,128)(2,1)} %bitcast.7), calls=%async_computation | async-start | bytes 3145728 | tf_op jit(solution)/shard_map/all_to_all | solution.py:166
  57.0 60.0 %all-to-all-start.1 = ((bf16[16,2,48,512]{3,2,1,0:T(8,128)(2,1)}), bf16[16,2,48,512]{3,2,1,0:T(8,128)(2,1)S(1)}, u32[]{:S(2)}, u32[]{:S(2)}) async-start(bf16[16,2,48,512]{3,2,1,0:T(8,128)(2,1)} %get-tuple-element.8), calls=%async_computation.1 | async-start | bytes 3145728 | tf_op jit(solution)/shard_map/all_to_all | solution.py:168
  64.0 4.3 %collective-permute-start = (bf16[1,48,1024]{2,1,0:T(8,128)(2,1)S(1)}, bf16[1,48,1024]{2,1,0:T(8,128)(2,1)S(1)}, u32[]{:S(2)}, u32[]{:S(2)}) collective-permute-start(bf16[1,48,1024]{2,1,0:T(8,128)(2,1)S(1)} %bitcast.3), channel_id=1, source_target_pairs={{0,1},{1,0},{2,3},{3,2},{4,5},{5,4},{6,7},{7,6},{8,9},{9,8},{10,11... | collective-permute-start | bytes 294920 | tf_op jit(solution)/shard_map/ppermute | solution.py:145
  68.3 11.4 %collective-permute-start.1 = (bf16[2,48,1024]{2,1,0:T(8,128)(2,1)S(1)}, bf16[2,48,1024]{2,1,0:T(8,128)(2,1)S(1)}, u32[]{:S(2)}, u32[]{:S(2)}) collective-permute-start(bf16[2,48,1024]{2,1,0:T(8,128)(2,1)S(1)} %pad_maximum_fusion.3.refs_0_), channel_id=1, source_target_pairs={{0,2},{1,15},{2,4},{3,1},{4,6},{5,3},{6,8},{7,5},{8,10},{9,7},{10,... | collective-permute-start | bytes 589832 | tf_op jit(solution)/shard_map/ppermute | solution.py:150
  70.4 9.3 %collective-permute-start.2 = (bf16[1,48,1024]{2,1,0:T(8,128)(2,1)S(1)}, bf16[1,48,1024]{2,1,0:T(8,128)(2,1)S(1)}, u32[]{:S(2)}, u32[]{:S(2)}) collective-permute-start(bf16[1,48,1024]{2,1,0:T(8,128)(2,1)S(1)} %bitcast.5), channel_id=1, source_target_pairs={{0,8},{1,9},{2,10},{3,11},{4,12},{5,13},{6,14},{7,15},{8,0},{9,1},... | collective-permute-start | bytes 294920 | tf_op jit(solution)/shard_map/ppermute | solution.py:149
  79.8 14.4 %collective-permute-start.3 = (bf16[4,48,1024]{2,1,0:T(8,128)(2,1)S(1)}, bf16[4,48,1024]{2,1,0:T(8,128)(2,1)S(1)}, u32[]{:S(2)}, u32[]{:S(2)}) collective-permute-start(bf16[4,48,1024]{2,1,0:T(8,128)(2,1)S(1)} %get-tuple-element.10), channel_id=1, source_target_pairs={{0,4},{1,13},{2,6},{3,15},{4,8},{5,1},{6,10},{7,3},{8,12},{9,5},{1... | collective-permute-start | bytes 1179656 | tf_op jit(solution)/shard_map/ppermute | solution.py:151
  83.6 20.0 %collective-permute-start.4 = (bf16[4,48,1024]{2,1,0:T(8,128)(2,1)S(1)}, bf16[4,48,1024]{2,1,0:T(8,128)(2,1)S(1)}, u32[]{:S(2)}, u32[]{:S(2)}) collective-permute-start(bf16[4,48,1024]{2,1,0:T(8,128)(2,1)S(1)} %get-tuple-element.9), channel_id=1, source_target_pairs={{0,16},{1,17},{2,18},{3,19},{4,20},{5,21},{6,22},{7,23},{8,24},{9,... | collective-permute-start | bytes 1179656 | tf_op jit(solution)/shard_map/ppermute | solution.py:142
  94.1 16.6 %collective-permute-start.5 = (bf16[4,48,1024]{2,1,0:T(8,128)(2,1)S(1)}, bf16[4,48,1024]{2,1,0:T(8,128)(2,1)S(1)}, u32[]{:S(2)}, u32[]{:S(2)}) collective-permute-start(bf16[4,48,1024]{2,1,0:T(8,128)(2,1)S(1)} %collective-permute-done.3.refs_3_), channel_id=1, source_target_pairs={{0,16},{1,17},{2,18},{3,19},{4,20},{5,21},{6,22},{7,23},{8,24},{9,... | collective-permute-start | bytes 1179656 | tf_op jit(solution)/shard_map/ppermute | solution.py:142
  103.7 12.6 %collective-permute-start.6 = (bf16[7,48,1024]{2,1,0:T(8,128)(2,1)S(1)}, bf16[7,48,1024]{2,1,0:T(8,128)(2,1)S(1)}, u32[]{:S(2)}, u32[]{:S(2)}) collective-permute-start(bf16[7,48,1024]{2,1,0:T(8,128)(2,1)S(1)} %pad_maximum_fusion), channel_id=1, source_target_pairs={{0,1},{1,0},{2,3},{3,2},{4,5},{5,4},{6,7},{7,6},{8,9},{9,8},{10,11... | collective-permute-start | bytes 2064392 | tf_op jit(solution)/shard_map/ppermute | solution.py:145
  106.9 8.7 %collective-permute-start.7 = (bf16[4,48,1024]{2,1,0:T(8,128)(2,1)S(1)}, bf16[4,48,1024]{2,1,0:T(8,128)(2,1)S(1)}, u32[]{:S(2)}, u32[]{:S(2)}) collective-permute-start(bf16[4,48,1024]{2,1,0:T(8,128)(2,1)S(1)} %collective-permute-done.3.refs_3_), channel_id=1, source_target_pairs={{0,1},{1,0},{2,3},{3,2},{4,5},{5,4},{6,7},{7,6},{8,9},{9,8},{10,11... | collective-permute-start | bytes 1179656 | tf_op jit(solution)/shard_map/ppermute | solution.py:145
  110.7 5.6 %collective-permute-start.8 = (bf16[4,48,1024]{2,1,0:T(8,128)(2,1)S(1)}, bf16[4,48,1024]{2,1,0:T(8,128)(2,1)S(1)}, u32[]{:S(2)}, u32[]{:S(2)}) collective-permute-start(bf16[4,48,1024]{2,1,0:T(8,128)(2,1)S(1)} %collective-permute-done.5.refs_5_), channel_id=1, source_target_pairs={{0,1},{1,0},{2,3},{3,2},{4,5},{5,4},{6,7},{7,6},{8,9},{9,8},{10,11... | collective-permute-start | bytes 1179656 | tf_op jit(solution)/shard_map/ppermute | solution.py:145
  114.8 0.8 copy-start
  115.5 0.8 copy-start.2
  116.3 0.8 copy-start.4
  117.1 1.0 copy-start.1
  118.1 1.0 copy-start.3
  119.1 1.0 copy-start.5

commit v4 on v3

--- a/solution.py
+++ b/solution.py
@@ -14,6 +14,7 @@
 LANE = 128
 VMEM_LIMIT = 16 * 1024 * 1024
 SELECT_LIMIT = 10 * 1024 * 1024
+ASSEMBLE_LIMIT = 12 * 1024 * 1024
 
 
 def select_kernel(start_ref, offsets_ref, weights_ref, own_ref, chosen_ref, piece_ref):
@@ -58,30 +59,43 @@
     )(step_start, cell_offsets, stencil_weights, own)
 
 
-def gram_kernel(*refs):
-    count = len(LAYOUT)
-    pieces, right_ref, out_ref, left = refs[:count], refs[count], refs[count + 1], refs[count + 2]
-    tile = pl.program_id(0)
+def placed(layout):
+    column = lax.axis_index("col")
+    xh = column // (N_Z * N_C)
+    z = lax.rem(column // N_C, N_Z)
+    core = lax.rem(column, N_C)
+    for array, (side, holds) in enumerate(layout):
+        side_core = core if side == 0 else 1 - core
+        up = 1 - 2 * side_core
+        for index, (hop, other_x, other_core) in enumerate(holds):
+            from_z = lax.rem(z - hop * up + N_Z, N_Z)
+            from_core = 1 - side_core if other_core else side_core
+            from_xh = 1 - xh if other_x else xh
+            yield array, index, (from_xh * N_Z + from_z) * N_C + from_core
+
+
+def assemble_kernel(*refs):
+    pieces, left = refs[:-1], refs[-1]
+    piece = pieces[0].shape[1]
+    for array, index, at in placed(LAYOUT):
+        left[pl.ds(pl.multiple_of(at * piece, piece), piece), :] = pieces[array][index]
+
+
+def assemble(pieces, rows_dev):
+    vmem = pl.BlockSpec(memory_space=pltpu.VMEM)
+    return pl.pallas_call(
+        assemble_kernel,
+        out_shape=jax.ShapeDtypeStruct((rows_dev, pieces[0].shape[2]), jnp.bfloat16),
+        in_specs=[vmem] * len(pieces),
+        out_specs=vmem,
+        compiler_params=pltpu.CompilerParams(vmem_limit_bytes=ASSEMBLE_LIMIT),
+    )(*pieces)
+
+
+def gram_kernel(left_ref, right_ref, out_ref):
     tile_rows = out_ref.shape[0]
     row_count, steps, piece, cells = right_ref.shape
-
-    @pl.when(tile == 0)
-    def _():
-        column = lax.axis_index("col")
-        xh = column // (N_Z * N_C)
-        z = lax.rem(column // N_C, N_Z)
-        core = lax.rem(column, N_C)
-        for ref, (side, holds) in zip(pieces, LAYOUT):
-            side_core = core if side == 0 else 1 - core
-            up = 1 - 2 * side_core
-            for index, (hop, other_x, other_core) in enumerate(holds):
-                from_z = lax.rem(z - hop * up + N_Z, N_Z)
-                from_core = 1 - side_core if other_core else side_core
-                from_xh = 1 - xh if other_x else xh
-                at = ((from_xh * N_Z + from_z) * N_C + from_core) * piece
-                left[pl.ds(pl.multiple_of(at, piece), piece), :] = ref[index]
-
-    rows = left[pl.ds(pl.multiple_of(tile * tile_rows, tile_rows), tile_rows), :]
+    rows = left_ref[pl.ds(pl.multiple_of(pl.program_id(0) * tile_rows, tile_rows), tile_rows), :]
     total = None
     for s in range(steps):
         columns = right_ref[:, s].reshape(row_count * piece, cells)
@@ -93,19 +107,20 @@
     out_ref[...] = total.astype(out_ref.dtype)
 
 
-def gram(pieces, right, rows_dev):
+def gram(left, right):
     row_count, steps, piece, cells = right.shape
+    rows_dev = left.shape[0]
     width = row_count * piece
     tiles = 4
+    vmem = pl.BlockSpec(memory_space=pltpu.VMEM)
     return pl.pallas_call(
         gram_kernel,
         out_shape=jax.ShapeDtypeStruct((rows_dev, width), jnp.bfloat16),
         grid=(tiles,),
-        in_specs=[pl.BlockSpec(memory_space=pltpu.VMEM)] * (len(LAYOUT) + 1),
+        in_specs=[vmem, vmem],
         out_specs=pl.BlockSpec((rows_dev // tiles, width), lambda t: (t, 0)),
-        scratch_shapes=[pltpu.VMEM((rows_dev, steps * cells), jnp.bfloat16)],
         compiler_params=pltpu.CompilerParams(vmem_limit_bytes=VMEM_LIMIT),
-    )(*pieces, right)
+    )(left, right)
 
 
 def place(xh, z, core):
@@ -148,7 +163,8 @@
     pair = jnp.concatenate([own, swap_core(own)])
     far = lax.ppermute(own, "col", RING[4])
     first = lax.ppermute(pair, "col", RING[1])
-    second = lax.ppermute(jnp.concatenate([pair, first]), "col", RING[2])
+    doubled, first = lax.optimization_barrier((jnp.concatenate([pair, first]), first))
+    second = lax.ppermute(doubled, "col", RING[2])
     near = jnp.concatenate([first, far])
     near_x = swap_x(jnp.concatenate([own, near]))
     second_x = swap_x(second)
@@ -167,7 +183,7 @@
     chosen, piece = select(own, stencil_weights, cell_offsets, step_start)
     right = lax.all_to_all(chosen, "row", split_axis=0, concat_axis=0, tiled=True)
     pieces = gather_left(piece)
-    return gram(pieces, right, rows_dev)[None]
+    return gram(assemble(pieces, rows_dev), right)[None]
 
 
 def solution(mesh):

time: 126 us -> 122 us (0.968)
  local copies, waits for them, and re-layouts: 5.25 us -> 0.01 us
  starting transfers between devices: 56.8 us -> 54.4 us
  waiting for transfers between devices: 54.5 us -> 56.4 us
  Pallas kernels: 6.98 us -> 8.37 us
    ppermute x2, starting transfers between devices: 11.2 us -> 5.43 us  [swap_x(): return lax.ppermute(block, 'col', SWAP_X)]
    unnamed x16 -> x4, local copies, waits for them, and re-layouts: 5.25 us -> 0.01 us
    ppermute x1, waiting for transfers between devices: 3.77 us -> 7.9 us  [gather_left(): second = lax.ppermute(doubled, 'col', RING[2])]
    ppermute x1, waiting for transfers between devices: 3.75 us -> 0.01 us  [gather_left(): far = lax.ppermute(own, 'col', RING[4])]
    ppermute x4, starting transfers between devices: 12.5 us -> 14.9 us  [swap_core(): return lax.ppermute(block, 'col', SWAP_CORE)]
    ppermute x4, waiting for transfers between devices: 0.93 us -> 2.23 us  [swap_core(): return lax.ppermute(block, 'col', SWAP_CORE)]
  transfers between devices with their start and end apart: 11 -> 11, of which waited for: 6 -> 7; matrix products, arithmetic and copies ran while one was open for 0% -> 0% of each run, Pallas kernels for 0% -> 0%
where the time goes in v4:
time: 122 us; the launch traced here: 120 us
  waiting for transfers between devices  56.4 us (46%)
  starting transfers between devices  54.4 us (45%)
  Pallas kernels  8.37 us (7%)
    all_to_all x1, waiting for transfers between devices, local(): own = lax.all_to_all(blocks, 'col', split_axis=0, concat_axis=0, tiled=True)  39.2 us
    ppermute x4, starting transfers between devices, swap_core(): return lax.ppermute(block, 'col', SWAP_CORE)  14.9 us
    all_to_all x1, starting transfers between devices, local(): own = lax.all_to_all(blocks, 'col', split_axis=0, concat_axis=0, tiled=True)  14.6 us
    ppermute x1, waiting for transfers between devices, gather_left(): second = lax.ppermute(doubled, 'col', RING[2])  7.9 us
    all_to_all x1, starting transfers between devices, local(): lax.all_to_all(chosen, 'row', split_axis=0, concat_axis=0, tiled=True)  7 us
    ppermute x2, waiting for transfers between devices, swap_x(): return lax.ppermute(block, 'col', SWAP_X)  6.95 us
    ppermute x1, starting transfers between devices, gather_left(): far = lax.ppermute(own, 'col', RING[4])  5.56 us
    pallas_call x1, Pallas kernels, gram(): pl.pallas_call(gram_kernel, out_shape=jax.ShapeDtypeStruct((rows_dev, wid...  5.52 us
  transfers between devices with their start and end apart: 11, of which 7 were waited for; matrix products, arithmetic and copies ran while one was open for 0% of the time, Pallas kernels for 0%

profile of v4, /device:TPU:1, one launch (start us, length us, event | category | flops | bytes accessed | tf_op | source)
XLA Modules:
  0.0 120.2 jit_solution(10958692734650732717)
XLA Ops:
  0.0 0.0 copy-start
  0.0 0.0 copy-start.1
  0.0 14.6 %all-to-all-start = ((bf16[32,48,512]{2,1,0:T(8,128)(2,1)}), bf16[32,48,512]{2,1,0:T(8,128)(2,1)S(1)}, u32[]{:S(2)}, u32[]{:S(2)}) async-start(bf16[32,48,512]{2,1,0:T(8,128)(2,1)} %bitcast.8), calls=%async_computation | async-start | bytes 3145728 | tf_op jit(solution)/shard_map/all_to_all | solution.py:182
  15.2 39.2 %all-to-all-done.own_ref = bf16[32,48,512]{2,1,0:T(8,128)(2,1)S(1)} async-done(((bf16[32,48,512]{2,1,0:T(8,128)(2,1)}), bf16[32,48,512]{2,1,0:T(8,128)(2,1)S(1)}, u32[]{:S(2)}, u32[]{:S(2)}) %all-to-all-start) | async-done | bytes 1572896 | tf_op jit(solution)/shard_map/all_to_all | solution.py:182
  54.4 0.0 copy-done
  54.4 0.0 copy-done.1
  54.4 2.6 %shard_map.46 = (bf16[16,2,48,512]{3,2,1,0:T(8,128)(2,1)}, bf16[48,1024]{1,0:T(8,128)(2,1)S(1)}) custom-call(s32[1]{0:T(128)S(6)} %copy.5.start_ref, s32[3]{0:T(128)S(1)} %copy-done, f32[4]{0:T(128)S(1)} %copy-done.1, bf16[32,48,512]{2,1,0:T(8,128)(2,1)S(1)} %all-to-all-done.own_ref), custom_call_target="tpu_custom_call" | custom-call | tf_op jit(solution)/shard_map/pallas_call | solution.py:50
  57.0 7.0 %all-to-all-start.1 = ((bf16[16,2,48,512]{3,2,1,0:T(8,128)(2,1)}), bf16[16,2,48,512]{3,2,1,0:T(8,128)(2,1)}, u32[]{:S(2)}, u32[]{:S(2)}) async-start(bf16[16,2,48,512]{3,2,1,0:T(8,128)(2,1)} %get-tuple-element.12), calls=%async_computation.1 | async-start | bytes 3145728 | tf_op jit(solution)/shard_map/all_to_all | solution.py:184
  64.0 3.4 %collective-permute-start = (bf16[1,48,1024]{2,1,0:T(8,128)(2,1)S(1)}, bf16[1,48,1024]{2,1,0:T(8,128)(2,1)S(1)}, u32[]{:S(2)}, u32[]{:S(2)}) collective-permute-start(bf16[1,48,1024]{2,1,0:T(8,128)(2,1)S(1)} %bitcast.3), channel_id=1, source_target_pairs={{0,1},{1,0},{2,3},{3,2},{4,5},{5,4},{6,7},{7,6},{8,9},{9,8},{10,11... | collective-permute-start | bytes 294920 | tf_op jit(solution)/shard_map/ppermute | solution.py:160
  67.4 0.9 collective-permute-done
  68.3 2.1 %collective-permute-start.1 = (bf16[2,48,1024]{2,1,0:T(8,128)(2,1)S(1)}, bf16[2,48,1024]{2,1,0:T(8,128)(2,1)S(1)}, u32[]{:S(2)}, u32[]{:S(2)}) collective-permute-start(bf16[2,48,1024]{2,1,0:T(8,128)(2,1)S(1)} %pad_maximum_fusion.3.refs_0_), channel_id=1, source_target_pairs={{0,2},{1,15},{2,4},{3,1},{4,6},{5,3},{6,8},{7,5},{8,10},{9,7},{10,... | collective-permute-start | bytes 589832 | tf_op jit(solution)/shard_map/ppermute | solution.py:165
  70.4 5.6 %collective-permute-start.2 = (bf16[1,48,1024]{2,1,0:T(8,128)(2,1)S(1)}, bf16[1,48,1024]{2,1,0:T(8,128)(2,1)S(1)}, u32[]{:S(2)}, u32[]{:S(2)}) collective-permute-start(bf16[1,48,1024]{2,1,0:T(8,128)(2,1)S(1)} %bitcast.5), channel_id=1, source_target_pairs={{0,8},{1,9},{2,10},{3,11},{4,12},{5,13},{6,14},{7,15},{8,0},{9,1},... | collective-permute-start | bytes 294920 | tf_op jit(solution)/shard_map/ppermute | solution.py:164
  76.0 0.2 collective-permute-done.1.refs_1_
  76.2 4.9 %collective-permute-start.3 = (bf16[4,48,1024]{2,1,0:T(8,128)(2,1)S(1)}, bf16[4,48,1024]{2,1,0:T(8,128)(2,1)S(1)}, u32[]{:S(2)}, u32[]{:S(2)}) collective-permute-start(bf16[4,48,1024]{2,1,0:T(8,128)(2,1)S(1)} %fusion), channel_id=1, source_target_pairs={{0,4},{1,13},{2,6},{3,15},{4,8},{5,1},{6,10},{7,3},{8,12},{9,5},{1... | collective-permute-start | bytes 1179656 | tf_op jit(solution)/shard_map/ppermute | solution.py:167
  81.1 0.0 collective-permute-done.2.refs_2_
  81.2 2.7 %collective-permute-start.4 = (bf16[4,48,1024]{2,1,0:T(8,128)(2,1)S(1)}, bf16[4,48,1024]{2,1,0:T(8,128)(2,1)S(1)}, u32[]{:S(2)}, u32[]{:S(2)}) collective-permute-start(bf16[4,48,1024]{2,1,0:T(8,128)(2,1)S(1)} %fusion.1), channel_id=1, source_target_pairs={{0,16},{1,17},{2,18},{3,19},{4,20},{5,21},{6,22},{7,23},{8,24},{9,... | collective-permute-start | bytes 1179656 | tf_op jit(solution)/shard_map/ppermute | solution.py:157
  83.9 7.9 %collective-permute-done.3.refs_3_ = bf16[4,48,1024]{2,1,0:T(8,128)(2,1)S(1)} collective-permute-done((bf16[4,48,1024]{2,1,0:T(8,128)(2,1)S(1)}, bf16[4,48,1024]{2,1,0:T(8,128)(2,1)S(1)}, u32[]{:S(2)}, u32[]{:S(2)}) %collective-permute-start.3) | collective-permute-done | bytes 393248 | tf_op jit(solution)/shard_map/ppermute | solution.py:167
  91.8 2.7 %collective-permute-start.5 = (bf16[4,48,1024]{2,1,0:T(8,128)(2,1)S(1)}, bf16[4,48,1024]{2,1,0:T(8,128)(2,1)S(1)}, u32[]{:S(2)}, u32[]{:S(2)}) collective-permute-start(bf16[4,48,1024]{2,1,0:T(8,128)(2,1)S(1)} %collective-permute-done.3.refs_3_), channel_id=1, source_target_pairs={{0,16},{1,17},{2,18},{3,19},{4,20},{5,21},{6,22},{7,23},{8,24},{9,... | collective-permute-start | bytes 1179656 | tf_op jit(solution)/shard_map/ppermute | solution.py:157
  94.5 5.5 %collective-permute-done.4.refs_4_ = bf16[4,48,1024]{2,1,0:T(8,128)(2,1)S(1)} collective-permute-done((bf16[4,48,1024]{2,1,0:T(8,128)(2,1)S(1)}, bf16[4,48,1024]{2,1,0:T(8,128)(2,1)S(1)}, u32[]{:S(2)}, u32[]{:S(2)}) %collective-permute-start.4) | collective-permute-done | bytes 393248 | tf_op jit(solution)/shard_map/ppermute | solution.py:157
  100.0 0.1 pad_maximum_fusion
  100.1 6.0 %collective-permute-start.6 = (bf16[7,48,1024]{2,1,0:T(8,128)(2,1)S(1)}, bf16[7,48,1024]{2,1,0:T(8,128)(2,1)S(1)}, u32[]{:S(2)}, u32[]{:S(2)}) collective-permute-start(bf16[7,48,1024]{2,1,0:T(8,128)(2,1)S(1)} %pad_maximum_fusion), channel_id=1, source_target_pairs={{0,1},{1,0},{2,3},{3,2},{4,5},{5,4},{6,7},{7,6},{8,9},{9,8},{10,11... | collective-permute-start | bytes 2064392 | tf_op jit(solution)/shard_map/ppermute | solution.py:160
  106.1 1.9 %collective-permute-start.7 = (bf16[4,48,1024]{2,1,0:T(8,128)(2,1)S(1)}, bf16[4,48,1024]{2,1,0:T(8,128)(2,1)S(1)}, u32[]{:S(2)}, u32[]{:S(2)}) collective-permute-start(bf16[4,48,1024]{2,1,0:T(8,128)(2,1)S(1)} %collective-permute-done.3.refs_3_), channel_id=1, source_target_pairs={{0,1},{1,0},{2,3},{3,2},{4,5},{5,4},{6,7},{7,6},{8,9},{9,8},{10,11... | collective-permute-start | bytes 1179656 | tf_op jit(solution)/shard_map/ppermute | solution.py:160
  108.0 1.4 %collective-permute-done.5.refs_5_ = bf16[4,48,1024]{2,1,0:T(8,128)(2,1)S(1)} collective-permute-done((bf16[4,48,1024]{2,1,0:T(8,128)(2,1)S(1)}, bf16[4,48,1024]{2,1,0:T(8,128)(2,1)S(1)}, u32[]{:S(2)}, u32[]{:S(2)}) %collective-permute-start.5) | collective-permute-done | bytes 393248 | tf_op jit(solution)/shard_map/ppermute | solution.py:157
  109.5 3.6 %collective-permute-start.8 = (bf16[4,48,1024]{2,1,0:T(8,128)(2,1)S(1)}, bf16[4,48,1024]{2,1,0:T(8,128)(2,1)S(1)}, u32[]{:S(2)}, u32[]{:S(2)}) collective-permute-start(bf16[4,48,1024]{2,1,0:T(8,128)(2,1)S(1)} %collective-permute-done.5.refs_5_), channel_id=1, source_target_pairs={{0,1},{1,0},{2,3},{3,2},{4,5},{5,4},{6,7},{7,6},{8,9},{9,8},{10,11... | collective-permute-start | bytes 1179656 | tf_op jit(solution)/shard_map/ppermute | solution.py:160
  113.1 0.0 collective-permute-done.7.refs_7_
  113.1 0.0 collective-permute-done.6.refs_6_
  113.1 1.3 %collective-permute-done.8.refs_8_ = bf16[4,48,1024]{2,1,0:T(8,128)(2,1)S(1)} collective-permute-done((bf16[4,48,1024]{2,1,0:T(8,128)(2,1)S(1)}, bf16[4,48,1024]{2,1,0:T(8,128)(2,1)S(1)}, u32[]{:S(2)}, u32[]{:S(2)}) %collective-permute-start.8) | collective-permute-done | bytes 393248 | tf_op jit(solution)/shard_map/ppermute | solution.py:160
  114.5 0.2 shard_map.47.left_ref
  114.7 0.0 all-to-all-done.1.right_ref
  114.7 5.5 %shard_map.48 = bf16[1536,768]{1,0:T(8,128)(2,1)} custom-call(bf16[1536,1024]{1,0:T(8,128)(2,1)S(1)} %shard_map.47.left_ref, bf16[16,2,48,512]{3,2,1,0:T(8,128)(2,1)} %all-to-all-done.1.right_ref), custom_call_target="tpu_custom_call" | custom-call | tf_op jit(solution)/shard_map/pallas_call | solution.py:116
  (3 shorter events, 0.1 us)
Async XLA Ops:
  0.0 54.4 %copy-start = (s32[3]{0:T(128)S(1)}, s32[3]{0:T(128)}, u32[]{:S(2)}) copy-start(s32[3]{0:T(128)} %offsets_ref.1) | copy-start | bytes 40
  0.0 54.4 %copy-start.1 = (f32[4]{0:T(128)S(1)}, f32[4]{0:T(128)}, u32[]{:S(2)}) copy-start(f32[4]{0:T(128)} %weights_ref.1) | copy-start | bytes 52
  0.0 54.4 %all-to-all-start = ((bf16[32,48,512]{2,1,0:T(8,128)(2,1)}), bf16[32,48,512]{2,1,0:T(8,128)(2,1)S(1)}, u32[]{:S(2)}, u32[]{:S(2)}) async-start(bf16[32,48,512]{2,1,0:T(8,128)(2,1)} %bitcast.8), calls=%async_computation | async-start | bytes 3145728 | tf_op jit(solution)/shard_map/all_to_all | solution.py:182
  57.0 57.7 %all-to-all-start.1 = ((bf16[16,2,48,512]{3,2,1,0:T(8,128)(2,1)}), bf16[16,2,48,512]{3,2,1,0:T(8,128)(2,1)}, u32[]{:S(2)}, u32[]{:S(2)}) async-start(bf16[16,2,48,512]{3,2,1,0:T(8,128)(2,1)} %get-tuple-element.12), calls=%async_computation.1 | async-start | bytes 3145728 | tf_op jit(solution)/shard_map/all_to_all | solution.py:184
  64.0 4.3 %collective-permute-start = (bf16[1,48,1024]{2,1,0:T(8,128)(2,1)S(1)}, bf16[1,48,1024]{2,1,0:T(8,128)(2,1)S(1)}, u32[]{:S(2)}, u32[]{:S(2)}) collective-permute-start(bf16[1,48,1024]{2,1,0:T(8,128)(2,1)S(1)} %bitcast.3), channel_id=1, source_target_pairs={{0,1},{1,0},{2,3},{3,2},{4,5},{5,4},{6,7},{7,6},{8,9},{9,8},{10,11... | collective-permute-start | bytes 294920 | tf_op jit(solution)/shard_map/ppermute | solution.py:160
  68.3 7.9 %collective-permute-start.1 = (bf16[2,48,1024]{2,1,0:T(8,128)(2,1)S(1)}, bf16[2,48,1024]{2,1,0:T(8,128)(2,1)S(1)}, u32[]{:S(2)}, u32[]{:S(2)}) collective-permute-start(bf16[2,48,1024]{2,1,0:T(8,128)(2,1)S(1)} %pad_maximum_fusion.3.refs_0_), channel_id=1, source_target_pairs={{0,2},{1,15},{2,4},{3,1},{4,6},{5,3},{6,8},{7,5},{8,10},{9,7},{10,... | collective-permute-start | bytes 589832 | tf_op jit(solution)/shard_map/ppermute | solution.py:165
  70.4 10.7 %collective-permute-start.2 = (bf16[1,48,1024]{2,1,0:T(8,128)(2,1)S(1)}, bf16[1,48,1024]{2,1,0:T(8,128)(2,1)S(1)}, u32[]{:S(2)}, u32[]{:S(2)}) collective-permute-start(bf16[1,48,1024]{2,1,0:T(8,128)(2,1)S(1)} %bitcast.5), channel_id=1, source_target_pairs={{0,8},{1,9},{2,10},{3,11},{4,12},{5,13},{6,14},{7,15},{8,0},{9,1},... | collective-permute-start | bytes 294920 | tf_op jit(solution)/shard_map/ppermute | solution.py:164
  76.2 15.6 %collective-permute-start.3 = (bf16[4,48,1024]{2,1,0:T(8,128)(2,1)S(1)}, bf16[4,48,1024]{2,1,0:T(8,128)(2,1)S(1)}, u32[]{:S(2)}, u32[]{:S(2)}) collective-permute-start(bf16[4,48,1024]{2,1,0:T(8,128)(2,1)S(1)} %fusion), channel_id=1, source_target_pairs={{0,4},{1,13},{2,6},{3,15},{4,8},{5,1},{6,10},{7,3},{8,12},{9,5},{1... | collective-permute-start | bytes 1179656 | tf_op jit(solution)/shard_map/ppermute | solution.py:167
  81.2 18.9 %collective-permute-start.4 = (bf16[4,48,1024]{2,1,0:T(8,128)(2,1)S(1)}, bf16[4,48,1024]{2,1,0:T(8,128)(2,1)S(1)}, u32[]{:S(2)}, u32[]{:S(2)}) collective-permute-start(bf16[4,48,1024]{2,1,0:T(8,128)(2,1)S(1)} %fusion.1), channel_id=1, source_target_pairs={{0,16},{1,17},{2,18},{3,19},{4,20},{5,21},{6,22},{7,23},{8,24},{9,... | collective-permute-start | bytes 1179656 | tf_op jit(solution)/shard_map/ppermute | solution.py:157
  91.8 17.7 %collective-permute-start.5 = (bf16[4,48,1024]{2,1,0:T(8,128)(2,1)S(1)}, bf16[4,48,1024]{2,1,0:T(8,128)(2,1)S(1)}, u32[]{:S(2)}, u32[]{:S(2)}) collective-permute-start(bf16[4,48,1024]{2,1,0:T(8,128)(2,1)S(1)} %collective-permute-done.3.refs_3_), channel_id=1, source_target_pairs={{0,16},{1,17},{2,18},{3,19},{4,20},{5,21},{6,22},{7,23},{8,24},{9,... | collective-permute-start | bytes 1179656 | tf_op jit(solution)/shard_map/ppermute | solution.py:157
  100.1 13.0 %collective-permute-start.6 = (bf16[7,48,1024]{2,1,0:T(8,128)(2,1)S(1)}, bf16[7,48,1024]{2,1,0:T(8,128)(2,1)S(1)}, u32[]{:S(2)}, u32[]{:S(2)}) collective-permute-start(bf16[7,48,1024]{2,1,0:T(8,128)(2,1)S(1)} %pad_maximum_fusion), channel_id=1, source_target_pairs={{0,1},{1,0},{2,3},{3,2},{4,5},{5,4},{6,7},{7,6},{8,9},{9,8},{10,11... | collective-permute-start | bytes 2064392 | tf_op jit(solution)/shard_map/ppermute | solution.py:160
  106.1 7.0 %collective-permute-start.7 = (bf16[4,48,1024]{2,1,0:T(8,128)(2,1)S(1)}, bf16[4,48,1024]{2,1,0:T(8,128)(2,1)S(1)}, u32[]{:S(2)}, u32[]{:S(2)}) collective-permute-start(bf16[4,48,1024]{2,1,0:T(8,128)(2,1)S(1)} %collective-permute-done.3.refs_3_), channel_id=1, source_target_pairs={{0,1},{1,0},{2,3},{3,2},{4,5},{5,4},{6,7},{7,6},{8,9},{9,8},{10,11... | collective-permute-start | bytes 1179656 | tf_op jit(solution)/shard_map/ppermute | solution.py:160
  109.5 5.0 %collective-permute-start.8 = (bf16[4,48,1024]{2,1,0:T(8,128)(2,1)S(1)}, bf16[4,48,1024]{2,1,0:T(8,128)(2,1)S(1)}, u32[]{:S(2)}, u32[]{:S(2)}) collective-permute-start(bf16[4,48,1024]{2,1,0:T(8,128)(2,1)S(1)} %collective-permute-done.5.refs_5_), channel_id=1, source_target_pairs={{0,1},{1,0},{2,3},{3,2},{4,5},{5,4},{6,7},{7,6},{8,9},{9,8},{10,11... | collective-permute-start | bytes 1179656 | tf_op jit(solution)/shard_map/ppermute | solution.py:160

commit v5 on v4

--- a/solution.py
+++ b/solution.py
@@ -131,24 +131,16 @@
 SWAP_X = [(place(x, z, c), place(x + 1, z, c)) for x, z, c in PLACES]
 SWAP_CORE = [(place(x, z, c), place(x, z, c + 1)) for x, z, c in PLACES]
 RING = [[(place(x, z, c), place(x, z + hop * (1 - 2 * c), c)) for x, z, c in PLACES] for hop in range(5)]
-OWN, FIRST, FAR = [(0, 0, 0)], [(1, 0, 0), (1, 0, 1)], [(4, 0, 0)]
-SECOND = [(2, 0, 0), (2, 0, 1), (3, 0, 0), (3, 0, 1)]
+FAR, FAR_X = [(4, 0, 0)], [(4, 1, 0)]
 
 
-def across(holds):
-    return [(hop, 1, core) for hop, _, core in holds]
+def four(hop):
+    return [(hop, 0, 0), (hop, 1, 0), (hop, 0, 1), (hop, 1, 1)]
 
 
 LAYOUT = [
-    (0, [(0, 0, 0), (0, 0, 1)]),
-    (0, FIRST),
-    (0, FAR),
-    (0, SECOND),
-    (0, across(OWN + FIRST + FAR)),
-    (0, across(SECOND)),
-    (1, FIRST + FAR + across(OWN + FIRST + FAR)),
-    (1, SECOND),
-    (1, across(SECOND)),
+    (0, four(0)), (0, four(1)), (0, four(2)), (0, four(3)), (0, FAR), (0, FAR_X),
+    (1, four(1)), (1, four(2) + FAR + FAR_X), (1, four(3)),
 ]
 
 
@@ -159,19 +151,19 @@
     def swap_core(block):
         return lax.ppermute(block, "col", SWAP_CORE)
 
+    def along(block, hop):
+        return lax.ppermute(block, "col", RING[hop])
+
     own = piece[None]
-    pair = jnp.concatenate([own, swap_core(own)])
-    far = lax.ppermute(own, "col", RING[4])
-    first = lax.ppermute(pair, "col", RING[1])
-    doubled, first = lax.optimization_barrier((jnp.concatenate([pair, first]), first))
-    second = lax.ppermute(doubled, "col", RING[2])
-    near = jnp.concatenate([first, far])
-    near_x = swap_x(jnp.concatenate([own, near]))
-    second_x = swap_x(second)
-    return [
-        pair, first, far, second, near_x, second_x,
-        swap_core(jnp.concatenate([near, near_x])), swap_core(second), swap_core(second_x),
-    ]
+    far = along(own, 4)
+    two = jnp.concatenate([own, swap_x(own)])
+    base = jnp.concatenate([two, swap_core(two)])
+    base, far = lax.optimization_barrier((base, far))
+    first, second = along(base, 1), along(base, 2)
+    third = along(first, 2)
+    far_x = swap_x(far)
+    later = jnp.concatenate([second, far, far_x])
+    return [base, first, second, third, far, far_x, swap_core(first), swap_core(later), swap_core(third)]
 
 
 def local(sensitivity, stencil_weights, cell_offsets, step_start):

time: 122 us -> 130 us (1.066)
  the two profiles are of different devices: /device:TPU:1 before, /device:TPU:17 now
where the time goes in v5:
time: 130 us; the launch traced here: 129 us
  waiting for transfers between devices  64.2 us (49%)
  starting transfers between devices  55.9 us (43%)
  Pallas kernels  8.36 us (6%)
    all_to_all x1, waiting for transfers between devices, local(): own = lax.all_to_all(blocks, 'col', split_axis=0, concat_axis=0, tiled=True)  39.2 us
    ppermute x4, starting transfers between devices, swap_core(): return lax.ppermute(block, 'col', SWAP_CORE)  14.7 us
    ppermute x4, starting transfers between devices, along(): return lax.ppermute(block, 'col', RING[hop])  14.3 us
    all_to_all x1, starting transfers between devices, local(): own = lax.all_to_all(blocks, 'col', split_axis=0, concat_axis=0, tiled=True)  13.7 us
    ppermute x4, waiting for transfers between devices, along(): return lax.ppermute(block, 'col', RING[hop])  12.2 us
    ppermute x2, waiting for transfers between devices, swap_x(): return lax.ppermute(block, 'col', SWAP_X)  11.5 us
    all_to_all x1, starting transfers between devices, local(): lax.all_to_all(chosen, 'row', split_axis=0, concat_axis=0, tiled=True)  6.92 us
    ppermute x2, starting transfers between devices, swap_x(): return lax.ppermute(block, 'col', SWAP_X)  6.25 us
  transfers between devices with their start and end apart: 12, of which 7 were waited for; matrix products, arithmetic and copies ran while one was open for 0% of the time, Pallas kernels for 0%

profile of v5, /device:TPU:17, one launch (start us, length us, event | category | flops | bytes accessed | tf_op | source)
XLA Modules:
  0.0 129.4 jit_solution(3891794493982519453)
XLA Ops:
  0.0 0.0 copy-start
  0.0 0.0 copy-start.1
  0.0 13.7 %all-to-all-start = ((bf16[32,48,512]{2,1,0:T(8,128)(2,1)}), bf16[32,48,512]{2,1,0:T(8,128)(2,1)S(1)}, u32[]{:S(2)}, u32[]{:S(2)}) async-start(bf16[32,48,512]{2,1,0:T(8,128)(2,1)} %bitcast.7), calls=%async_computation | async-start | bytes 3145728 | tf_op jit(solution)/shard_map/all_to_all | solution.py:174
  14.4 39.2 %all-to-all-done.own_ref = bf16[32,48,512]{2,1,0:T(8,128)(2,1)S(1)} async-done(((bf16[32,48,512]{2,1,0:T(8,128)(2,1)}), bf16[32,48,512]{2,1,0:T(8,128)(2,1)S(1)}, u32[]{:S(2)}, u32[]{:S(2)}) %all-to-all-start) | async-done | bytes 1572896 | tf_op jit(solution)/shard_map/all_to_all | solution.py:174
  53.6 0.0 copy-done
  53.6 0.0 copy-done.1
  53.6 2.6 %shard_map.46 = (bf16[16,2,48,512]{3,2,1,0:T(8,128)(2,1)}, bf16[48,1024]{1,0:T(8,128)(2,1)S(1)}) custom-call(s32[1]{0:T(128)S(6)} %copy.5.start_ref, s32[3]{0:T(128)S(1)} %copy-done, f32[4]{0:T(128)S(1)} %copy-done.1, bf16[32,48,512]{2,1,0:T(8,128)(2,1)S(1)} %all-to-all-done.own_ref), custom_call_target="tpu_custom_call" | custom-call | tf_op jit(solution)/shard_map/pallas_call | solution.py:50
  56.2 6.9 %all-to-all-start.1 = ((bf16[16,2,48,512]{3,2,1,0:T(8,128)(2,1)}), bf16[16,2,48,512]{3,2,1,0:T(8,128)(2,1)}, u32[]{:S(2)}, u32[]{:S(2)}) async-start(bf16[16,2,48,512]{3,2,1,0:T(8,128)(2,1)} %get-tuple-element.12), calls=%async_computation.1 | async-start | bytes 3145728 | tf_op jit(solution)/shard_map/all_to_all | solution.py:176
  63.1 3.4 %collective-permute-start = (bf16[1,48,1024]{2,1,0:T(8,128)(2,1)S(1)}, bf16[1,48,1024]{2,1,0:T(8,128)(2,1)S(1)}, u32[]{:S(2)}, u32[]{:S(2)}) collective-permute-start(bf16[1,48,1024]{2,1,0:T(8,128)(2,1)S(1)} %bitcast.3), channel_id=1, source_target_pairs={{0,16},{1,17},{2,18},{3,19},{4,20},{5,21},{6,22},{7,23},{8,24},{9,... | collective-permute-start | bytes 294920 | tf_op jit(solution)/shard_map/ppermute | solution.py:149
  66.6 10.5 %collective-permute-done = bf16[1,48,1024]{2,1,0:T(8,128)(2,1)S(1)} collective-permute-done((bf16[1,48,1024]{2,1,0:T(8,128)(2,1)S(1)}, bf16[1,48,1024]{2,1,0:T(8,128)(2,1)S(1)}, u32[]{:S(2)}, u32[]{:S(2)}) %collective-permute-start) | collective-permute-done | bytes 98336 | tf_op jit(solution)/shard_map/ppermute | solution.py:149
  77.0 2.3 %collective-permute-start.1 = (bf16[2,48,1024]{2,1,0:T(8,128)(2,1)S(1)}, bf16[2,48,1024]{2,1,0:T(8,128)(2,1)S(1)}, u32[]{:S(2)}, u32[]{:S(2)}) collective-permute-start(bf16[2,48,1024]{2,1,0:T(8,128)(2,1)S(1)} %pad_maximum_fusion.2), channel_id=1, source_target_pairs={{0,1},{1,0},{2,3},{3,2},{4,5},{5,4},{6,7},{7,6},{8,9},{9,8},{10,11... | collective-permute-start | bytes 589832 | tf_op jit(solution)/shard_map/ppermute | solution.py:152
  79.4 4.1 %collective-permute-start.2 = (bf16[1,48,1024]{2,1,0:T(8,128)(2,1)S(1)}, bf16[1,48,1024]{2,1,0:T(8,128)(2,1)S(1)}, u32[]{:S(2)}, u32[]{:S(2)}) collective-permute-start(bf16[1,48,1024]{2,1,0:T(8,128)(2,1)S(1)} %bitcast.5), channel_id=1, source_target_pairs={{0,8},{1,9},{2,10},{3,11},{4,12},{5,13},{6,14},{7,15},{8,0},{9,1},... | collective-permute-start | bytes 294920 | tf_op jit(solution)/shard_map/ppermute | solution.py:155
  83.5 0.0 collective-permute-done.1
  83.5 8.2 %collective-permute-done.2.refs_4_ = bf16[1,48,1024]{2,1,0:T(8,128)(2,1)S(1)} collective-permute-done((bf16[1,48,1024]{2,1,0:T(8,128)(2,1)S(1)}, bf16[1,48,1024]{2,1,0:T(8,128)(2,1)S(1)}, u32[]{:S(2)}, u32[]{:S(2)}) %collective-permute-start.2) | collective-permute-done | bytes 98336 | tf_op jit(solution)/shard_map/ppermute | solution.py:155
  91.7 1.9 %collective-permute-start.3 = (bf16[4,48,1024]{2,1,0:T(8,128)(2,1)S(1)}, bf16[4,48,1024]{2,1,0:T(8,128)(2,1)S(1)}, u32[]{:S(2)}, u32[]{:S(2)}) collective-permute-start(bf16[4,48,1024]{2,1,0:T(8,128)(2,1)S(1)} %pad_maximum_fusion.1.refs_0_), channel_id=1, source_target_pairs={{0,2},{1,15},{2,4},{3,1},{4,6},{5,3},{6,8},{7,5},{8,10},{9,7},{10,... | collective-permute-start | bytes 1179656 | tf_op jit(solution)/shard_map/ppermute | solution.py:155
  93.7 4.4 %collective-permute-start.4 = (bf16[4,48,1024]{2,1,0:T(8,128)(2,1)S(1)}, bf16[4,48,1024]{2,1,0:T(8,128)(2,1)S(1)}, u32[]{:S(2)}, u32[]{:S(2)}) collective-permute-start(bf16[4,48,1024]{2,1,0:T(8,128)(2,1)S(1)} %pad_maximum_fusion.1.refs_0_), channel_id=1, source_target_pairs={{0,4},{1,13},{2,6},{3,15},{4,8},{5,1},{6,10},{7,3},{8,12},{9,5},{1... | collective-permute-start | bytes 1179656 | tf_op jit(solution)/shard_map/ppermute | solution.py:155
  98.1 2.8 %collective-permute-start.6 = (bf16[1,48,1024]{2,1,0:T(8,128)(2,1)S(1)}, bf16[1,48,1024]{2,1,0:T(8,128)(2,1)S(1)}, u32[]{:S(2)}, u32[]{:S(2)}) collective-permute-start(bf16[1,48,1024]{2,1,0:T(8,128)(2,1)S(1)} %collective-permute-done.2.refs_4_), channel_id=1, source_target_pairs={{0,16},{1,17},{2,18},{3,19},{4,20},{5,21},{6,22},{7,23},{8,24},{9,... | collective-permute-start | bytes 294920 | tf_op jit(solution)/shard_map/ppermute | solution.py:149
  100.9 0.0 collective-permute-done.3.refs_1_
  100.9 3.9 %collective-permute-start.5 = (bf16[4,48,1024]{2,1,0:T(8,128)(2,1)S(1)}, bf16[4,48,1024]{2,1,0:T(8,128)(2,1)S(1)}, u32[]{:S(2)}, u32[]{:S(2)}) collective-permute-start(bf16[4,48,1024]{2,1,0:T(8,128)(2,1)S(1)} %collective-permute-done.3.refs_1_), channel_id=1, source_target_pairs={{0,4},{1,13},{2,6},{3,15},{4,8},{5,1},{6,10},{7,3},{8,12},{9,5},{1... | collective-permute-start | bytes 1179656 | tf_op jit(solution)/shard_map/ppermute | solution.py:155
  104.8 1.0 collective-permute-done.6.refs_5_
  105.9 3.6 %collective-permute-done.4.refs_2_ = bf16[4,48,1024]{2,1,0:T(8,128)(2,1)S(1)} collective-permute-done((bf16[4,48,1024]{2,1,0:T(8,128)(2,1)S(1)}, bf16[4,48,1024]{2,1,0:T(8,128)(2,1)S(1)}, u32[]{:S(2)}, u32[]{:S(2)}) %collective-permute-start.4) | collective-permute-done | bytes 393248 | tf_op jit(solution)/shard_map/ppermute | solution.py:155
  109.5 0.1 pad_maximum_fusion
  109.5 1.9 %collective-permute-start.8 = (bf16[6,48,1024]{2,1,0:T(8,128)(2,1)S(1)}, bf16[6,48,1024]{2,1,0:T(8,128)(2,1)S(1)}, u32[]{:S(2)}, u32[]{:S(2)}) collective-permute-start(bf16[6,48,1024]{2,1,0:T(8,128)(2,1)S(1)} %pad_maximum_fusion), channel_id=1, source_target_pairs={{0,1},{1,0},{2,3},{3,2},{4,5},{5,4},{6,7},{7,6},{8,9},{9,8},{10,11... | collective-permute-start | bytes 1769480 | tf_op jit(solution)/shard_map/ppermute | solution.py:152
  111.5 2.4 %collective-permute-start.7 = (bf16[4,48,1024]{2,1,0:T(8,128)(2,1)S(1)}, bf16[4,48,1024]{2,1,0:T(8,128)(2,1)S(1)}, u32[]{:S(2)}, u32[]{:S(2)}) collective-permute-start(bf16[4,48,1024]{2,1,0:T(8,128)(2,1)S(1)} %collective-permute-done.3.refs_1_), channel_id=1, source_target_pairs={{0,1},{1,0},{2,3},{3,2},{4,5},{5,4},{6,7},{7,6},{8,9},{9,8},{10,11... | collective-permute-start | bytes 1179656 | tf_op jit(solution)/shard_map/ppermute | solution.py:152
  113.9 0.3 collective-permute-done.5.refs_3_
  114.2 8.0 %collective-permute-start.9 = (bf16[4,48,1024]{2,1,0:T(8,128)(2,1)S(1)}, bf16[4,48,1024]{2,1,0:T(8,128)(2,1)S(1)}, u32[]{:S(2)}, u32[]{:S(2)}) collective-permute-start(bf16[4,48,1024]{2,1,0:T(8,128)(2,1)S(1)} %collective-permute-done.5.refs_3_), channel_id=1, source_target_pairs={{0,1},{1,0},{2,3},{3,2},{4,5},{5,4},{6,7},{7,6},{8,9},{9,8},{10,11... | collective-permute-start | bytes 1179656 | tf_op jit(solution)/shard_map/ppermute | solution.py:152
  122.3 0.0 collective-permute-done.7.refs_6_
  122.3 0.0 collective-permute-done.8.refs_7_
  122.3 1.3 %collective-permute-done.9.refs_8_ = bf16[4,48,1024]{2,1,0:T(8,128)(2,1)S(1)} collective-permute-done((bf16[4,48,1024]{2,1,0:T(8,128)(2,1)S(1)}, bf16[4,48,1024]{2,1,0:T(8,128)(2,1)S(1)}, u32[]{:S(2)}, u32[]{:S(2)}) %collective-permute-start.9) | collective-permute-done | bytes 393248 | tf_op jit(solution)/shard_map/ppermute | solution.py:152
  123.6 0.2 shard_map.47.left_ref
  123.8 0.0 all-to-all-done.1.right_ref
  123.8 5.5 %shard_map.48 = bf16[1536,768]{1,0:T(8,128)(2,1)} custom-call(bf16[1536,1024]{1,0:T(8,128)(2,1)S(1)} %shard_map.47.left_ref, bf16[16,2,48,512]{3,2,1,0:T(8,128)(2,1)} %all-to-all-done.1.right_ref), custom_call_target="tpu_custom_call" | custom-call | tf_op jit(solution)/shard_map/pallas_call | solution.py:116
  (2 shorter events, 0.1 us)
Async XLA Ops:
  0.0 53.6 %copy-start = (s32[3]{0:T(128)S(1)}, s32[3]{0:T(128)}, u32[]{:S(2)}) copy-start(s32[3]{0:T(128)} %offsets_ref.1) | copy-start | bytes 40
  0.0 53.6 %copy-start.1 = (f32[4]{0:T(128)S(1)}, f32[4]{0:T(128)}, u32[]{:S(2)}) copy-start(f32[4]{0:T(128)} %weights_ref.1) | copy-start | bytes 52
  0.0 53.6 %all-to-all-start = ((bf16[32,48,512]{2,1,0:T(8,128)(2,1)}), bf16[32,48,512]{2,1,0:T(8,128)(2,1)S(1)}, u32[]{:S(2)}, u32[]{:S(2)}) async-start(bf16[32,48,512]{2,1,0:T(8,128)(2,1)} %bitcast.7), calls=%async_computation | async-start | bytes 3145728 | tf_op jit(solution)/shard_map/all_to_all | solution.py:174
  56.2 67.6 %all-to-all-start.1 = ((bf16[16,2,48,512]{3,2,1,0:T(8,128)(2,1)}), bf16[16,2,48,512]{3,2,1,0:T(8,128)(2,1)}, u32[]{:S(2)}, u32[]{:S(2)}) async-start(bf16[16,2,48,512]{3,2,1,0:T(8,128)(2,1)} %get-tuple-element.12), calls=%async_computation.1 | async-start | bytes 3145728 | tf_op jit(solution)/shard_map/all_to_all | solution.py:176
  63.1 13.9 %collective-permute-start = (bf16[1,48,1024]{2,1,0:T(8,128)(2,1)S(1)}, bf16[1,48,1024]{2,1,0:T(8,128)(2,1)S(1)}, u32[]{:S(2)}, u32[]{:S(2)}) collective-permute-start(bf16[1,48,1024]{2,1,0:T(8,128)(2,1)S(1)} %bitcast.3), channel_id=1, source_target_pairs={{0,16},{1,17},{2,18},{3,19},{4,20},{5,21},{6,22},{7,23},{8,24},{9,... | collective-permute-start | bytes 294920 | tf_op jit(solution)/shard_map/ppermute | solution.py:149
  77.0 6.4 %collective-permute-start.1 = (bf16[2,48,1024]{2,1,0:T(8,128)(2,1)S(1)}, bf16[2,48,1024]{2,1,0:T(8,128)(2,1)S(1)}, u32[]{:S(2)}, u32[]{:S(2)}) collective-permute-start(bf16[2,48,1024]{2,1,0:T(8,128)(2,1)S(1)} %pad_maximum_fusion.2), channel_id=1, source_target_pairs={{0,1},{1,0},{2,3},{3,2},{4,5},{5,4},{6,7},{7,6},{8,9},{9,8},{10,11... | collective-permute-start | bytes 589832 | tf_op jit(solution)/shard_map/ppermute | solution.py:152
  79.4 12.4 %collective-permute-start.2 = (bf16[1,48,1024]{2,1,0:T(8,128)(2,1)S(1)}, bf16[1,48,1024]{2,1,0:T(8,128)(2,1)S(1)}, u32[]{:S(2)}, u32[]{:S(2)}) collective-permute-start(bf16[1,48,1024]{2,1,0:T(8,128)(2,1)S(1)} %bitcast.5), channel_id=1, source_target_pairs={{0,8},{1,9},{2,10},{3,11},{4,12},{5,13},{6,14},{7,15},{8,0},{9,1},... | collective-permute-start | bytes 294920 | tf_op jit(solution)/shard_map/ppermute | solution.py:155
  91.7 9.2 %collective-permute-start.3 = (bf16[4,48,1024]{2,1,0:T(8,128)(2,1)S(1)}, bf16[4,48,1024]{2,1,0:T(8,128)(2,1)S(1)}, u32[]{:S(2)}, u32[]{:S(2)}) collective-permute-start(bf16[4,48,1024]{2,1,0:T(8,128)(2,1)S(1)} %pad_maximum_fusion.1.refs_0_), channel_id=1, source_target_pairs={{0,2},{1,15},{2,4},{3,1},{4,6},{5,3},{6,8},{7,5},{8,10},{9,7},{10,... | collective-permute-start | bytes 1179656 | tf_op jit(solution)/shard_map/ppermute | solution.py:155
  93.7 15.8 %collective-permute-start.4 = (bf16[4,48,1024]{2,1,0:T(8,128)(2,1)S(1)}, bf16[4,48,1024]{2,1,0:T(8,128)(2,1)S(1)}, u32[]{:S(2)}, u32[]{:S(2)}) collective-permute-start(bf16[4,48,1024]{2,1,0:T(8,128)(2,1)S(1)} %pad_maximum_fusion.1.refs_0_), channel_id=1, source_target_pairs={{0,4},{1,13},{2,6},{3,15},{4,8},{5,1},{6,10},{7,3},{8,12},{9,5},{1... | collective-permute-start | bytes 1179656 | tf_op jit(solution)/shard_map/ppermute | solution.py:155
  98.1 7.8 %collective-permute-start.6 = (bf16[1,48,1024]{2,1,0:T(8,128)(2,1)S(1)}, bf16[1,48,1024]{2,1,0:T(8,128)(2,1)S(1)}, u32[]{:S(2)}, u32[]{:S(2)}) collective-permute-start(bf16[1,48,1024]{2,1,0:T(8,128)(2,1)S(1)} %collective-permute-done.2.refs_4_), channel_id=1, source_target_pairs={{0,16},{1,17},{2,18},{3,19},{4,20},{5,21},{6,22},{7,23},{8,24},{9,... | collective-permute-start | bytes 294920 | tf_op jit(solution)/shard_map/ppermute | solution.py:149
  100.9 13.3 %collective-permute-start.5 = (bf16[4,48,1024]{2,1,0:T(8,128)(2,1)S(1)}, bf16[4,48,1024]{2,1,0:T(8,128)(2,1)S(1)}, u32[]{:S(2)}, u32[]{:S(2)}) collective-permute-start(bf16[4,48,1024]{2,1,0:T(8,128)(2,1)S(1)} %collective-permute-done.3.refs_1_), channel_id=1, source_target_pairs={{0,4},{1,13},{2,6},{3,15},{4,8},{5,1},{6,10},{7,3},{8,12},{9,5},{1... | collective-permute-start | bytes 1179656 | tf_op jit(solution)/shard_map/ppermute | solution.py:155
  109.5 12.7 %collective-permute-start.8 = (bf16[6,48,1024]{2,1,0:T(8,128)(2,1)S(1)}, bf16[6,48,1024]{2,1,0:T(8,128)(2,1)S(1)}, u32[]{:S(2)}, u32[]{:S(2)}) collective-permute-start(bf16[6,48,1024]{2,1,0:T(8,128)(2,1)S(1)} %pad_maximum_fusion), channel_id=1, source_target_pairs={{0,1},{1,0},{2,3},{3,2},{4,5},{5,4},{6,7},{7,6},{8,9},{9,8},{10,11... | collective-permute-start | bytes 1769480 | tf_op jit(solution)/shard_map/ppermute | solution.py:152
  111.5 10.8 %collective-permute-start.7 = (bf16[4,48,1024]{2,1,0:T(8,128)(2,1)S(1)}, bf16[4,48,1024]{2,1,0:T(8,128)(2,1)S(1)}, u32[]{:S(2)}, u32[]{:S(2)}) collective-permute-start(bf16[4,48,1024]{2,1,0:T(8,128)(2,1)S(1)} %collective-permute-done.3.refs_1_), channel_id=1, source_target_pairs={{0,1},{1,0},{2,3},{3,2},{4,5},{5,4},{6,7},{7,6},{8,9},{9,8},{10,11... | collective-permute-start | bytes 1179656 | tf_op jit(solution)/shard_map/ppermute | solution.py:152
  114.2 9.4 %collective-permute-start.9 = (bf16[4,48,1024]{2,1,0:T(8,128)(2,1)S(1)}, bf16[4,48,1024]{2,1,0:T(8,128)(2,1)S(1)}, u32[]{:S(2)}, u32[]{:S(2)}) collective-permute-start(bf16[4,48,1024]{2,1,0:T(8,128)(2,1)S(1)} %collective-permute-done.5.refs_3_), channel_id=1, source_target_pairs={{0,1},{1,0},{2,3},{3,2},{4,5},{5,4},{6,7},{7,6},{8,9},{9,8},{10,11... | collective-permute-start | bytes 1179656 | tf_op jit(solution)/shard_map/ppermute | solution.py:152

commit v6 on v5

--- a/solution.py
+++ b/solution.py
@@ -17,10 +17,9 @@
 ASSEMBLE_LIMIT = 12 * 1024 * 1024
 
 
-def select_kernel(start_ref, offsets_ref, weights_ref, own_ref, chosen_ref, piece_ref):
+def smooth_kernel(start_ref, offsets_ref, weights_ref, own_ref, piece_ref):
     count, rows, cells = own_ref.shape
-    start = lax.rem(start_ref[0], count)
-    first = lax.rem(STEPS * lax.axis_index("row") + start, count)
+    first = lax.rem(STEPS * lax.axis_index("row") + lax.rem(start_ref[0], count), count)
     for s in range(STEPS):
         here = lax.rem(first + s, count)
         left = own_ref[lax.rem(here + count - 1, count)][:, cells - LANE:].astype(jnp.float32)
@@ -38,25 +37,40 @@
             total = total + weights_ref[m + 1] * (forward + backward)
         piece_ref[:, s * cells:(s + 1) * cells] = total.astype(jnp.bfloat16)
 
+
+def smooth(own, stencil_weights, cell_offsets, step_start):
+    _, rows, cells = own.shape
+    smem = pl.BlockSpec(memory_space=pltpu.SMEM)
+    vmem = pl.BlockSpec(memory_space=pltpu.VMEM)
+    return pl.pallas_call(
+        smooth_kernel,
+        out_shape=jax.ShapeDtypeStruct((rows, STEPS * cells), own.dtype),
+        in_specs=[smem, smem, smem, vmem],
+        out_specs=vmem,
+        compiler_params=pltpu.CompilerParams(vmem_limit_bytes=SELECT_LIMIT),
+    )(step_start, cell_offsets, stencil_weights, own)
+
+
+def order_kernel(start_ref, own_ref, chosen_ref):
+    count = own_ref.shape[0]
+    start = lax.rem(start_ref[0], count)
+
     @pl.loop(0, count)
     def _(t):
         chosen_ref[t // STEPS, lax.rem(t, STEPS)] = own_ref[lax.rem(t + start, count)]
 
 
-def select(own, stencil_weights, cell_offsets, step_start):
+def order(own, step_start):
     count, rows, cells = own.shape
-    smem = pl.BlockSpec(memory_space=pltpu.SMEM)
-    vmem = pl.BlockSpec(memory_space=pltpu.VMEM)
-    return pl.pallas_call(
-        select_kernel,
-        out_shape=(
-            jax.ShapeDtypeStruct((count // STEPS, STEPS, rows, cells), own.dtype),
-            jax.ShapeDtypeStruct((rows, STEPS * cells), own.dtype),
-        ),
-        in_specs=[smem, smem, smem, vmem],
-        out_specs=(vmem, vmem),
+    vmem = pl.BlockSpec(memory_space=pltpu.VMEM)
+    return pl.pallas_call(
+        order_kernel,
+        out_shape=jax.ShapeDtypeStruct((count // STEPS, STEPS, rows, cells), own.dtype),
+        in_specs=[pl.BlockSpec(memory_space=pltpu.SMEM), vmem],
+        out_specs=vmem,
         compiler_params=pltpu.CompilerParams(vmem_limit_bytes=SELECT_LIMIT),
-    )(step_start, cell_offsets, stencil_weights, own)
+        cost_estimate=pl.CostEstimate(flops=0, bytes_accessed=4 * own.size, transcendentals=0),
+    )(step_start, own)
 
 
 def placed(layout):
@@ -144,21 +158,21 @@
 ]
 
 
-def gather_left(piece):
-    def swap_x(block):
-        return lax.ppermute(block, "col", SWAP_X)
-
-    def swap_core(block):
-        return lax.ppermute(block, "col", SWAP_CORE)
-
-    def along(block, hop):
-        return lax.ppermute(block, "col", RING[hop])
-
-    own = piece[None]
-    far = along(own, 4)
-    two = jnp.concatenate([own, swap_x(own)])
+def swap_x(block):
+    return lax.ppermute(block, "col", SWAP_X)
+
+
+def swap_core(block):
+    return lax.ppermute(block, "col", SWAP_CORE)
+
+
+def along(block, hop):
+    return lax.ppermute(block, "col", RING[hop])
+
+
+def gather_left(piece, piece_x, far):
+    two = jnp.concatenate([piece, piece_x])
     base = jnp.concatenate([two, swap_core(two)])
-    base, far = lax.optimization_barrier((base, far))
     first, second = along(base, 1), along(base, 2)
     third = along(first, 2)
     far_x = swap_x(far)
@@ -172,9 +186,13 @@
     piece_rows = rows_dev // col_count
     blocks = sensitivity.reshape(col_count, piece_rows, cells_dev)
     own = lax.all_to_all(blocks, "col", split_axis=0, concat_axis=0, tiled=True)
-    chosen, piece = select(own, stencil_weights, cell_offsets, step_start)
+    piece = smooth(own, stencil_weights, cell_offsets, step_start)[None]
+    far = along(piece, 4)
+    piece_x = swap_x(piece)
+    chosen = order(own, step_start)
+    chosen, piece_x, far = lax.optimization_barrier((chosen, piece_x, far))
     right = lax.all_to_all(chosen, "row", split_axis=0, concat_axis=0, tiled=True)
-    pieces = gather_left(piece)
+    pieces = gather_left(piece, piece_x, far)
     return gram(assemble(pieces, rows_dev), right)[None]
 
 

time: 130 us -> 117 us (0.900)
  the two profiles are of different devices: /device:TPU:17 before, /device:TPU:1 now
where the time goes in v6:
time: 117 us; the launch traced here: 116 us
  starting transfers between devices  61.1 us (52%)
  waiting for transfers between devices  45.2 us (39%)
  Pallas kernels  8.37 us (7%)
    all_to_all x1, waiting for transfers between devices, local(): own = lax.all_to_all(blocks, 'col', split_axis=0, concat_axis=0, tiled=True)  39.2 us
    ppermute x4, starting transfers between devices, along(): return lax.ppermute(block, 'col', RING[hop])  19 us
    all_to_all x1, starting transfers between devices, local(): own = lax.all_to_all(blocks, 'col', split_axis=0, concat_axis=0, tiled=True)  14.6 us
    ppermute x4, starting transfers between devices, swap_core(): return lax.ppermute(block, 'col', SWAP_CORE)  13.7 us
    all_to_all x1, starting transfers between devices, local(): lax.all_to_all(chosen, 'row', split_axis=0, concat_axis=0, tiled=True)  7 us
    ppermute x2, starting transfers between devices, swap_x(): return lax.ppermute(block, 'col', SWAP_X)  6.86 us
    pallas_call x1, Pallas kernels, gram(): pl.pallas_call(gram_kernel, out_shape=jax.ShapeDtypeStruct((rows_dev, wid...  5.52 us
    ppermute x4, waiting for transfers between devices, along(): return lax.ppermute(block, 'col', RING[hop])  2.69 us
  transfers between devices with their start and end apart: 12, of which 7 were waited for; matrix products, arithmetic and copies ran while one was open for 0% of the time, Pallas kernels for 2%

profile of v6, /device:TPU:1, one launch (start us, length us, event | category | flops | bytes accessed | tf_op | source)
XLA Modules:
  0.0 115.6 jit_solution(4447959350927353557)
XLA Ops:
  0.0 0.0 copy-start
  0.0 14.6 %all-to-all-start = ((bf16[32,48,512]{2,1,0:T(8,128)(2,1)}), bf16[32,48,512]{2,1,0:T(8,128)(2,1)S(1)}, u32[]{:S(2)}, u32[]{:S(2)}) async-start(bf16[32,48,512]{2,1,0:T(8,128)(2,1)} %bitcast.7), calls=%async_computation | async-start | bytes 3145728 | tf_op jit(solution)/shard_map/all_to_all | solution.py:188
  15.2 39.2 %all-to-all-done.own_ref = bf16[32,48,512]{2,1,0:T(8,128)(2,1)S(1)} async-done(((bf16[32,48,512]{2,1,0:T(8,128)(2,1)}), bf16[32,48,512]{2,1,0:T(8,128)(2,1)S(1)}, u32[]{:S(2)}, u32[]{:S(2)}) %all-to-all-start) | async-done | bytes 1572896 | tf_op jit(solution)/shard_map/all_to_all | solution.py:188
  54.4 0.0 copy-done
  54.4 0.0 copy-done.1
  54.4 1.0 shard_map.46
  55.4 3.1 %collective-permute-start.1 = (bf16[1,48,1024]{2,1,0:T(8,128)(2,1)S(1)}, bf16[1,48,1024]{2,1,0:T(8,128)(2,1)S(1)}, u32[]{:S(2)}, u32[]{:S(2)}) collective-permute-start(bf16[1,48,1024]{2,1,0:T(8,128)(2,1)S(1)} %bitcast.3), channel_id=1, source_target_pairs={{0,8},{1,9},{2,10},{3,11},{4,12},{5,13},{6,14},{7,15},{8,0},{9,1},... | collective-permute-start | bytes 294920 | tf_op jit(solution)/shard_map/ppermute | solution.py:170
  58.6 4.1 %collective-permute-start = (bf16[1,48,1024]{2,1,0:T(8,128)(2,1)S(1)}, bf16[1,48,1024]{2,1,0:T(8,128)(2,1)S(1)}, u32[]{:S(2)}, u32[]{:S(2)}) collective-permute-start(bf16[1,48,1024]{2,1,0:T(8,128)(2,1)S(1)} %bitcast.4), channel_id=1, source_target_pairs={{0,16},{1,17},{2,18},{3,19},{4,20},{5,21},{6,22},{7,23},{8,24},{9,... | collective-permute-start | bytes 294920 | tf_op jit(solution)/shard_map/ppermute | solution.py:162
  62.7 1.6 %shard_map.47 = bf16[16,2,48,512]{3,2,1,0:T(8,128)(2,1)} custom-call(s32[1]{0:T(128)S(6)} %copy.5.start_ref, bf16[32,48,512]{2,1,0:T(8,128)(2,1)S(1)} %all-to-all-done.own_ref), custom_call_target="tpu_custom_call" | custom-call | bytes 3145728 | tf_op jit(solution)/shard_map/pallas_call | solution.py:66
  64.3 0.5 collective-permute-done.1.refs_4_
  64.8 0.9 collective-permute-done
  65.7 7.0 %all-to-all-start.1 = ((bf16[16,2,48,512]{3,2,1,0:T(8,128)(2,1)}), bf16[16,2,48,512]{3,2,1,0:T(8,128)(2,1)}, u32[]{:S(2)}, u32[]{:S(2)}) async-start(bf16[16,2,48,512]{3,2,1,0:T(8,128)(2,1)} %shard_map.47), calls=%async_computation.1 | async-start | bytes 3145728 | tf_op jit(solution)/shard_map/all_to_all | solution.py:194
  72.8 4.3 %collective-permute-start.2 = (bf16[2,48,1024]{2,1,0:T(8,128)(2,1)S(1)}, bf16[2,48,1024]{2,1,0:T(8,128)(2,1)S(1)}, u32[]{:S(2)}, u32[]{:S(2)}) collective-permute-start(bf16[2,48,1024]{2,1,0:T(8,128)(2,1)S(1)} %pad_maximum_fusion.2), channel_id=1, source_target_pairs={{0,1},{1,0},{2,3},{3,2},{4,5},{5,4},{6,7},{7,6},{8,9},{9,8},{10,11... | collective-permute-start | bytes 589832 | tf_op jit(solution)/shard_map/ppermute | solution.py:166
  77.1 1.0 collective-permute-done.2
  78.2 4.7 %collective-permute-start.3 = (bf16[4,48,1024]{2,1,0:T(8,128)(2,1)S(1)}, bf16[4,48,1024]{2,1,0:T(8,128)(2,1)S(1)}, u32[]{:S(2)}, u32[]{:S(2)}) collective-permute-start(bf16[4,48,1024]{2,1,0:T(8,128)(2,1)S(1)} %pad_maximum_fusion.1.refs_0_), channel_id=1, source_target_pairs={{0,2},{1,15},{2,4},{3,1},{4,6},{5,3},{6,8},{7,5},{8,10},{9,7},{10,... | collective-permute-start | bytes 1179656 | tf_op jit(solution)/shard_map/ppermute | solution.py:170
  82.9 5.0 %collective-permute-start.4 = (bf16[4,48,1024]{2,1,0:T(8,128)(2,1)S(1)}, bf16[4,48,1024]{2,1,0:T(8,128)(2,1)S(1)}, u32[]{:S(2)}, u32[]{:S(2)}) collective-permute-start(bf16[4,48,1024]{2,1,0:T(8,128)(2,1)S(1)} %pad_maximum_fusion.1.refs_0_), channel_id=1, source_target_pairs={{0,4},{1,13},{2,6},{3,15},{4,8},{5,1},{6,10},{7,3},{8,12},{9,5},{1... | collective-permute-start | bytes 1179656 | tf_op jit(solution)/shard_map/ppermute | solution.py:170
  87.9 2.7 %collective-permute-start.6 = (bf16[1,48,1024]{2,1,0:T(8,128)(2,1)S(1)}, bf16[1,48,1024]{2,1,0:T(8,128)(2,1)S(1)}, u32[]{:S(2)}, u32[]{:S(2)}) collective-permute-start(bf16[1,48,1024]{2,1,0:T(8,128)(2,1)S(1)} %collective-permute-done.1.refs_4_), channel_id=1, source_target_pairs={{0,16},{1,17},{2,18},{3,19},{4,20},{5,21},{6,22},{7,23},{8,24},{9,... | collective-permute-start | bytes 294920 | tf_op jit(solution)/shard_map/ppermute | solution.py:162
  90.7 0.0 collective-permute-done.3.refs_1_
  90.7 6.1 %collective-permute-start.5 = (bf16[4,48,1024]{2,1,0:T(8,128)(2,1)S(1)}, bf16[4,48,1024]{2,1,0:T(8,128)(2,1)S(1)}, u32[]{:S(2)}, u32[]{:S(2)}) collective-permute-start(bf16[4,48,1024]{2,1,0:T(8,128)(2,1)S(1)} %collective-permute-done.3.refs_1_), channel_id=1, source_target_pairs={{0,4},{1,13},{2,6},{3,15},{4,8},{5,1},{6,10},{7,3},{8,12},{9,5},{1... | collective-permute-start | bytes 1179656 | tf_op jit(solution)/shard_map/ppermute | solution.py:170
  96.8 0.0 collective-permute-done.6.refs_5_
  96.8 1.2 %collective-permute-done.4.refs_2_ = bf16[4,48,1024]{2,1,0:T(8,128)(2,1)S(1)} collective-permute-done((bf16[4,48,1024]{2,1,0:T(8,128)(2,1)S(1)}, bf16[4,48,1024]{2,1,0:T(8,128)(2,1)S(1)}, u32[]{:S(2)}, u32[]{:S(2)}) %collective-permute-start.4) | collective-permute-done | bytes 393248 | tf_op jit(solution)/shard_map/ppermute | solution.py:170
  98.0 0.1 pad_maximum_fusion
  98.1 4.7 %collective-permute-start.8 = (bf16[6,48,1024]{2,1,0:T(8,128)(2,1)S(1)}, bf16[6,48,1024]{2,1,0:T(8,128)(2,1)S(1)}, u32[]{:S(2)}, u32[]{:S(2)}) collective-permute-start(bf16[6,48,1024]{2,1,0:T(8,128)(2,1)S(1)} %pad_maximum_fusion), channel_id=1, source_target_pairs={{0,1},{1,0},{2,3},{3,2},{4,5},{5,4},{6,7},{7,6},{8,9},{9,8},{10,11... | collective-permute-start | bytes 1769480 | tf_op jit(solution)/shard_map/ppermute | solution.py:166
  102.8 1.9 %collective-permute-start.7 = (bf16[4,48,1024]{2,1,0:T(8,128)(2,1)S(1)}, bf16[4,48,1024]{2,1,0:T(8,128)(2,1)S(1)}, u32[]{:S(2)}, u32[]{:S(2)}) collective-permute-start(bf16[4,48,1024]{2,1,0:T(8,128)(2,1)S(1)} %collective-permute-done.3.refs_1_), channel_id=1, source_target_pairs={{0,1},{1,0},{2,3},{3,2},{4,5},{5,4},{6,7},{7,6},{8,9},{9,8},{10,11... | collective-permute-start | bytes 1179656 | tf_op jit(solution)/shard_map/ppermute | solution.py:166
  104.7 1.0 collective-permute-done.5.refs_3_
  105.7 2.8 %collective-permute-start.9 = (bf16[4,48,1024]{2,1,0:T(8,128)(2,1)S(1)}, bf16[4,48,1024]{2,1,0:T(8,128)(2,1)S(1)}, u32[]{:S(2)}, u32[]{:S(2)}) collective-permute-start(bf16[4,48,1024]{2,1,0:T(8,128)(2,1)S(1)} %collective-permute-done.5.refs_3_), channel_id=1, source_target_pairs={{0,1},{1,0},{2,3},{3,2},{4,5},{5,4},{6,7},{7,6},{8,9},{9,8},{10,11... | collective-permute-start | bytes 1179656 | tf_op jit(solution)/shard_map/ppermute | solution.py:166
  108.5 0.0 collective-permute-done.7.refs_6_
  108.5 0.0 collective-permute-done.8.refs_7_
  108.5 1.3 %collective-permute-done.9.refs_8_ = bf16[4,48,1024]{2,1,0:T(8,128)(2,1)S(1)} collective-permute-done((bf16[4,48,1024]{2,1,0:T(8,128)(2,1)S(1)}, bf16[4,48,1024]{2,1,0:T(8,128)(2,1)S(1)}, u32[]{:S(2)}, u32[]{:S(2)}) %collective-permute-start.9) | collective-permute-done | bytes 393248 | tf_op jit(solution)/shard_map/ppermute | solution.py:166
  109.9 0.2 shard_map.48.left_ref
  110.1 0.0 all-to-all-done.1.right_ref
  110.1 5.5 %shard_map.49 = bf16[1536,768]{1,0:T(8,128)(2,1)} custom-call(bf16[1536,1024]{1,0:T(8,128)(2,1)S(1)} %shard_map.48.left_ref, bf16[16,2,48,512]{3,2,1,0:T(8,128)(2,1)} %all-to-all-done.1.right_ref), custom_call_target="tpu_custom_call" | custom-call | tf_op jit(solution)/shard_map/pallas_call | solution.py:130
  (3 shorter events, 0.1 us)
Async XLA Ops:
  0.0 54.4 %copy-start = (s32[3]{0:T(128)S(1)}, s32[3]{0:T(128)}, u32[]{:S(2)}) copy-start(s32[3]{0:T(128)} %offsets_ref.1) | copy-start | bytes 40
  0.0 54.4 %copy-start.1 = (f32[4]{0:T(128)S(1)}, f32[4]{0:T(128)}, u32[]{:S(2)}) copy-start(f32[4]{0:T(128)} %weights_ref.1) | copy-start | bytes 52
  0.0 54.4 %all-to-all-start = ((bf16[32,48,512]{2,1,0:T(8,128)(2,1)}), bf16[32,48,512]{2,1,0:T(8,128)(2,1)S(1)}, u32[]{:S(2)}, u32[]{:S(2)}) async-start(bf16[32,48,512]{2,1,0:T(8,128)(2,1)} %bitcast.7), calls=%async_computation | async-start | bytes 3145728 | tf_op jit(solution)/shard_map/all_to_all | solution.py:188
  55.4 9.4 %collective-permute-start.1 = (bf16[1,48,1024]{2,1,0:T(8,128)(2,1)S(1)}, bf16[1,48,1024]{2,1,0:T(8,128)(2,1)S(1)}, u32[]{:S(2)}, u32[]{:S(2)}) collective-permute-start(bf16[1,48,1024]{2,1,0:T(8,128)(2,1)S(1)} %bitcast.3), channel_id=1, source_target_pairs={{0,8},{1,9},{2,10},{3,11},{4,12},{5,13},{6,14},{7,15},{8,0},{9,1},... | collective-permute-start | bytes 294920 | tf_op jit(solution)/shard_map/ppermute | solution.py:170
  58.6 7.2 %collective-permute-start = (bf16[1,48,1024]{2,1,0:T(8,128)(2,1)S(1)}, bf16[1,48,1024]{2,1,0:T(8,128)(2,1)S(1)}, u32[]{:S(2)}, u32[]{:S(2)}) collective-permute-start(bf16[1,48,1024]{2,1,0:T(8,128)(2,1)S(1)} %bitcast.4), channel_id=1, source_target_pairs={{0,16},{1,17},{2,18},{3,19},{4,20},{5,21},{6,22},{7,23},{8,24},{9,... | collective-permute-start | bytes 294920 | tf_op jit(solution)/shard_map/ppermute | solution.py:162
  65.7 44.3 %all-to-all-start.1 = ((bf16[16,2,48,512]{3,2,1,0:T(8,128)(2,1)}), bf16[16,2,48,512]{3,2,1,0:T(8,128)(2,1)}, u32[]{:S(2)}, u32[]{:S(2)}) async-start(bf16[16,2,48,512]{3,2,1,0:T(8,128)(2,1)} %shard_map.47), calls=%async_computation.1 | async-start | bytes 3145728 | tf_op jit(solution)/shard_map/all_to_all | solution.py:194
  72.8 5.4 %collective-permute-start.2 = (bf16[2,48,1024]{2,1,0:T(8,128)(2,1)S(1)}, bf16[2,48,1024]{2,1,0:T(8,128)(2,1)S(1)}, u32[]{:S(2)}, u32[]{:S(2)}) collective-permute-start(bf16[2,48,1024]{2,1,0:T(8,128)(2,1)S(1)} %pad_maximum_fusion.2), channel_id=1, source_target_pairs={{0,1},{1,0},{2,3},{3,2},{4,5},{5,4},{6,7},{7,6},{8,9},{9,8},{10,11... | collective-permute-start | bytes 589832 | tf_op jit(solution)/shard_map/ppermute | solution.py:166
  78.2 12.5 %collective-permute-start.3 = (bf16[4,48,1024]{2,1,0:T(8,128)(2,1)S(1)}, bf16[4,48,1024]{2,1,0:T(8,128)(2,1)S(1)}, u32[]{:S(2)}, u32[]{:S(2)}) collective-permute-start(bf16[4,48,1024]{2,1,0:T(8,128)(2,1)S(1)} %pad_maximum_fusion.1.refs_0_), channel_id=1, source_target_pairs={{0,2},{1,15},{2,4},{3,1},{4,6},{5,3},{6,8},{7,5},{8,10},{9,7},{10,... | collective-permute-start | bytes 1179656 | tf_op jit(solution)/shard_map/ppermute | solution.py:170
  82.9 15.1 %collective-permute-start.4 = (bf16[4,48,1024]{2,1,0:T(8,128)(2,1)S(1)}, bf16[4,48,1024]{2,1,0:T(8,128)(2,1)S(1)}, u32[]{:S(2)}, u32[]{:S(2)}) collective-permute-start(bf16[4,48,1024]{2,1,0:T(8,128)(2,1)S(1)} %pad_maximum_fusion.1.refs_0_), channel_id=1, source_target_pairs={{0,4},{1,13},{2,6},{3,15},{4,8},{5,1},{6,10},{7,3},{8,12},{9,5},{1... | collective-permute-start | bytes 1179656 | tf_op jit(solution)/shard_map/ppermute | solution.py:170
  87.9 8.9 %collective-permute-start.6 = (bf16[1,48,1024]{2,1,0:T(8,128)(2,1)S(1)}, bf16[1,48,1024]{2,1,0:T(8,128)(2,1)S(1)}, u32[]{:S(2)}, u32[]{:S(2)}) collective-permute-start(bf16[1,48,1024]{2,1,0:T(8,128)(2,1)S(1)} %collective-permute-done.1.refs_4_), channel_id=1, source_target_pairs={{0,16},{1,17},{2,18},{3,19},{4,20},{5,21},{6,22},{7,23},{8,24},{9,... | collective-permute-start | bytes 294920 | tf_op jit(solution)/shard_map/ppermute | solution.py:162
  90.7 15.0 %collective-permute-start.5 = (bf16[4,48,1024]{2,1,0:T(8,128)(2,1)S(1)}, bf16[4,48,1024]{2,1,0:T(8,128)(2,1)S(1)}, u32[]{:S(2)}, u32[]{:S(2)}) collective-permute-start(bf16[4,48,1024]{2,1,0:T(8,128)(2,1)S(1)} %collective-permute-done.3.refs_1_), channel_id=1, source_target_pairs={{0,4},{1,13},{2,6},{3,15},{4,8},{5,1},{6,10},{7,3},{8,12},{9,5},{1... | collective-permute-start | bytes 1179656 | tf_op jit(solution)/shard_map/ppermute | solution.py:170
  98.1 10.5 %collective-permute-start.8 = (bf16[6,48,1024]{2,1,0:T(8,128)(2,1)S(1)}, bf16[6,48,1024]{2,1,0:T(8,128)(2,1)S(1)}, u32[]{:S(2)}, u32[]{:S(2)}) collective-permute-start(bf16[6,48,1024]{2,1,0:T(8,128)(2,1)S(1)} %pad_maximum_fusion), channel_id=1, source_target_pairs={{0,1},{1,0},{2,3},{3,2},{4,5},{5,4},{6,7},{7,6},{8,9},{9,8},{10,11... | collective-permute-start | bytes 1769480 | tf_op jit(solution)/shard_map/ppermute | solution.py:166
  102.8 5.8 %collective-permute-start.7 = (bf16[4,48,1024]{2,1,0:T(8,128)(2,1)S(1)}, bf16[4,48,1024]{2,1,0:T(8,128)(2,1)S(1)}, u32[]{:S(2)}, u32[]{:S(2)}) collective-permute-start(bf16[4,48,1024]{2,1,0:T(8,128)(2,1)S(1)} %collective-permute-done.3.refs_1_), channel_id=1, source_target_pairs={{0,1},{1,0},{2,3},{3,2},{4,5},{5,4},{6,7},{7,6},{8,9},{9,8},{10,11... | collective-permute-start | bytes 1179656 | tf_op jit(solution)/shard_map/ppermute | solution.py:166
  105.7 4.1 %collective-permute-start.9 = (bf16[4,48,1024]{2,1,0:T(8,128)(2,1)S(1)}, bf16[4,48,1024]{2,1,0:T(8,128)(2,1)S(1)}, u32[]{:S(2)}, u32[]{:S(2)}) collective-permute-start(bf16[4,48,1024]{2,1,0:T(8,128)(2,1)S(1)} %collective-permute-done.5.refs_3_), channel_id=1, source_target_pairs={{0,1},{1,0},{2,3},{3,2},{4,5},{5,4},{6,7},{7,6},{8,9},{9,8},{10,11... | collective-permute-start | bytes 1179656 | tf_op jit(solution)/shard_map/ppermute | solution.py:166

commit v7 on v6

--- a/solution.py
+++ b/solution.py
@@ -103,6 +103,7 @@
         in_specs=[vmem] * len(pieces),
         out_specs=vmem,
         compiler_params=pltpu.CompilerParams(vmem_limit_bytes=ASSEMBLE_LIMIT),
+        cost_estimate=pl.CostEstimate(flops=14 * 10**9, bytes_accessed=0, transcendentals=10**9),
     )(*pieces)
 
 
@@ -190,7 +191,7 @@
     far = along(piece, 4)
     piece_x = swap_x(piece)
     chosen = order(own, step_start)
-    chosen, piece_x, far = lax.optimization_barrier((chosen, piece_x, far))
+    piece_x, far = lax.optimization_barrier((piece_x, far))
     right = lax.all_to_all(chosen, "row", split_axis=0, concat_axis=0, tiled=True)
     pieces = gather_left(piece, piece_x, far)
     return gram(assemble(pieces, rows_dev), right)[None]

time: 117 us -> 115 us (0.983)
  starting transfers between devices: 61.1 us -> 55.4 us
  waiting for transfers between devices: 45.2 us -> 48.5 us
    ppermute x4, starting transfers between devices: 19 us -> 13.4 us  [along(): return lax.ppermute(block, 'col', RING[hop])]
    ppermute x4, starting transfers between devices: 13.7 us -> 11.1 us  [swap_core(): return lax.ppermute(block, 'col', SWAP_CORE)]
    ppermute x2, starting transfers between devices: 6.86 us -> 9.37 us  [swap_x(): return lax.ppermute(block, 'col', SWAP_X)]
    all_to_all x1, waiting for transfers between devices: 0.01 us -> 1.97 us  [local(): lax.all_to_all(chosen, 'row', split_axis=0, concat_axis=0, tiled=True)]
    ppermute x2, waiting for transfers between devices: 0.95 us -> 2.14 us  [swap_x(): return lax.ppermute(block, 'col', SWAP_X)]
where the time goes in v7:
time: 115 us; the launch traced here: 113 us
  starting transfers between devices  55.4 us (48%)
  waiting for transfers between devices  48.5 us (42%)
  Pallas kernels  8.34 us (7%)
    all_to_all x1, waiting for transfers between devices, local(): own = lax.all_to_all(blocks, 'col', split_axis=0, concat_axis=0, tiled=True)  39.2 us
    all_to_all x1, starting transfers between devices, local(): own = lax.all_to_all(blocks, 'col', split_axis=0, concat_axis=0, tiled=True)  14.6 us
    ppermute x4, starting transfers between devices, along(): return lax.ppermute(block, 'col', RING[hop])  13.4 us
    ppermute x4, starting transfers between devices, swap_core(): return lax.ppermute(block, 'col', SWAP_CORE)  11.1 us
    ppermute x2, starting transfers between devices, swap_x(): return lax.ppermute(block, 'col', SWAP_X)  9.37 us
    all_to_all x1, starting transfers between devices, local(): lax.all_to_all(chosen, 'row', split_axis=0, concat_axis=0, tiled=True)  7 us
    pallas_call x1, Pallas kernels, gram(): pl.pallas_call(gram_kernel, out_shape=jax.ShapeDtypeStruct((rows_dev, wid...  5.49 us
    ppermute x4, waiting for transfers between devices, along(): return lax.ppermute(block, 'col', RING[hop])  2.84 us
  transfers between devices with their start and end apart: 12, of which 7 were waited for; matrix products, arithmetic and copies ran while one was open for 0% of the time, Pallas kernels for 2%

profile of v7, /device:TPU:1, one launch (start us, length us, event | category | flops | bytes accessed | tf_op | source)
XLA Modules:
  0.0 113.2 jit_solution(16383271984600086254)
XLA Ops:
  0.0 0.0 copy-start
  0.0 14.6 %all-to-all-start = ((bf16[32,48,512]{2,1,0:T(8,128)(2,1)}), bf16[32,48,512]{2,1,0:T(8,128)(2,1)S(1)}, u32[]{:S(2)}, u32[]{:S(2)}) async-start(bf16[32,48,512]{2,1,0:T(8,128)(2,1)} %bitcast.7), calls=%async_computation | async-start | bytes 3145728 | tf_op jit(solution)/shard_map/all_to_all | solution.py:189
  15.2 39.2 %all-to-all-done.own_ref = bf16[32,48,512]{2,1,0:T(8,128)(2,1)S(1)} async-done(((bf16[32,48,512]{2,1,0:T(8,128)(2,1)}), bf16[32,48,512]{2,1,0:T(8,128)(2,1)S(1)}, u32[]{:S(2)}, u32[]{:S(2)}) %all-to-all-start) | async-done | bytes 1572896 | tf_op jit(solution)/shard_map/all_to_all | solution.py:189
  54.4 0.0 copy-done
  54.4 0.0 copy-done.1
  54.4 1.0 shard_map.46
  55.4 3.1 %collective-permute-start.1 = (bf16[1,48,1024]{2,1,0:T(8,128)(2,1)S(1)}, bf16[1,48,1024]{2,1,0:T(8,128)(2,1)S(1)}, u32[]{:S(2)}, u32[]{:S(2)}) collective-permute-start(bf16[1,48,1024]{2,1,0:T(8,128)(2,1)S(1)} %bitcast.3), channel_id=1, source_target_pairs={{0,8},{1,9},{2,10},{3,11},{4,12},{5,13},{6,14},{7,15},{8,0},{9,1},... | collective-permute-start | bytes 294920 | tf_op jit(solution)/shard_map/ppermute | solution.py:171
  58.6 4.1 %collective-permute-start = (bf16[1,48,1024]{2,1,0:T(8,128)(2,1)S(1)}, bf16[1,48,1024]{2,1,0:T(8,128)(2,1)S(1)}, u32[]{:S(2)}, u32[]{:S(2)}) collective-permute-start(bf16[1,48,1024]{2,1,0:T(8,128)(2,1)S(1)} %bitcast.4), channel_id=1, source_target_pairs={{0,16},{1,17},{2,18},{3,19},{4,20},{5,21},{6,22},{7,23},{8,24},{9,... | collective-permute-start | bytes 294920 | tf_op jit(solution)/shard_map/ppermute | solution.py:163
  62.7 1.6 %shard_map.48 = bf16[16,2,48,512]{3,2,1,0:T(8,128)(2,1)} custom-call(s32[1]{0:T(128)S(6)} %copy.5.start_ref, bf16[32,48,512]{2,1,0:T(8,128)(2,1)S(1)} %all-to-all-done.own_ref), custom_call_target="tpu_custom_call" | custom-call | bytes 3145728 | tf_op jit(solution)/shard_map/pallas_call | solution.py:66
  64.3 7.0 %all-to-all-start.1 = ((bf16[16,2,48,512]{3,2,1,0:T(8,128)(2,1)}), bf16[16,2,48,512]{3,2,1,0:T(8,128)(2,1)}, u32[]{:S(2)}, u32[]{:S(2)}) async-start(bf16[16,2,48,512]{3,2,1,0:T(8,128)(2,1)} %shard_map.48), calls=%async_computation.1 | async-start | bytes 3145728 | tf_op jit(solution)/shard_map/all_to_all | solution.py:195
  71.3 0.0 collective-permute-done.1.refs_4_
  71.3 0.0 collective-permute-done
  71.4 3.1 %collective-permute-start.2 = (bf16[2,48,1024]{2,1,0:T(8,128)(2,1)S(1)}, bf16[2,48,1024]{2,1,0:T(8,128)(2,1)S(1)}, u32[]{:S(2)}, u32[]{:S(2)}) collective-permute-start(bf16[2,48,1024]{2,1,0:T(8,128)(2,1)S(1)} %pad_maximum_fusion.2), channel_id=1, source_target_pairs={{0,1},{1,0},{2,3},{3,2},{4,5},{5,4},{6,7},{7,6},{8,9},{9,8},{10,11... | collective-permute-start | bytes 589832 | tf_op jit(solution)/shard_map/ppermute | solution.py:167
  74.5 1.0 collective-permute-done.2
  75.6 3.6 %collective-permute-start.3 = (bf16[4,48,1024]{2,1,0:T(8,128)(2,1)S(1)}, bf16[4,48,1024]{2,1,0:T(8,128)(2,1)S(1)}, u32[]{:S(2)}, u32[]{:S(2)}) collective-permute-start(bf16[4,48,1024]{2,1,0:T(8,128)(2,1)S(1)} %pad_maximum_fusion.1.refs_0_), channel_id=1, source_target_pairs={{0,2},{1,15},{2,4},{3,1},{4,6},{5,3},{6,8},{7,5},{8,10},{9,7},{10,... | collective-permute-start | bytes 1179656 | tf_op jit(solution)/shard_map/ppermute | solution.py:171
  79.2 4.7 %collective-permute-start.4 = (bf16[4,48,1024]{2,1,0:T(8,128)(2,1)S(1)}, bf16[4,48,1024]{2,1,0:T(8,128)(2,1)S(1)}, u32[]{:S(2)}, u32[]{:S(2)}) collective-permute-start(bf16[4,48,1024]{2,1,0:T(8,128)(2,1)S(1)} %pad_maximum_fusion.1.refs_0_), channel_id=1, source_target_pairs={{0,4},{1,13},{2,6},{3,15},{4,8},{5,1},{6,10},{7,3},{8,12},{9,5},{1... | collective-permute-start | bytes 1179656 | tf_op jit(solution)/shard_map/ppermute | solution.py:171
  84.0 5.3 %collective-permute-start.6 = (bf16[1,48,1024]{2,1,0:T(8,128)(2,1)S(1)}, bf16[1,48,1024]{2,1,0:T(8,128)(2,1)S(1)}, u32[]{:S(2)}, u32[]{:S(2)}) collective-permute-start(bf16[1,48,1024]{2,1,0:T(8,128)(2,1)S(1)} %collective-permute-done.1.refs_4_), channel_id=1, source_target_pairs={{0,16},{1,17},{2,18},{3,19},{4,20},{5,21},{6,22},{7,23},{8,24},{9,... | collective-permute-start | bytes 294920 | tf_op jit(solution)/shard_map/ppermute | solution.py:163
  89.2 0.0 collective-permute-done.3.refs_1_
  89.2 1.9 %collective-permute-start.5 = (bf16[4,48,1024]{2,1,0:T(8,128)(2,1)S(1)}, bf16[4,48,1024]{2,1,0:T(8,128)(2,1)S(1)}, u32[]{:S(2)}, u32[]{:S(2)}) collective-permute-start(bf16[4,48,1024]{2,1,0:T(8,128)(2,1)S(1)} %collective-permute-done.3.refs_1_), channel_id=1, source_target_pairs={{0,4},{1,13},{2,6},{3,15},{4,8},{5,1},{6,10},{7,3},{8,12},{9,5},{1... | collective-permute-start | bytes 1179656 | tf_op jit(solution)/shard_map/ppermute | solution.py:171
  91.2 2.1 %collective-permute-done.6.refs_5_ = bf16[1,48,1024]{2,1,0:T(8,128)(2,1)S(1)} collective-permute-done((bf16[1,48,1024]{2,1,0:T(8,128)(2,1)S(1)}, bf16[1,48,1024]{2,1,0:T(8,128)(2,1)S(1)}, u32[]{:S(2)}, u32[]{:S(2)}) %collective-permute-start.6) | collective-permute-done | bytes 98336 | tf_op jit(solution)/shard_map/ppermute | solution.py:163
  93.3 1.2 %collective-permute-done.4.refs_2_ = bf16[4,48,1024]{2,1,0:T(8,128)(2,1)S(1)} collective-permute-done((bf16[4,48,1024]{2,1,0:T(8,128)(2,1)S(1)}, bf16[4,48,1024]{2,1,0:T(8,128)(2,1)S(1)}, u32[]{:S(2)}, u32[]{:S(2)}) %collective-permute-start.4) | collective-permute-done | bytes 393248 | tf_op jit(solution)/shard_map/ppermute | solution.py:171
  94.5 0.1 pad_maximum_fusion
  94.6 3.7 %collective-permute-start.8 = (bf16[6,48,1024]{2,1,0:T(8,128)(2,1)S(1)}, bf16[6,48,1024]{2,1,0:T(8,128)(2,1)S(1)}, u32[]{:S(2)}, u32[]{:S(2)}) collective-permute-start(bf16[6,48,1024]{2,1,0:T(8,128)(2,1)S(1)} %pad_maximum_fusion), channel_id=1, source_target_pairs={{0,1},{1,0},{2,3},{3,2},{4,5},{5,4},{6,7},{7,6},{8,9},{9,8},{10,11... | collective-permute-start | bytes 1769480 | tf_op jit(solution)/shard_map/ppermute | solution.py:167
  98.3 1.9 %collective-permute-start.7 = (bf16[4,48,1024]{2,1,0:T(8,128)(2,1)S(1)}, bf16[4,48,1024]{2,1,0:T(8,128)(2,1)S(1)}, u32[]{:S(2)}, u32[]{:S(2)}) collective-permute-start(bf16[4,48,1024]{2,1,0:T(8,128)(2,1)S(1)} %collective-permute-done.3.refs_1_), channel_id=1, source_target_pairs={{0,1},{1,0},{2,3},{3,2},{4,5},{5,4},{6,7},{7,6},{8,9},{9,8},{10,11... | collective-permute-start | bytes 1179656 | tf_op jit(solution)/shard_map/ppermute | solution.py:167
  100.2 1.7 %collective-permute-done.5.refs_3_ = bf16[4,48,1024]{2,1,0:T(8,128)(2,1)S(1)} collective-permute-done((bf16[4,48,1024]{2,1,0:T(8,128)(2,1)S(1)}, bf16[4,48,1024]{2,1,0:T(8,128)(2,1)S(1)}, u32[]{:S(2)}, u32[]{:S(2)}) %collective-permute-start.5) | collective-permute-done | bytes 393248 | tf_op jit(solution)/shard_map/ppermute | solution.py:171
  101.9 2.3 %collective-permute-start.9 = (bf16[4,48,1024]{2,1,0:T(8,128)(2,1)S(1)}, bf16[4,48,1024]{2,1,0:T(8,128)(2,1)S(1)}, u32[]{:S(2)}, u32[]{:S(2)}) collective-permute-start(bf16[4,48,1024]{2,1,0:T(8,128)(2,1)S(1)} %collective-permute-done.5.refs_3_), channel_id=1, source_target_pairs={{0,1},{1,0},{2,3},{3,2},{4,5},{5,4},{6,7},{7,6},{8,9},{9,8},{10,11... | collective-permute-start | bytes 1179656 | tf_op jit(solution)/shard_map/ppermute | solution.py:167
  104.2 0.0 collective-permute-done.7.refs_6_
  104.2 0.0 collective-permute-done.8.refs_7_
  104.2 1.3 %collective-permute-done.9.refs_8_ = bf16[4,48,1024]{2,1,0:T(8,128)(2,1)S(1)} collective-permute-done((bf16[4,48,1024]{2,1,0:T(8,128)(2,1)S(1)}, bf16[4,48,1024]{2,1,0:T(8,128)(2,1)S(1)}, u32[]{:S(2)}, u32[]{:S(2)}) %collective-permute-start.9) | collective-permute-done | bytes 393248 | tf_op jit(solution)/shard_map/ppermute | solution.py:167
  105.5 0.2 shard_map.47.left_ref
  105.7 2.0 %all-to-all-done.1.right_ref = bf16[16,2,48,512]{3,2,1,0:T(8,128)(2,1)} async-done(((bf16[16,2,48,512]{3,2,1,0:T(8,128)(2,1)}), bf16[16,2,48,512]{3,2,1,0:T(8,128)(2,1)}, u32[]{:S(2)}, u32[]{:S(2)}) %all-to-all-start.1) | async-done | bytes 1572896 | tf_op jit(solution)/shard_map/all_to_all | solution.py:195
  107.7 5.5 %shard_map.49 = bf16[1536,768]{1,0:T(8,128)(2,1)} custom-call(bf16[1536,1024]{1,0:T(8,128)(2,1)S(1)} %shard_map.47.left_ref, bf16[16,2,48,512]{3,2,1,0:T(8,128)(2,1)} %all-to-all-done.1.right_ref), custom_call_target="tpu_custom_call" | custom-call | tf_op jit(solution)/shard_map/pallas_call | solution.py:131
  (3 shorter events, 0.1 us)
Async XLA Ops:
  0.0 54.4 %copy-start = (s32[3]{0:T(128)S(1)}, s32[3]{0:T(128)}, u32[]{:S(2)}) copy-start(s32[3]{0:T(128)} %offsets_ref.1) | copy-start | bytes 40
  0.0 54.4 %copy-start.1 = (f32[4]{0:T(128)S(1)}, f32[4]{0:T(128)}, u32[]{:S(2)}) copy-start(f32[4]{0:T(128)} %weights_ref.1) | copy-start | bytes 52
  0.0 54.4 %all-to-all-start = ((bf16[32,48,512]{2,1,0:T(8,128)(2,1)}), bf16[32,48,512]{2,1,0:T(8,128)(2,1)S(1)}, u32[]{:S(2)}, u32[]{:S(2)}) async-start(bf16[32,48,512]{2,1,0:T(8,128)(2,1)} %bitcast.7), calls=%async_computation | async-start | bytes 3145728 | tf_op jit(solution)/shard_map/all_to_all | solution.py:189
  55.4 15.9 %collective-permute-start.1 = (bf16[1,48,1024]{2,1,0:T(8,128)(2,1)S(1)}, bf16[1,48,1024]{2,1,0:T(8,128)(2,1)S(1)}, u32[]{:S(2)}, u32[]{:S(2)}) collective-permute-start(bf16[1,48,1024]{2,1,0:T(8,128)(2,1)S(1)} %bitcast.3), channel_id=1, source_target_pairs={{0,8},{1,9},{2,10},{3,11},{4,12},{5,13},{6,14},{7,15},{8,0},{9,1},... | collective-permute-start | bytes 294920 | tf_op jit(solution)/shard_map/ppermute | solution.py:171
  58.6 12.7 %collective-permute-start = (bf16[1,48,1024]{2,1,0:T(8,128)(2,1)S(1)}, bf16[1,48,1024]{2,1,0:T(8,128)(2,1)S(1)}, u32[]{:S(2)}, u32[]{:S(2)}) collective-permute-start(bf16[1,48,1024]{2,1,0:T(8,128)(2,1)S(1)} %bitcast.4), channel_id=1, source_target_pairs={{0,16},{1,17},{2,18},{3,19},{4,20},{5,21},{6,22},{7,23},{8,24},{9,... | collective-permute-start | bytes 294920 | tf_op jit(solution)/shard_map/ppermute | solution.py:163
  64.3 43.4 %all-to-all-start.1 = ((bf16[16,2,48,512]{3,2,1,0:T(8,128)(2,1)}), bf16[16,2,48,512]{3,2,1,0:T(8,128)(2,1)}, u32[]{:S(2)}, u32[]{:S(2)}) async-start(bf16[16,2,48,512]{3,2,1,0:T(8,128)(2,1)} %shard_map.48), calls=%async_computation.1 | async-start | bytes 3145728 | tf_op jit(solution)/shard_map/all_to_all | solution.py:195
  71.4 4.2 %collective-permute-start.2 = (bf16[2,48,1024]{2,1,0:T(8,128)(2,1)S(1)}, bf16[2,48,1024]{2,1,0:T(8,128)(2,1)S(1)}, u32[]{:S(2)}, u32[]{:S(2)}) collective-permute-start(bf16[2,48,1024]{2,1,0:T(8,128)(2,1)S(1)} %pad_maximum_fusion.2), channel_id=1, source_target_pairs={{0,1},{1,0},{2,3},{3,2},{4,5},{5,4},{6,7},{7,6},{8,9},{9,8},{10,11... | collective-permute-start | bytes 589832 | tf_op jit(solution)/shard_map/ppermute | solution.py:167
  75.6 13.6 %collective-permute-start.3 = (bf16[4,48,1024]{2,1,0:T(8,128)(2,1)S(1)}, bf16[4,48,1024]{2,1,0:T(8,128)(2,1)S(1)}, u32[]{:S(2)}, u32[]{:S(2)}) collective-permute-start(bf16[4,48,1024]{2,1,0:T(8,128)(2,1)S(1)} %pad_maximum_fusion.1.refs_0_), channel_id=1, source_target_pairs={{0,2},{1,15},{2,4},{3,1},{4,6},{5,3},{6,8},{7,5},{8,10},{9,7},{10,... | collective-permute-start | bytes 1179656 | tf_op jit(solution)/shard_map/ppermute | solution.py:171
  79.2 15.2 %collective-permute-start.4 = (bf16[4,48,1024]{2,1,0:T(8,128)(2,1)S(1)}, bf16[4,48,1024]{2,1,0:T(8,128)(2,1)S(1)}, u32[]{:S(2)}, u32[]{:S(2)}) collective-permute-start(bf16[4,48,1024]{2,1,0:T(8,128)(2,1)S(1)} %pad_maximum_fusion.1.refs_0_), channel_id=1, source_target_pairs={{0,4},{1,13},{2,6},{3,15},{4,8},{5,1},{6,10},{7,3},{8,12},{9,5},{1... | collective-permute-start | bytes 1179656 | tf_op jit(solution)/shard_map/ppermute | solution.py:171
  84.0 9.3 %collective-permute-start.6 = (bf16[1,48,1024]{2,1,0:T(8,128)(2,1)S(1)}, bf16[1,48,1024]{2,1,0:T(8,128)(2,1)S(1)}, u32[]{:S(2)}, u32[]{:S(2)}) collective-permute-start(bf16[1,48,1024]{2,1,0:T(8,128)(2,1)S(1)} %collective-permute-done.1.refs_4_), channel_id=1, source_target_pairs={{0,16},{1,17},{2,18},{3,19},{4,20},{5,21},{6,22},{7,23},{8,24},{9,... | collective-permute-start | bytes 294920 | tf_op jit(solution)/shard_map/ppermute | solution.py:163
  89.2 12.6 %collective-permute-start.5 = (bf16[4,48,1024]{2,1,0:T(8,128)(2,1)S(1)}, bf16[4,48,1024]{2,1,0:T(8,128)(2,1)S(1)}, u32[]{:S(2)}, u32[]{:S(2)}) collective-permute-start(bf16[4,48,1024]{2,1,0:T(8,128)(2,1)S(1)} %collective-permute-done.3.refs_1_), channel_id=1, source_target_pairs={{0,4},{1,13},{2,6},{3,15},{4,8},{5,1},{6,10},{7,3},{8,12},{9,5},{1... | collective-permute-start | bytes 1179656 | tf_op jit(solution)/shard_map/ppermute | solution.py:171
  94.6 9.6 %collective-permute-start.8 = (bf16[6,48,1024]{2,1,0:T(8,128)(2,1)S(1)}, bf16[6,48,1024]{2,1,0:T(8,128)(2,1)S(1)}, u32[]{:S(2)}, u32[]{:S(2)}) collective-permute-start(bf16[6,48,1024]{2,1,0:T(8,128)(2,1)S(1)} %pad_maximum_fusion), channel_id=1, source_target_pairs={{0,1},{1,0},{2,3},{3,2},{4,5},{5,4},{6,7},{7,6},{8,9},{9,8},{10,11... | collective-permute-start | bytes 1769480 | tf_op jit(solution)/shard_map/ppermute | solution.py:167
  98.3 5.9 %collective-permute-start.7 = (bf16[4,48,1024]{2,1,0:T(8,128)(2,1)S(1)}, bf16[4,48,1024]{2,1,0:T(8,128)(2,1)S(1)}, u32[]{:S(2)}, u32[]{:S(2)}) collective-permute-start(bf16[4,48,1024]{2,1,0:T(8,128)(2,1)S(1)} %collective-permute-done.3.refs_1_), channel_id=1, source_target_pairs={{0,1},{1,0},{2,3},{3,2},{4,5},{5,4},{6,7},{7,6},{8,9},{9,8},{10,11... | collective-permute-start | bytes 1179656 | tf_op jit(solution)/shard_map/ppermute | solution.py:167
  101.9 3.6 %collective-permute-start.9 = (bf16[4,48,1024]{2,1,0:T(8,128)(2,1)S(1)}, bf16[4,48,1024]{2,1,0:T(8,128)(2,1)S(1)}, u32[]{:S(2)}, u32[]{:S(2)}) collective-permute-start(bf16[4,48,1024]{2,1,0:T(8,128)(2,1)S(1)} %collective-permute-done.5.refs_3_), channel_id=1, source_target_pairs={{0,1},{1,0},{2,3},{3,2},{4,5},{5,4},{6,7},{7,6},{8,9},{9,8},{10,11... | collective-permute-start | bytes 1179656 | tf_op jit(solution)/shard_map/ppermute | solution.py:167

commit v8 on v7

--- a/solution.py
+++ b/solution.py
@@ -174,6 +174,7 @@
 def gather_left(piece, piece_x, far):
     two = jnp.concatenate([piece, piece_x])
     base = jnp.concatenate([two, swap_core(two)])
+    base, far = lax.optimization_barrier((base, far))
     first, second = along(base, 1), along(base, 2)
     third = along(first, 2)
     far_x = swap_x(far)
@@ -191,7 +192,6 @@
     far = along(piece, 4)
     piece_x = swap_x(piece)
     chosen = order(own, step_start)
-    piece_x, far = lax.optimization_barrier((piece_x, far))
     right = lax.all_to_all(chosen, "row", split_axis=0, concat_axis=0, tiled=True)
     pieces = gather_left(piece, piece_x, far)
     return gram(assemble(pieces, rows_dev), right)[None]

time: 115 us -> 121 us (1.052)
  waiting for transfers between devices: 48.5 us -> 55.7 us
    ppermute x4, waiting for transfers between devices: 2.84 us -> 12.2 us  [along(): return lax.ppermute(block, 'col', RING[hop])]
    ppermute x4, starting transfers between devices: 13.4 us -> 15.8 us  [along(): return lax.ppermute(block, 'col', RING[hop])]
    ppermute x2, starting transfers between devices: 9.37 us -> 7.27 us  [swap_x(): return lax.ppermute(block, 'col', SWAP_X)]
    all_to_all x1, waiting for transfers between devices: 1.97 us -> 0.01 us  [local(): lax.all_to_all(chosen, 'row', split_axis=0, concat_axis=0, tiled=True)]
  transfers between devices with their start and end apart: 12 -> 12, of which waited for: 7 -> 6; matrix products, arithmetic and copies ran while one was open for 0% -> 0% of each run, Pallas kernels for 2% -> 2%
where the time goes in v8:
time: 121 us; the launch traced here: 120 us
  waiting for transfers between devices  55.7 us (46%)
  starting transfers between devices  55.3 us (46%)
  Pallas kernels  8.37 us (7%)
    all_to_all x1, waiting for transfers between devices, local(): own = lax.all_to_all(blocks, 'col', split_axis=0, concat_axis=0, tiled=True)  39.2 us
    ppermute x4, starting transfers between devices, along(): return lax.ppermute(block, 'col', RING[hop])  15.8 us
    all_to_all x1, starting transfers between devices, local(): own = lax.all_to_all(blocks, 'col', split_axis=0, concat_axis=0, tiled=True)  14.6 us
    ppermute x4, waiting for transfers between devices, along(): return lax.ppermute(block, 'col', RING[hop])  12.2 us
    ppermute x4, starting transfers between devices, swap_core(): return lax.ppermute(block, 'col', SWAP_CORE)  10.7 us
    ppermute x2, starting transfers between devices, swap_x(): return lax.ppermute(block, 'col', SWAP_X)  7.27 us
    all_to_all x1, starting transfers between devices, local(): lax.all_to_all(chosen, 'row', split_axis=0, concat_axis=0, tiled=True)  7 us
    pallas_call x1, Pallas kernels, gram(): pl.pallas_call(gram_kernel, out_shape=jax.ShapeDtypeStruct((rows_dev, wid...  5.52 us
  transfers between devices with their start and end apart: 12, of which 6 were waited for; matrix products, arithmetic and copies ran while one was open for 0% of the time, Pallas kernels for 2%

profile of v8, /device:TPU:1, one launch (start us, length us, event | category | flops | bytes accessed | tf_op | source)
XLA Modules:
  0.0 120.3 jit_solution(4221287034565280194)
XLA Ops:
  0.0 0.0 copy-start
  0.0 14.6 %all-to-all-start = ((bf16[32,48,512]{2,1,0:T(8,128)(2,1)}), bf16[32,48,512]{2,1,0:T(8,128)(2,1)S(1)}, u32[]{:S(2)}, u32[]{:S(2)}) async-start(bf16[32,48,512]{2,1,0:T(8,128)(2,1)} %bitcast.7), calls=%async_computation | async-start | bytes 3145728 | tf_op jit(solution)/shard_map/all_to_all | solution.py:190
  15.2 39.2 %all-to-all-done.own_ref = bf16[32,48,512]{2,1,0:T(8,128)(2,1)S(1)} async-done(((bf16[32,48,512]{2,1,0:T(8,128)(2,1)}), bf16[32,48,512]{2,1,0:T(8,128)(2,1)S(1)}, u32[]{:S(2)}, u32[]{:S(2)}) %all-to-all-start) | async-done | bytes 1572896 | tf_op jit(solution)/shard_map/all_to_all | solution.py:190
  54.4 0.0 copy-done
  54.4 0.0 copy-done.1
  54.4 1.0 shard_map.46
  55.4 2.8 %collective-permute-start = (bf16[1,48,1024]{2,1,0:T(8,128)(2,1)S(1)}, bf16[1,48,1024]{2,1,0:T(8,128)(2,1)S(1)}, u32[]{:S(2)}, u32[]{:S(2)}) collective-permute-start(bf16[1,48,1024]{2,1,0:T(8,128)(2,1)S(1)} %bitcast.3), channel_id=1, source_target_pairs={{0,16},{1,17},{2,18},{3,19},{4,20},{5,21},{6,22},{7,23},{8,24},{9,... | collective-permute-start | bytes 294920 | tf_op jit(solution)/shard_map/ppermute | solution.py:163
  58.3 1.6 %shard_map.48 = bf16[16,2,48,512]{3,2,1,0:T(8,128)(2,1)} custom-call(s32[1]{0:T(128)S(6)} %copy.5.start_ref, bf16[32,48,512]{2,1,0:T(8,128)(2,1)S(1)} %all-to-all-done.own_ref), custom_call_target="tpu_custom_call" | custom-call | bytes 3145728 | tf_op jit(solution)/shard_map/pallas_call | solution.py:66
  59.9 7.0 %all-to-all-start.1 = ((bf16[16,2,48,512]{3,2,1,0:T(8,128)(2,1)}), bf16[16,2,48,512]{3,2,1,0:T(8,128)(2,1)}, u32[]{:S(2)}, u32[]{:S(2)}) async-start(bf16[16,2,48,512]{3,2,1,0:T(8,128)(2,1)} %shard_map.48), calls=%async_computation.1 | async-start | bytes 3145728 | tf_op jit(solution)/shard_map/all_to_all | solution.py:195
  66.9 0.0 collective-permute-done
  66.9 2.9 %collective-permute-start.1 = (bf16[2,48,1024]{2,1,0:T(8,128)(2,1)S(1)}, bf16[2,48,1024]{2,1,0:T(8,128)(2,1)S(1)}, u32[]{:S(2)}, u32[]{:S(2)}) collective-permute-start(bf16[2,48,1024]{2,1,0:T(8,128)(2,1)S(1)} %pad_maximum_fusion.2), channel_id=1, source_target_pairs={{0,1},{1,0},{2,3},{3,2},{4,5},{5,4},{6,7},{7,6},{8,9},{9,8},{10,11... | collective-permute-start | bytes 589832 | tf_op jit(solution)/shard_map/ppermute | solution.py:167
  69.8 4.4 %collective-permute-start.2 = (bf16[1,48,1024]{2,1,0:T(8,128)(2,1)S(1)}, bf16[1,48,1024]{2,1,0:T(8,128)(2,1)S(1)}, u32[]{:S(2)}, u32[]{:S(2)}) collective-permute-start(bf16[1,48,1024]{2,1,0:T(8,128)(2,1)S(1)} %bitcast.5), channel_id=1, source_target_pairs={{0,8},{1,9},{2,10},{3,11},{4,12},{5,13},{6,14},{7,15},{8,0},{9,1},... | collective-permute-start | bytes 294920 | tf_op jit(solution)/shard_map/ppermute | solution.py:171
  74.2 0.0 collective-permute-done.1
  74.3 5.8 %collective-permute-done.2.refs_4_ = bf16[1,48,1024]{2,1,0:T(8,128)(2,1)S(1)} collective-permute-done((bf16[1,48,1024]{2,1,0:T(8,128)(2,1)S(1)}, bf16[1,48,1024]{2,1,0:T(8,128)(2,1)S(1)}, u32[]{:S(2)}, u32[]{:S(2)}) %collective-permute-start.2) | collective-permute-done | bytes 98336 | tf_op jit(solution)/shard_map/ppermute | solution.py:171
  80.1 2.3 %collective-permute-start.3 = (bf16[4,48,1024]{2,1,0:T(8,128)(2,1)S(1)}, bf16[4,48,1024]{2,1,0:T(8,128)(2,1)S(1)}, u32[]{:S(2)}, u32[]{:S(2)}) collective-permute-start(bf16[4,48,1024]{2,1,0:T(8,128)(2,1)S(1)} %pad_maximum_fusion.1.refs_0_), channel_id=1, source_target_pairs={{0,2},{1,15},{2,4},{3,1},{4,6},{5,3},{6,8},{7,5},{8,10},{9,7},{10,... | collective-permute-start | bytes 1179656 | tf_op jit(solution)/shard_map/ppermute | solution.py:171
  82.4 6.3 %collective-permute-start.4 = (bf16[4,48,1024]{2,1,0:T(8,128)(2,1)S(1)}, bf16[4,48,1024]{2,1,0:T(8,128)(2,1)S(1)}, u32[]{:S(2)}, u32[]{:S(2)}) collective-permute-start(bf16[4,48,1024]{2,1,0:T(8,128)(2,1)S(1)} %pad_maximum_fusion.1.refs_0_), channel_id=1, source_target_pairs={{0,4},{1,13},{2,6},{3,15},{4,8},{5,1},{6,10},{7,3},{8,12},{9,5},{1... | collective-permute-start | bytes 1179656 | tf_op jit(solution)/shard_map/ppermute | solution.py:171
  88.8 4.4 %collective-permute-start.6 = (bf16[1,48,1024]{2,1,0:T(8,128)(2,1)S(1)}, bf16[1,48,1024]{2,1,0:T(8,128)(2,1)S(1)}, u32[]{:S(2)}, u32[]{:S(2)}) collective-permute-start(bf16[1,48,1024]{2,1,0:T(8,128)(2,1)S(1)} %collective-permute-done.2.refs_4_), channel_id=1, source_target_pairs={{0,16},{1,17},{2,18},{3,19},{4,20},{5,21},{6,22},{7,23},{8,24},{9,... | collective-permute-start | bytes 294920 | tf_op jit(solution)/shard_map/ppermute | solution.py:163
  93.2 0.0 collective-permute-done.3.refs_1_
  93.2 2.8 %collective-permute-start.5 = (bf16[4,48,1024]{2,1,0:T(8,128)(2,1)S(1)}, bf16[4,48,1024]{2,1,0:T(8,128)(2,1)S(1)}, u32[]{:S(2)}, u32[]{:S(2)}) collective-permute-start(bf16[4,48,1024]{2,1,0:T(8,128)(2,1)S(1)} %collective-permute-done.3.refs_1_), channel_id=1, source_target_pairs={{0,4},{1,13},{2,6},{3,15},{4,8},{5,1},{6,10},{7,3},{8,12},{9,5},{1... | collective-permute-start | bytes 1179656 | tf_op jit(solution)/shard_map/ppermute | solution.py:171
  96.0 3.0 %collective-permute-done.6.refs_5_ = bf16[1,48,1024]{2,1,0:T(8,128)(2,1)S(1)} collective-permute-done((bf16[1,48,1024]{2,1,0:T(8,128)(2,1)S(1)}, bf16[1,48,1024]{2,1,0:T(8,128)(2,1)S(1)}, u32[]{:S(2)}, u32[]{:S(2)}) %collective-permute-start.6) | collective-permute-done | bytes 98336 | tf_op jit(solution)/shard_map/ppermute | solution.py:163
  99.0 2.8 %collective-permute-done.4.refs_2_ = bf16[4,48,1024]{2,1,0:T(8,128)(2,1)S(1)} collective-permute-done((bf16[4,48,1024]{2,1,0:T(8,128)(2,1)S(1)}, bf16[4,48,1024]{2,1,0:T(8,128)(2,1)S(1)}, u32[]{:S(2)}, u32[]{:S(2)}) %collective-permute-start.4) | collective-permute-done | bytes 393248 | tf_op jit(solution)/shard_map/ppermute | solution.py:171
  101.8 0.1 pad_maximum_fusion
  101.9 1.9 %collective-permute-start.8 = (bf16[6,48,1024]{2,1,0:T(8,128)(2,1)S(1)}, bf16[6,48,1024]{2,1,0:T(8,128)(2,1)S(1)}, u32[]{:S(2)}, u32[]{:S(2)}) collective-permute-start(bf16[6,48,1024]{2,1,0:T(8,128)(2,1)S(1)} %pad_maximum_fusion), channel_id=1, source_target_pairs={{0,1},{1,0},{2,3},{3,2},{4,5},{5,4},{6,7},{7,6},{8,9},{9,8},{10,11... | collective-permute-start | bytes 1769480 | tf_op jit(solution)/shard_map/ppermute | solution.py:167
  103.8 2.4 %collective-permute-start.7 = (bf16[4,48,1024]{2,1,0:T(8,128)(2,1)S(1)}, bf16[4,48,1024]{2,1,0:T(8,128)(2,1)S(1)}, u32[]{:S(2)}, u32[]{:S(2)}) collective-permute-start(bf16[4,48,1024]{2,1,0:T(8,128)(2,1)S(1)} %collective-permute-done.3.refs_1_), channel_id=1, source_target_pairs={{0,1},{1,0},{2,3},{3,2},{4,5},{5,4},{6,7},{7,6},{8,9},{9,8},{10,11... | collective-permute-start | bytes 1179656 | tf_op jit(solution)/shard_map/ppermute | solution.py:167
  106.2 3.5 %collective-permute-done.5.refs_3_ = bf16[4,48,1024]{2,1,0:T(8,128)(2,1)S(1)} collective-permute-done((bf16[4,48,1024]{2,1,0:T(8,128)(2,1)S(1)}, bf16[4,48,1024]{2,1,0:T(8,128)(2,1)S(1)}, u32[]{:S(2)}, u32[]{:S(2)}) %collective-permute-start.5) | collective-permute-done | bytes 393248 | tf_op jit(solution)/shard_map/ppermute | solution.py:171
  109.7 3.5 %collective-permute-start.9 = (bf16[4,48,1024]{2,1,0:T(8,128)(2,1)S(1)}, bf16[4,48,1024]{2,1,0:T(8,128)(2,1)S(1)}, u32[]{:S(2)}, u32[]{:S(2)}) collective-permute-start(bf16[4,48,1024]{2,1,0:T(8,128)(2,1)S(1)} %collective-permute-done.5.refs_3_), channel_id=1, source_target_pairs={{0,1},{1,0},{2,3},{3,2},{4,5},{5,4},{6,7},{7,6},{8,9},{9,8},{10,11... | collective-permute-start | bytes 1179656 | tf_op jit(solution)/shard_map/ppermute | solution.py:167
  113.2 0.0 collective-permute-done.7.refs_6_
  113.2 0.0 collective-permute-done.8.refs_7_
  113.2 1.3 %collective-permute-done.9.refs_8_ = bf16[4,48,1024]{2,1,0:T(8,128)(2,1)S(1)} collective-permute-done((bf16[4,48,1024]{2,1,0:T(8,128)(2,1)S(1)}, bf16[4,48,1024]{2,1,0:T(8,128)(2,1)S(1)}, u32[]{:S(2)}, u32[]{:S(2)}) %collective-permute-start.9) | collective-permute-done | bytes 393248 | tf_op jit(solution)/shard_map/ppermute | solution.py:167
  114.5 0.2 shard_map.47.left_ref
  114.8 0.0 all-to-all-done.1.right_ref
  114.8 5.5 %shard_map.49 = bf16[1536,768]{1,0:T(8,128)(2,1)} custom-call(bf16[1536,1024]{1,0:T(8,128)(2,1)S(1)} %shard_map.47.left_ref, bf16[16,2,48,512]{3,2,1,0:T(8,128)(2,1)} %all-to-all-done.1.right_ref), custom_call_target="tpu_custom_call" | custom-call | tf_op jit(solution)/shard_map/pallas_call | solution.py:131
  (3 shorter events, 0.1 us)
Async XLA Ops:
  0.0 54.4 %copy-start = (s32[3]{0:T(128)S(1)}, s32[3]{0:T(128)}, u32[]{:S(2)}) copy-start(s32[3]{0:T(128)} %offsets_ref.1) | copy-start | bytes 40
  0.0 54.4 %copy-start.1 = (f32[4]{0:T(128)S(1)}, f32[4]{0:T(128)}, u32[]{:S(2)}) copy-start(f32[4]{0:T(128)} %weights_ref.1) | copy-start | bytes 52
  0.0 54.4 %all-to-all-start = ((bf16[32,48,512]{2,1,0:T(8,128)(2,1)}), bf16[32,48,512]{2,1,0:T(8,128)(2,1)S(1)}, u32[]{:S(2)}, u32[]{:S(2)}) async-start(bf16[32,48,512]{2,1,0:T(8,128)(2,1)} %bitcast.7), calls=%async_computation | async-start | bytes 3145728 | tf_op jit(solution)/shard_map/all_to_all | solution.py:190
  55.4 11.5 %collective-permute-start = (bf16[1,48,1024]{2,1,0:T(8,128)(2,1)S(1)}, bf16[1,48,1024]{2,1,0:T(8,128)(2,1)S(1)}, u32[]{:S(2)}, u32[]{:S(2)}) collective-permute-start(bf16[1,48,1024]{2,1,0:T(8,128)(2,1)S(1)} %bitcast.3), channel_id=1, source_target_pairs={{0,16},{1,17},{2,18},{3,19},{4,20},{5,21},{6,22},{7,23},{8,24},{9,... | collective-permute-start | bytes 294920 | tf_op jit(solution)/shard_map/ppermute | solution.py:163
  59.9 54.9 %all-to-all-start.1 = ((bf16[16,2,48,512]{3,2,1,0:T(8,128)(2,1)}), bf16[16,2,48,512]{3,2,1,0:T(8,128)(2,1)}, u32[]{:S(2)}, u32[]{:S(2)}) async-start(bf16[16,2,48,512]{3,2,1,0:T(8,128)(2,1)} %shard_map.48), calls=%async_computation.1 | async-start | bytes 3145728 | tf_op jit(solution)/shard_map/all_to_all | solution.py:195
  66.9 7.3 %collective-permute-start.1 = (bf16[2,48,1024]{2,1,0:T(8,128)(2,1)S(1)}, bf16[2,48,1024]{2,1,0:T(8,128)(2,1)S(1)}, u32[]{:S(2)}, u32[]{:S(2)}) collective-permute-start(bf16[2,48,1024]{2,1,0:T(8,128)(2,1)S(1)} %pad_maximum_fusion.2), channel_id=1, source_target_pairs={{0,1},{1,0},{2,3},{3,2},{4,5},{5,4},{6,7},{7,6},{8,9},{9,8},{10,11... | collective-permute-start | bytes 589832 | tf_op jit(solution)/shard_map/ppermute | solution.py:167
  69.8 10.3 %collective-permute-start.2 = (bf16[1,48,1024]{2,1,0:T(8,128)(2,1)S(1)}, bf16[1,48,1024]{2,1,0:T(8,128)(2,1)S(1)}, u32[]{:S(2)}, u32[]{:S(2)}) collective-permute-start(bf16[1,48,1024]{2,1,0:T(8,128)(2,1)S(1)} %bitcast.5), channel_id=1, source_target_pairs={{0,8},{1,9},{2,10},{3,11},{4,12},{5,13},{6,14},{7,15},{8,0},{9,1},... | collective-permute-start | bytes 294920 | tf_op jit(solution)/shard_map/ppermute | solution.py:171
  80.1 13.1 %collective-permute-start.3 = (bf16[4,48,1024]{2,1,0:T(8,128)(2,1)S(1)}, bf16[4,48,1024]{2,1,0:T(8,128)(2,1)S(1)}, u32[]{:S(2)}, u32[]{:S(2)}) collective-permute-start(bf16[4,48,1024]{2,1,0:T(8,128)(2,1)S(1)} %pad_maximum_fusion.1.refs_0_), channel_id=1, source_target_pairs={{0,2},{1,15},{2,4},{3,1},{4,6},{5,3},{6,8},{7,5},{8,10},{9,7},{10,... | collective-permute-start | bytes 1179656 | tf_op jit(solution)/shard_map/ppermute | solution.py:171
  82.4 19.4 %collective-permute-start.4 = (bf16[4,48,1024]{2,1,0:T(8,128)(2,1)S(1)}, bf16[4,48,1024]{2,1,0:T(8,128)(2,1)S(1)}, u32[]{:S(2)}, u32[]{:S(2)}) collective-permute-start(bf16[4,48,1024]{2,1,0:T(8,128)(2,1)S(1)} %pad_maximum_fusion.1.refs_0_), channel_id=1, source_target_pairs={{0,4},{1,13},{2,6},{3,15},{4,8},{5,1},{6,10},{7,3},{8,12},{9,5},{1... | collective-permute-start | bytes 1179656 | tf_op jit(solution)/shard_map/ppermute | solution.py:171
  88.8 10.2 %collective-permute-start.6 = (bf16[1,48,1024]{2,1,0:T(8,128)(2,1)S(1)}, bf16[1,48,1024]{2,1,0:T(8,128)(2,1)S(1)}, u32[]{:S(2)}, u32[]{:S(2)}) collective-permute-start(bf16[1,48,1024]{2,1,0:T(8,128)(2,1)S(1)} %collective-permute-done.2.refs_4_), channel_id=1, source_target_pairs={{0,16},{1,17},{2,18},{3,19},{4,20},{5,21},{6,22},{7,23},{8,24},{9,... | collective-permute-start | bytes 294920 | tf_op jit(solution)/shard_map/ppermute | solution.py:163
  93.2 16.5 %collective-permute-start.5 = (bf16[4,48,1024]{2,1,0:T(8,128)(2,1)S(1)}, bf16[4,48,1024]{2,1,0:T(8,128)(2,1)S(1)}, u32[]{:S(2)}, u32[]{:S(2)}) collective-permute-start(bf16[4,48,1024]{2,1,0:T(8,128)(2,1)S(1)} %collective-permute-done.3.refs_1_), channel_id=1, source_target_pairs={{0,4},{1,13},{2,6},{3,15},{4,8},{5,1},{6,10},{7,3},{8,12},{9,5},{1... | collective-permute-start | bytes 1179656 | tf_op jit(solution)/shard_map/ppermute | solution.py:171
  101.9 11.3 %collective-permute-start.8 = (bf16[6,48,1024]{2,1,0:T(8,128)(2,1)S(1)}, bf16[6,48,1024]{2,1,0:T(8,128)(2,1)S(1)}, u32[]{:S(2)}, u32[]{:S(2)}) collective-permute-start(bf16[6,48,1024]{2,1,0:T(8,128)(2,1)S(1)} %pad_maximum_fusion), channel_id=1, source_target_pairs={{0,1},{1,0},{2,3},{3,2},{4,5},{5,4},{6,7},{7,6},{8,9},{9,8},{10,11... | collective-permute-start | bytes 1769480 | tf_op jit(solution)/shard_map/ppermute | solution.py:167
  103.8 9.4 %collective-permute-start.7 = (bf16[4,48,1024]{2,1,0:T(8,128)(2,1)S(1)}, bf16[4,48,1024]{2,1,0:T(8,128)(2,1)S(1)}, u32[]{:S(2)}, u32[]{:S(2)}) collective-permute-start(bf16[4,48,1024]{2,1,0:T(8,128)(2,1)S(1)} %collective-permute-done.3.refs_1_), channel_id=1, source_target_pairs={{0,1},{1,0},{2,3},{3,2},{4,5},{5,4},{6,7},{7,6},{8,9},{9,8},{10,11... | collective-permute-start | bytes 1179656 | tf_op jit(solution)/shard_map/ppermute | solution.py:167
  109.7 4.8 %collective-permute-start.9 = (bf16[4,48,1024]{2,1,0:T(8,128)(2,1)S(1)}, bf16[4,48,1024]{2,1,0:T(8,128)(2,1)S(1)}, u32[]{:S(2)}, u32[]{:S(2)}) collective-permute-start(bf16[4,48,1024]{2,1,0:T(8,128)(2,1)S(1)} %collective-permute-done.5.refs_3_), channel_id=1, source_target_pairs={{0,1},{1,0},{2,3},{3,2},{4,5},{5,4},{6,7},{7,6},{8,9},{9,8},{10,11... | collective-permute-start | bytes 1179656 | tf_op jit(solution)/shard_map/ppermute | solution.py:167

commit v9 on v6

--- a/solution.py
+++ b/solution.py
@@ -103,6 +103,7 @@
         in_specs=[vmem] * len(pieces),
         out_specs=vmem,
         compiler_params=pltpu.CompilerParams(vmem_limit_bytes=ASSEMBLE_LIMIT),
+        cost_estimate=pl.CostEstimate(flops=11 * 10**9, bytes_accessed=0, transcendentals=10**9),
     )(*pieces)
 
 
@@ -145,7 +146,7 @@
 SWAP_X = [(place(x, z, c), place(x + 1, z, c)) for x, z, c in PLACES]
 SWAP_CORE = [(place(x, z, c), place(x, z, c + 1)) for x, z, c in PLACES]
 RING = [[(place(x, z, c), place(x, z + hop * (1 - 2 * c), c)) for x, z, c in PLACES] for hop in range(5)]
-FAR, FAR_X = [(4, 0, 0)], [(4, 1, 0)]
+FAR = [(4, 0, 0), (4, 1, 0)]
 
 
 def four(hop):
@@ -153,8 +154,8 @@
 
 
 LAYOUT = [
-    (0, four(0)), (0, four(1)), (0, four(2)), (0, four(3)), (0, FAR), (0, FAR_X),
-    (1, four(1)), (1, four(2) + FAR + FAR_X), (1, four(3)),
+    (0, four(0)), (0, four(1)), (0, four(2)), (0, four(3)), (0, FAR),
+    (1, four(1)), (1, four(2)), (1, four(3) + FAR),
 ]
 
 
@@ -170,14 +171,15 @@
     return lax.ppermute(block, "col", RING[hop])
 
 
-def gather_left(piece, piece_x, far):
+def gather_left(piece, piece_x):
     two = jnp.concatenate([piece, piece_x])
     base = jnp.concatenate([two, swap_core(two)])
     first, second = along(base, 1), along(base, 2)
+    far = along(first[:2], 3)
     third = along(first, 2)
-    far_x = swap_x(far)
-    later = jnp.concatenate([second, far, far_x])
-    return [base, first, second, third, far, far_x, swap_core(first), swap_core(later), swap_core(third)]
+    third, far, first_c = lax.optimization_barrier((third, far, swap_core(first)))
+    late = jnp.concatenate([third, far])
+    return [base, first, second, third, far, first_c, swap_core(second), swap_core(late)]
 
 
 def local(sensitivity, stencil_weights, cell_offsets, step_start):
@@ -187,12 +189,10 @@
     blocks = sensitivity.reshape(col_count, piece_rows, cells_dev)
     own = lax.all_to_all(blocks, "col", split_axis=0, concat_axis=0, tiled=True)
     piece = smooth(own, stencil_weights, cell_offsets, step_start)[None]
-    far = along(piece, 4)
     piece_x = swap_x(piece)
     chosen = order(own, step_start)
-    chosen, piece_x, far = lax.optimization_barrier((chosen, piece_x, far))
     right = lax.all_to_all(chosen, "row", split_axis=0, concat_axis=0, tiled=True)
-    pieces = gather_left(piece, piece_x, far)
+    pieces = gather_left(piece, piece_x)
     return gram(assemble(pieces, rows_dev), right)[None]
 
 

time: 117 us -> 124 us (1.060)
  waiting for transfers between devices: 45.2 us -> 64.5 us
  starting transfers between devices: 61.1 us -> 48.8 us
    ppermute x4, waiting for transfers between devices: 2.69 us -> 23 us  [along(): return lax.ppermute(block, 'col', RING[hop])]
    ppermute x4, starting transfers between devices: 19 us -> 13.8 us  [along(): return lax.ppermute(block, 'col', RING[hop])]
    ppermute x2 -> x1, starting transfers between devices: 6.86 us -> 2.85 us  [swap_x(): return lax.ppermute(block, 'col', SWAP_X)]
    ppermute x4, starting transfers between devices: 13.7 us -> 10.6 us  [swap_core(): return lax.ppermute(block, 'col', SWAP_CORE)]
  transfers between devices with their start and end apart: 12 -> 11, of which waited for: 7 -> 6; matrix products, arithmetic and copies ran while one was open for 0% -> 0% of each run, Pallas kernels for 2% -> 1%
where the time goes in v9:
time: 124 us; the launch traced here: 123 us
  waiting for transfers between devices  64.5 us (52%)
  starting transfers between devices  48.8 us (39%)
  Pallas kernels  8.37 us (7%)
    all_to_all x1, waiting for transfers between devices, local(): own = lax.all_to_all(blocks, 'col', split_axis=0, concat_axis=0, tiled=True)  39.2 us
    ppermute x4, waiting for transfers between devices, along(): return lax.ppermute(block, 'col', RING[hop])  23 us
    all_to_all x1, starting transfers between devices, local(): own = lax.all_to_all(blocks, 'col', split_axis=0, concat_axis=0, tiled=True)  14.6 us
    ppermute x4, starting transfers between devices, along(): return lax.ppermute(block, 'col', RING[hop])  13.8 us
    ppermute x4, starting transfers between devices, swap_core(): return lax.ppermute(block, 'col', SWAP_CORE)  10.6 us
    all_to_all x1, starting transfers between devices, local(): lax.all_to_all(chosen, 'row', split_axis=0, concat_axis=0, tiled=True)  7 us
    pallas_call x1, Pallas kernels, gram(): pl.pallas_call(gram_kernel, out_shape=jax.ShapeDtypeStruct((rows_dev, wid...  5.52 us
    ppermute x1, starting transfers between devices, swap_x(): return lax.ppermute(block, 'col', SWAP_X)  2.85 us
  transfers between devices with their start and end apart: 11, of which 6 were waited for; matrix products, arithmetic and copies ran while one was open for 0% of the time, Pallas kernels for 1%

profile of v9, /device:TPU:1, one launch (start us, length us, event | category | flops | bytes accessed | tf_op | source)
XLA Modules:
  0.0 122.6 jit_solution(9146367884735577757)
XLA Ops:
  0.0 0.0 copy-start
  0.0 0.0 copy-start.1
  0.0 14.6 %all-to-all-start = ((bf16[32,48,512]{2,1,0:T(8,128)(2,1)}), bf16[32,48,512]{2,1,0:T(8,128)(2,1)S(1)}, u32[]{:S(2)}, u32[]{:S(2)}) async-start(bf16[32,48,512]{2,1,0:T(8,128)(2,1)} %bitcast.6), calls=%async_computation | async-start | bytes 3145728 | tf_op jit(solution)/shard_map/all_to_all | solution.py:190
  15.2 39.2 %all-to-all-done.own_ref = bf16[32,48,512]{2,1,0:T(8,128)(2,1)S(1)} async-done(((bf16[32,48,512]{2,1,0:T(8,128)(2,1)}), bf16[32,48,512]{2,1,0:T(8,128)(2,1)S(1)}, u32[]{:S(2)}, u32[]{:S(2)}) %all-to-all-start) | async-done | bytes 1572896 | tf_op jit(solution)/shard_map/all_to_all | solution.py:190
  54.4 0.0 copy-done
  54.4 0.0 copy-done.1
  54.4 1.0 shard_map.46
  55.4 2.8 %collective-permute-start = (bf16[1,48,1024]{2,1,0:T(8,128)(2,1)S(1)}, bf16[1,48,1024]{2,1,0:T(8,128)(2,1)S(1)}, u32[]{:S(2)}, u32[]{:S(2)}) collective-permute-start(bf16[1,48,1024]{2,1,0:T(8,128)(2,1)S(1)} %bitcast.3), channel_id=1, source_target_pairs={{0,16},{1,17},{2,18},{3,19},{4,20},{5,21},{6,22},{7,23},{8,24},{9,... | collective-permute-start | bytes 294920 | tf_op jit(solution)/shard_map/ppermute | solution.py:163
  58.3 1.6 %shard_map.48 = bf16[16,2,48,512]{3,2,1,0:T(8,128)(2,1)} custom-call(s32[1]{0:T(128)S(6)} %copy.5.start_ref, bf16[32,48,512]{2,1,0:T(8,128)(2,1)S(1)} %all-to-all-done.own_ref), custom_call_target="tpu_custom_call" | custom-call | bytes 3145728 | tf_op jit(solution)/shard_map/pallas_call | solution.py:66
  59.9 7.0 %all-to-all-start.1 = ((bf16[16,2,48,512]{3,2,1,0:T(8,128)(2,1)}), bf16[16,2,48,512]{3,2,1,0:T(8,128)(2,1)}, u32[]{:S(2)}, u32[]{:S(2)}) async-start(bf16[16,2,48,512]{3,2,1,0:T(8,128)(2,1)} %shard_map.48), calls=%async_computation.1 | async-start | bytes 3145728 | tf_op jit(solution)/shard_map/all_to_all | solution.py:194
  66.9 0.0 collective-permute-done
  66.9 2.9 %collective-permute-start.1 = (bf16[2,48,1024]{2,1,0:T(8,128)(2,1)S(1)}, bf16[2,48,1024]{2,1,0:T(8,128)(2,1)S(1)}, u32[]{:S(2)}, u32[]{:S(2)}) collective-permute-start(bf16[2,48,1024]{2,1,0:T(8,128)(2,1)S(1)} %pad_maximum_fusion.2), channel_id=1, source_target_pairs={{0,1},{1,0},{2,3},{3,2},{4,5},{5,4},{6,7},{7,6},{8,9},{9,8},{10,11... | collective-permute-start | bytes 589832 | tf_op jit(solution)/shard_map/ppermute | solution.py:167
  69.8 1.0 collective-permute-done.1
  70.9 2.3 %collective-permute-start.2 = (bf16[4,48,1024]{2,1,0:T(8,128)(2,1)S(1)}, bf16[4,48,1024]{2,1,0:T(8,128)(2,1)S(1)}, u32[]{:S(2)}, u32[]{:S(2)}) collective-permute-start(bf16[4,48,1024]{2,1,0:T(8,128)(2,1)S(1)} %pad_maximum_fusion.1.refs_0_), channel_id=1, source_target_pairs={{0,2},{1,15},{2,4},{3,1},{4,6},{5,3},{6,8},{7,5},{8,10},{9,7},{10,... | collective-permute-start | bytes 1179656 | tf_op jit(solution)/shard_map/ppermute | solution.py:171
  73.2 7.7 %collective-permute-done.2.refs_1_ = bf16[4,48,1024]{2,1,0:T(8,128)(2,1)S(1)} collective-permute-done((bf16[4,48,1024]{2,1,0:T(8,128)(2,1)S(1)}, bf16[4,48,1024]{2,1,0:T(8,128)(2,1)S(1)}, u32[]{:S(2)}, u32[]{:S(2)}) %collective-permute-start.2) | collective-permute-done | bytes 393248 | tf_op jit(solution)/shard_map/ppermute | solution.py:171
  80.9 3.1 %collective-permute-start.6 = (bf16[4,48,1024]{2,1,0:T(8,128)(2,1)S(1)}, bf16[4,48,1024]{2,1,0:T(8,128)(2,1)S(1)}, u32[]{:S(2)}, u32[]{:S(2)}) collective-permute-start(bf16[4,48,1024]{2,1,0:T(8,128)(2,1)S(1)} %collective-permute-done.2.refs_1_), channel_id=1, source_target_pairs={{0,1},{1,0},{2,3},{3,2},{4,5},{5,4},{6,7},{7,6},{8,9},{9,8},{10,11... | collective-permute-start | bytes 1179656 | tf_op jit(solution)/shard_map/ppermute | solution.py:167
  84.1 2.8 %collective-permute-start.4 = (bf16[4,48,1024]{2,1,0:T(8,128)(2,1)S(1)}, bf16[4,48,1024]{2,1,0:T(8,128)(2,1)S(1)}, u32[]{:S(2)}, u32[]{:S(2)}) collective-permute-start(bf16[4,48,1024]{2,1,0:T(8,128)(2,1)S(1)} %collective-permute-done.2.refs_1_), channel_id=1, source_target_pairs={{0,4},{1,13},{2,6},{3,15},{4,8},{5,1},{6,10},{7,3},{8,12},{9,5},{1... | collective-permute-start | bytes 1179656 | tf_op jit(solution)/shard_map/ppermute | solution.py:171
  86.9 4.0 %collective-permute-start.5 = (bf16[2,48,1024]{2,1,0:T(8,128)(2,1)S(1)}, bf16[2,48,1024]{2,1,0:T(8,128)(2,1)S(1)}, u32[]{:S(2)}, u32[]{:S(2)}) collective-permute-start(bf16[2,48,1024]{2,1,0:T(8,128)(2,1)S(1)} %slice.4), channel_id=1, source_target_pairs={{0,6},{1,11},{2,8},{3,13},{4,10},{5,15},{6,12},{7,1},{8,14},{9,3},... | collective-permute-start | bytes 589832 | tf_op jit(solution)/shard_map/ppermute | solution.py:171
  90.9 4.7 %collective-permute-start.3 = (bf16[4,48,1024]{2,1,0:T(8,128)(2,1)S(1)}, bf16[4,48,1024]{2,1,0:T(8,128)(2,1)S(1)}, u32[]{:S(2)}, u32[]{:S(2)}) collective-permute-start(bf16[4,48,1024]{2,1,0:T(8,128)(2,1)S(1)} %pad_maximum_fusion.1.refs_0_), channel_id=1, source_target_pairs={{0,4},{1,13},{2,6},{3,15},{4,8},{5,1},{6,10},{7,3},{8,12},{9,5},{1... | collective-permute-start | bytes 1179656 | tf_op jit(solution)/shard_map/ppermute | solution.py:171
  95.6 9.8 %collective-permute-done.5.refs_4_ = bf16[2,48,1024]{2,1,0:T(8,128)(2,1)S(1)} collective-permute-done((bf16[2,48,1024]{2,1,0:T(8,128)(2,1)S(1)}, bf16[2,48,1024]{2,1,0:T(8,128)(2,1)S(1)}, u32[]{:S(2)}, u32[]{:S(2)}) %collective-permute-start.5) | collective-permute-done | bytes 196640 | tf_op jit(solution)/shard_map/ppermute | solution.py:171
  105.5 0.0 collective-permute-done.6.refs_5_
  105.5 0.0 collective-permute-done.4.refs_3_
  105.5 0.1 pad_maximum_fusion
  105.6 1.9 %collective-permute-start.8 = (bf16[6,48,1024]{2,1,0:T(8,128)(2,1)S(1)}, bf16[6,48,1024]{2,1,0:T(8,128)(2,1)S(1)}, u32[]{:S(2)}, u32[]{:S(2)}) collective-permute-start(bf16[6,48,1024]{2,1,0:T(8,128)(2,1)S(1)} %pad_maximum_fusion), channel_id=1, source_target_pairs={{0,1},{1,0},{2,3},{3,2},{4,5},{5,4},{6,7},{7,6},{8,9},{9,8},{10,11... | collective-permute-start | bytes 1769480 | tf_op jit(solution)/shard_map/ppermute | solution.py:167
  107.5 5.4 %collective-permute-done.3.refs_2_ = bf16[4,48,1024]{2,1,0:T(8,128)(2,1)S(1)} collective-permute-done((bf16[4,48,1024]{2,1,0:T(8,128)(2,1)S(1)}, bf16[4,48,1024]{2,1,0:T(8,128)(2,1)S(1)}, u32[]{:S(2)}, u32[]{:S(2)}) %collective-permute-start.3) | collective-permute-done | bytes 393248 | tf_op jit(solution)/shard_map/ppermute | solution.py:171
  112.9 2.7 %collective-permute-start.7 = (bf16[4,48,1024]{2,1,0:T(8,128)(2,1)S(1)}, bf16[4,48,1024]{2,1,0:T(8,128)(2,1)S(1)}, u32[]{:S(2)}, u32[]{:S(2)}) collective-permute-start(bf16[4,48,1024]{2,1,0:T(8,128)(2,1)S(1)} %collective-permute-done.3.refs_2_), channel_id=1, source_target_pairs={{0,1},{1,0},{2,3},{3,2},{4,5},{5,4},{6,7},{7,6},{8,9},{9,8},{10,11... | collective-permute-start | bytes 1179656 | tf_op jit(solution)/shard_map/ppermute | solution.py:167
  115.5 1.3 %collective-permute-done.7.refs_6_ = bf16[4,48,1024]{2,1,0:T(8,128)(2,1)S(1)} collective-permute-done((bf16[4,48,1024]{2,1,0:T(8,128)(2,1)S(1)}, bf16[4,48,1024]{2,1,0:T(8,128)(2,1)S(1)}, u32[]{:S(2)}, u32[]{:S(2)}) %collective-permute-start.7) | collective-permute-done | bytes 393248 | tf_op jit(solution)/shard_map/ppermute | solution.py:167
  116.9 0.0 collective-permute-done.8.refs_7_
  116.9 0.2 shard_map.47.left_ref
  117.1 0.0 all-to-all-done.1.right_ref
  117.1 5.5 %shard_map.49 = bf16[1536,768]{1,0:T(8,128)(2,1)} custom-call(bf16[1536,1024]{1,0:T(8,128)(2,1)S(1)} %shard_map.47.left_ref, bf16[16,2,48,512]{3,2,1,0:T(8,128)(2,1)} %all-to-all-done.1.right_ref), custom_call_target="tpu_custom_call" | custom-call | tf_op jit(solution)/shard_map/pallas_call | solution.py:131
  (3 shorter events, 0.1 us)
Async XLA Ops:
  0.0 54.4 %copy-start = (s32[3]{0:T(128)S(1)}, s32[3]{0:T(128)}, u32[]{:S(2)}) copy-start(s32[3]{0:T(128)} %offsets_ref.1) | copy-start | bytes 40
  0.0 54.4 %copy-start.1 = (f32[4]{0:T(128)S(1)}, f32[4]{0:T(128)}, u32[]{:S(2)}) copy-start(f32[4]{0:T(128)} %weights_ref.1) | copy-start | bytes 52
  0.0 54.4 %all-to-all-start = ((bf16[32,48,512]{2,1,0:T(8,128)(2,1)}), bf16[32,48,512]{2,1,0:T(8,128)(2,1)S(1)}, u32[]{:S(2)}, u32[]{:S(2)}) async-start(bf16[32,48,512]{2,1,0:T(8,128)(2,1)} %bitcast.6), calls=%async_computation | async-start | bytes 3145728 | tf_op jit(solution)/shard_map/all_to_all | solution.py:190
  55.4 11.5 %collective-permute-start = (bf16[1,48,1024]{2,1,0:T(8,128)(2,1)S(1)}, bf16[1,48,1024]{2,1,0:T(8,128)(2,1)S(1)}, u32[]{:S(2)}, u32[]{:S(2)}) collective-permute-start(bf16[1,48,1024]{2,1,0:T(8,128)(2,1)S(1)} %bitcast.3), channel_id=1, source_target_pairs={{0,16},{1,17},{2,18},{3,19},{4,20},{5,21},{6,22},{7,23},{8,24},{9,... | collective-permute-start | bytes 294920 | tf_op jit(solution)/shard_map/ppermute | solution.py:163
  59.9 57.2 %all-to-all-start.1 = ((bf16[16,2,48,512]{3,2,1,0:T(8,128)(2,1)}), bf16[16,2,48,512]{3,2,1,0:T(8,128)(2,1)}, u32[]{:S(2)}, u32[]{:S(2)}) async-start(bf16[16,2,48,512]{3,2,1,0:T(8,128)(2,1)} %shard_map.48), calls=%async_computation.1 | async-start | bytes 3145728 | tf_op jit(solution)/shard_map/all_to_all | solution.py:194
  66.9 3.9 %collective-permute-start.1 = (bf16[2,48,1024]{2,1,0:T(8,128)(2,1)S(1)}, bf16[2,48,1024]{2,1,0:T(8,128)(2,1)S(1)}, u32[]{:S(2)}, u32[]{:S(2)}) collective-permute-start(bf16[2,48,1024]{2,1,0:T(8,128)(2,1)S(1)} %pad_maximum_fusion.2), channel_id=1, source_target_pairs={{0,1},{1,0},{2,3},{3,2},{4,5},{5,4},{6,7},{7,6},{8,9},{9,8},{10,11... | collective-permute-start | bytes 589832 | tf_op jit(solution)/shard_map/ppermute | solution.py:167
  70.9 10.0 %collective-permute-start.2 = (bf16[4,48,1024]{2,1,0:T(8,128)(2,1)S(1)}, bf16[4,48,1024]{2,1,0:T(8,128)(2,1)S(1)}, u32[]{:S(2)}, u32[]{:S(2)}) collective-permute-start(bf16[4,48,1024]{2,1,0:T(8,128)(2,1)S(1)} %pad_maximum_fusion.1.refs_0_), channel_id=1, source_target_pairs={{0,2},{1,15},{2,4},{3,1},{4,6},{5,3},{6,8},{7,5},{8,10},{9,7},{10,... | collective-permute-start | bytes 1179656 | tf_op jit(solution)/shard_map/ppermute | solution.py:171
  80.9 24.6 %collective-permute-start.6 = (bf16[4,48,1024]{2,1,0:T(8,128)(2,1)S(1)}, bf16[4,48,1024]{2,1,0:T(8,128)(2,1)S(1)}, u32[]{:S(2)}, u32[]{:S(2)}) collective-permute-start(bf16[4,48,1024]{2,1,0:T(8,128)(2,1)S(1)} %collective-permute-done.2.refs_1_), channel_id=1, source_target_pairs={{0,1},{1,0},{2,3},{3,2},{4,5},{5,4},{6,7},{7,6},{8,9},{9,8},{10,11... | collective-permute-start | bytes 1179656 | tf_op jit(solution)/shard_map/ppermute | solution.py:167
  84.1 21.4 %collective-permute-start.4 = (bf16[4,48,1024]{2,1,0:T(8,128)(2,1)S(1)}, bf16[4,48,1024]{2,1,0:T(8,128)(2,1)S(1)}, u32[]{:S(2)}, u32[]{:S(2)}) collective-permute-start(bf16[4,48,1024]{2,1,0:T(8,128)(2,1)S(1)} %collective-permute-done.2.refs_1_), channel_id=1, source_target_pairs={{0,4},{1,13},{2,6},{3,15},{4,8},{5,1},{6,10},{7,3},{8,12},{9,5},{1... | collective-permute-start | bytes 1179656 | tf_op jit(solution)/shard_map/ppermute | solution.py:171
  86.9 18.6 %collective-permute-start.5 = (bf16[2,48,1024]{2,1,0:T(8,128)(2,1)S(1)}, bf16[2,48,1024]{2,1,0:T(8,128)(2,1)S(1)}, u32[]{:S(2)}, u32[]{:S(2)}) collective-permute-start(bf16[2,48,1024]{2,1,0:T(8,128)(2,1)S(1)} %slice.4), channel_id=1, source_target_pairs={{0,6},{1,11},{2,8},{3,13},{4,10},{5,15},{6,12},{7,1},{8,14},{9,3},... | collective-permute-start | bytes 589832 | tf_op jit(solution)/shard_map/ppermute | solution.py:171
  90.9 22.0 %collective-permute-start.3 = (bf16[4,48,1024]{2,1,0:T(8,128)(2,1)S(1)}, bf16[4,48,1024]{2,1,0:T(8,128)(2,1)S(1)}, u32[]{:S(2)}, u32[]{:S(2)}) collective-permute-start(bf16[4,48,1024]{2,1,0:T(8,128)(2,1)S(1)} %pad_maximum_fusion.1.refs_0_), channel_id=1, source_target_pairs={{0,4},{1,13},{2,6},{3,15},{4,8},{5,1},{6,10},{7,3},{8,12},{9,5},{1... | collective-permute-start | bytes 1179656 | tf_op jit(solution)/shard_map/ppermute | solution.py:171
  105.6 11.3 %collective-permute-start.8 = (bf16[6,48,1024]{2,1,0:T(8,128)(2,1)S(1)}, bf16[6,48,1024]{2,1,0:T(8,128)(2,1)S(1)}, u32[]{:S(2)}, u32[]{:S(2)}) collective-permute-start(bf16[6,48,1024]{2,1,0:T(8,128)(2,1)S(1)} %pad_maximum_fusion), channel_id=1, source_target_pairs={{0,1},{1,0},{2,3},{3,2},{4,5},{5,4},{6,7},{7,6},{8,9},{9,8},{10,11... | collective-permute-start | bytes 1769480 | tf_op jit(solution)/shard_map/ppermute | solution.py:167
  112.9 4.0 %collective-permute-start.7 = (bf16[4,48,1024]{2,1,0:T(8,128)(2,1)S(1)}, bf16[4,48,1024]{2,1,0:T(8,128)(2,1)S(1)}, u32[]{:S(2)}, u32[]{:S(2)}) collective-permute-start(bf16[4,48,1024]{2,1,0:T(8,128)(2,1)S(1)} %collective-permute-done.3.refs_2_), channel_id=1, source_target_pairs={{0,1},{1,0},{2,3},{3,2},{4,5},{5,4},{6,7},{7,6},{8,9},{9,8},{10,11... | collective-permute-start | bytes 1179656 | tf_op jit(solution)/shard_map/ppermute | solution.py:167

commit v10 on v7

--- a/solution.py
+++ b/solution.py
@@ -51,13 +51,17 @@
     )(step_start, cell_offsets, stencil_weights, own)
 
 
-def order_kernel(start_ref, own_ref, chosen_ref):
+def order_kernel(start_ref, own_ref, chosen_ref, sem):
     count = own_ref.shape[0]
     start = lax.rem(start_ref[0], count)
-
-    @pl.loop(0, count)
-    def _(t):
-        chosen_ref[t // STEPS, lax.rem(t, STEPS)] = own_ref[lax.rem(t + start, count)]
+    moves = [
+        pltpu.make_async_copy(own_ref.at[lax.rem(t + start, count)], chosen_ref.at[t // STEPS, t % STEPS], sem.at[t])
+        for t in range(count)
+    ]
+    for move in moves:
+        move.start()
+    for move in moves:
+        move.wait()
 
 
 def order(own, step_start):
@@ -67,7 +71,8 @@
         order_kernel,
         out_shape=jax.ShapeDtypeStruct((count // STEPS, STEPS, rows, cells), own.dtype),
         in_specs=[pl.BlockSpec(memory_space=pltpu.SMEM), vmem],
-        out_specs=vmem,
+        out_specs=pl.BlockSpec(memory_space=pl.ANY),
+        scratch_shapes=[pltpu.SemaphoreType.DMA((count,))],
         compiler_params=pltpu.CompilerParams(vmem_limit_bytes=SELECT_LIMIT),
         cost_estimate=pl.CostEstimate(flops=0, bytes_accessed=4 * own.size, transcendentals=0),
     )(step_start, own)

time: 115 us -> 115 us (level)
  transfers between devices with their start and end apart: 12 -> 12, of which waited for: 7 -> 7; matrix products, arithmetic and copies ran while one was open for 0% -> 0% of each run, Pallas kernels for 2% -> 1%
where the time goes in v10:
time: 115 us; the launch traced here: 113 us
  starting transfers between devices  55.4 us (48%)
  waiting for transfers between devices  48.5 us (42%)
  Pallas kernels  8.14 us (7%)
    all_to_all x1, waiting for transfers between devices, local(): own = lax.all_to_all(blocks, 'col', split_axis=0, concat_axis=0, tiled=True)  39.2 us
    all_to_all x1, starting transfers between devices, local(): own = lax.all_to_all(blocks, 'col', split_axis=0, concat_axis=0, tiled=True)  14.6 us
    ppermute x4, starting transfers between devices, along(): return lax.ppermute(block, 'col', RING[hop])  13.4 us
    ppermute x4, starting transfers between devices, swap_core(): return lax.ppermute(block, 'col', SWAP_CORE)  11.1 us
    ppermute x2, starting transfers between devices, swap_x(): return lax.ppermute(block, 'col', SWAP_X)  9.37 us
    all_to_all x1, starting transfers between devices, local(): lax.all_to_all(chosen, 'row', split_axis=0, concat_axis=0, tiled=True)  7.01 us
    pallas_call x1, Pallas kernels, gram(): pl.pallas_call(gram_kernel, out_shape=jax.ShapeDtypeStruct((rows_dev, wid...  5.49 us
    ppermute x4, waiting for transfers between devices, along(): return lax.ppermute(block, 'col', RING[hop])  2.84 us
  transfers between devices with their start and end apart: 12, of which 7 were waited for; matrix products, arithmetic and copies ran while one was open for 0% of the time, Pallas kernels for 1%

profile of v10, /device:TPU:1, one launch (start us, length us, event | category | flops | bytes accessed | tf_op | source)
XLA Modules:
  0.0 113.0 jit_solution(7061508034770201553)
XLA Ops:
  0.0 0.0 copy-start
  0.0 14.6 %all-to-all-start = ((bf16[32,48,512]{2,1,0:T(8,128)(2,1)}), bf16[32,48,512]{2,1,0:T(8,128)(2,1)S(1)}, u32[]{:S(2)}, u32[]{:S(2)}) async-start(bf16[32,48,512]{2,1,0:T(8,128)(2,1)} %bitcast.7), calls=%async_computation | async-start | bytes 3145728 | tf_op jit(solution)/shard_map/all_to_all | solution.py:194
  15.2 39.2 %all-to-all-done.own_ref = bf16[32,48,512]{2,1,0:T(8,128)(2,1)S(1)} async-done(((bf16[32,48,512]{2,1,0:T(8,128)(2,1)}), bf16[32,48,512]{2,1,0:T(8,128)(2,1)S(1)}, u32[]{:S(2)}, u32[]{:S(2)}) %all-to-all-start) | async-done | bytes 1572896 | tf_op jit(solution)/shard_map/all_to_all | solution.py:194
  54.4 0.0 copy-done
  54.4 0.0 copy-done.1
  54.4 1.0 shard_map.46
  55.4 3.1 %collective-permute-start.1 = (bf16[1,48,1024]{2,1,0:T(8,128)(2,1)S(1)}, bf16[1,48,1024]{2,1,0:T(8,128)(2,1)S(1)}, u32[]{:S(2)}, u32[]{:S(2)}) collective-permute-start(bf16[1,48,1024]{2,1,0:T(8,128)(2,1)S(1)} %bitcast.3), channel_id=1, source_target_pairs={{0,8},{1,9},{2,10},{3,11},{4,12},{5,13},{6,14},{7,15},{8,0},{9,1},... | collective-permute-start | bytes 294920 | tf_op jit(solution)/shard_map/ppermute | solution.py:176
  58.6 4.1 %collective-permute-start = (bf16[1,48,1024]{2,1,0:T(8,128)(2,1)S(1)}, bf16[1,48,1024]{2,1,0:T(8,128)(2,1)S(1)}, u32[]{:S(2)}, u32[]{:S(2)}) collective-permute-start(bf16[1,48,1024]{2,1,0:T(8,128)(2,1)S(1)} %bitcast.4), channel_id=1, source_target_pairs={{0,16},{1,17},{2,18},{3,19},{4,20},{5,21},{6,22},{7,23},{8,24},{9,... | collective-permute-start | bytes 294920 | tf_op jit(solution)/shard_map/ppermute | solution.py:168
  62.7 1.4 %shard_map.48 = bf16[16,2,48,512]{3,2,1,0:T(8,128)(2,1)} custom-call(s32[1]{0:T(128)S(6)} %copy.5.start_ref, bf16[32,48,512]{2,1,0:T(8,128)(2,1)S(1)} %all-to-all-done.own_ref), custom_call_target="tpu_custom_call" | custom-call | bytes 3145728 | tf_op jit(solution)/shard_map/pallas_call | solution.py:70
  64.1 7.0 %all-to-all-start.1 = ((bf16[16,2,48,512]{3,2,1,0:T(8,128)(2,1)}), bf16[16,2,48,512]{3,2,1,0:T(8,128)(2,1)}, u32[]{:S(2)}, u32[]{:S(2)}) async-start(bf16[16,2,48,512]{3,2,1,0:T(8,128)(2,1)} %shard_map.48), calls=%async_computation.1 | async-start | bytes 3145728 | tf_op jit(solution)/shard_map/all_to_all | solution.py:200
  71.1 0.0 collective-permute-done.1.refs_4_
  71.2 0.0 collective-permute-done
  71.2 3.1 %collective-permute-start.2 = (bf16[2,48,1024]{2,1,0:T(8,128)(2,1)S(1)}, bf16[2,48,1024]{2,1,0:T(8,128)(2,1)S(1)}, u32[]{:S(2)}, u32[]{:S(2)}) collective-permute-start(bf16[2,48,1024]{2,1,0:T(8,128)(2,1)S(1)} %pad_maximum_fusion.2), channel_id=1, source_target_pairs={{0,1},{1,0},{2,3},{3,2},{4,5},{5,4},{6,7},{7,6},{8,9},{9,8},{10,11... | collective-permute-start | bytes 589832 | tf_op jit(solution)/shard_map/ppermute | solution.py:172
  74.3 1.0 collective-permute-done.2
  75.4 3.6 %collective-permute-start.3 = (bf16[4,48,1024]{2,1,0:T(8,128)(2,1)S(1)}, bf16[4,48,1024]{2,1,0:T(8,128)(2,1)S(1)}, u32[]{:S(2)}, u32[]{:S(2)}) collective-permute-start(bf16[4,48,1024]{2,1,0:T(8,128)(2,1)S(1)} %pad_maximum_fusion.1.refs_0_), channel_id=1, source_target_pairs={{0,2},{1,15},{2,4},{3,1},{4,6},{5,3},{6,8},{7,5},{8,10},{9,7},{10,... | collective-permute-start | bytes 1179656 | tf_op jit(solution)/shard_map/ppermute | solution.py:176
  79.1 4.7 %collective-permute-start.4 = (bf16[4,48,1024]{2,1,0:T(8,128)(2,1)S(1)}, bf16[4,48,1024]{2,1,0:T(8,128)(2,1)S(1)}, u32[]{:S(2)}, u32[]{:S(2)}) collective-permute-start(bf16[4,48,1024]{2,1,0:T(8,128)(2,1)S(1)} %pad_maximum_fusion.1.refs_0_), channel_id=1, source_target_pairs={{0,4},{1,13},{2,6},{3,15},{4,8},{5,1},{6,10},{7,3},{8,12},{9,5},{1... | collective-permute-start | bytes 1179656 | tf_op jit(solution)/shard_map/ppermute | solution.py:176
  83.8 5.3 %collective-permute-start.6 = (bf16[1,48,1024]{2,1,0:T(8,128)(2,1)S(1)}, bf16[1,48,1024]{2,1,0:T(8,128)(2,1)S(1)}, u32[]{:S(2)}, u32[]{:S(2)}) collective-permute-start(bf16[1,48,1024]{2,1,0:T(8,128)(2,1)S(1)} %collective-permute-done.1.refs_4_), channel_id=1, source_target_pairs={{0,16},{1,17},{2,18},{3,19},{4,20},{5,21},{6,22},{7,23},{8,24},{9,... | collective-permute-start | bytes 294920 | tf_op jit(solution)/shard_map/ppermute | solution.py:168
  89.1 0.0 collective-permute-done.3.refs_1_
  89.1 1.9 %collective-permute-start.5 = (bf16[4,48,1024]{2,1,0:T(8,128)(2,1)S(1)}, bf16[4,48,1024]{2,1,0:T(8,128)(2,1)S(1)}, u32[]{:S(2)}, u32[]{:S(2)}) collective-permute-start(bf16[4,48,1024]{2,1,0:T(8,128)(2,1)S(1)} %collective-permute-done.3.refs_1_), channel_id=1, source_target_pairs={{0,4},{1,13},{2,6},{3,15},{4,8},{5,1},{6,10},{7,3},{8,12},{9,5},{1... | collective-permute-start | bytes 1179656 | tf_op jit(solution)/shard_map/ppermute | solution.py:176
  91.0 2.1 %collective-permute-done.6.refs_5_ = bf16[1,48,1024]{2,1,0:T(8,128)(2,1)S(1)} collective-permute-done((bf16[1,48,1024]{2,1,0:T(8,128)(2,1)S(1)}, bf16[1,48,1024]{2,1,0:T(8,128)(2,1)S(1)}, u32[]{:S(2)}, u32[]{:S(2)}) %collective-permute-start.6) | collective-permute-done | bytes 98336 | tf_op jit(solution)/shard_map/ppermute | solution.py:168
  93.1 1.2 %collective-permute-done.4.refs_2_ = bf16[4,48,1024]{2,1,0:T(8,128)(2,1)S(1)} collective-permute-done((bf16[4,48,1024]{2,1,0:T(8,128)(2,1)S(1)}, bf16[4,48,1024]{2,1,0:T(8,128)(2,1)S(1)}, u32[]{:S(2)}, u32[]{:S(2)}) %collective-permute-start.4) | collective-permute-done | bytes 393248 | tf_op jit(solution)/shard_map/ppermute | solution.py:176
  94.3 0.1 pad_maximum_fusion
  94.4 3.7 %collective-permute-start.8 = (bf16[6,48,1024]{2,1,0:T(8,128)(2,1)S(1)}, bf16[6,48,1024]{2,1,0:T(8,128)(2,1)S(1)}, u32[]{:S(2)}, u32[]{:S(2)}) collective-permute-start(bf16[6,48,1024]{2,1,0:T(8,128)(2,1)S(1)} %pad_maximum_fusion), channel_id=1, source_target_pairs={{0,1},{1,0},{2,3},{3,2},{4,5},{5,4},{6,7},{7,6},{8,9},{9,8},{10,11... | collective-permute-start | bytes 1769480 | tf_op jit(solution)/shard_map/ppermute | solution.py:172
  98.1 1.9 %collective-permute-start.7 = (bf16[4,48,1024]{2,1,0:T(8,128)(2,1)S(1)}, bf16[4,48,1024]{2,1,0:T(8,128)(2,1)S(1)}, u32[]{:S(2)}, u32[]{:S(2)}) collective-permute-start(bf16[4,48,1024]{2,1,0:T(8,128)(2,1)S(1)} %collective-permute-done.3.refs_1_), channel_id=1, source_target_pairs={{0,1},{1,0},{2,3},{3,2},{4,5},{5,4},{6,7},{7,6},{8,9},{9,8},{10,11... | collective-permute-start | bytes 1179656 | tf_op jit(solution)/shard_map/ppermute | solution.py:172
  100.0 1.7 %collective-permute-done.5.refs_3_ = bf16[4,48,1024]{2,1,0:T(8,128)(2,1)S(1)} collective-permute-done((bf16[4,48,1024]{2,1,0:T(8,128)(2,1)S(1)}, bf16[4,48,1024]{2,1,0:T(8,128)(2,1)S(1)}, u32[]{:S(2)}, u32[]{:S(2)}) %collective-permute-start.5) | collective-permute-done | bytes 393248 | tf_op jit(solution)/shard_map/ppermute | solution.py:176
  101.7 2.3 %collective-permute-start.9 = (bf16[4,48,1024]{2,1,0:T(8,128)(2,1)S(1)}, bf16[4,48,1024]{2,1,0:T(8,128)(2,1)S(1)}, u32[]{:S(2)}, u32[]{:S(2)}) collective-permute-start(bf16[4,48,1024]{2,1,0:T(8,128)(2,1)S(1)} %collective-permute-done.5.refs_3_), channel_id=1, source_target_pairs={{0,1},{1,0},{2,3},{3,2},{4,5},{5,4},{6,7},{7,6},{8,9},{9,8},{10,11... | collective-permute-start | bytes 1179656 | tf_op jit(solution)/shard_map/ppermute | solution.py:172
  104.0 0.0 collective-permute-done.7.refs_6_
  104.0 0.0 collective-permute-done.8.refs_7_
  104.0 1.3 %collective-permute-done.9.refs_8_ = bf16[4,48,1024]{2,1,0:T(8,128)(2,1)S(1)} collective-permute-done((bf16[4,48,1024]{2,1,0:T(8,128)(2,1)S(1)}, bf16[4,48,1024]{2,1,0:T(8,128)(2,1)S(1)}, u32[]{:S(2)}, u32[]{:S(2)}) %collective-permute-start.9) | collective-permute-done | bytes 393248 | tf_op jit(solution)/shard_map/ppermute | solution.py:172
  105.3 0.2 shard_map.47.left_ref
  105.5 2.0 %all-to-all-done.1.right_ref = bf16[16,2,48,512]{3,2,1,0:T(8,128)(2,1)} async-done(((bf16[16,2,48,512]{3,2,1,0:T(8,128)(2,1)}), bf16[16,2,48,512]{3,2,1,0:T(8,128)(2,1)}, u32[]{:S(2)}, u32[]{:S(2)}) %all-to-all-start.1) | async-done | bytes 1572896 | tf_op jit(solution)/shard_map/all_to_all | solution.py:200
  107.5 5.5 %shard_map.49 = bf16[1536,768]{1,0:T(8,128)(2,1)} custom-call(bf16[1536,1024]{1,0:T(8,128)(2,1)S(1)} %shard_map.47.left_ref, bf16[16,2,48,512]{3,2,1,0:T(8,128)(2,1)} %all-to-all-done.1.right_ref), custom_call_target="tpu_custom_call" | custom-call | tf_op jit(solution)/shard_map/pallas_call | solution.py:136
  (3 shorter events, 0.1 us)
Async XLA Ops:
  0.0 54.4 %copy-start = (s32[3]{0:T(128)S(1)}, s32[3]{0:T(128)}, u32[]{:S(2)}) copy-start(s32[3]{0:T(128)} %offsets_ref.1) | copy-start | bytes 40
  0.0 54.4 %copy-start.1 = (f32[4]{0:T(128)S(1)}, f32[4]{0:T(128)}, u32[]{:S(2)}) copy-start(f32[4]{0:T(128)} %weights_ref.1) | copy-start | bytes 52
  0.0 54.4 %all-to-all-start = ((bf16[32,48,512]{2,1,0:T(8,128)(2,1)}), bf16[32,48,512]{2,1,0:T(8,128)(2,1)S(1)}, u32[]{:S(2)}, u32[]{:S(2)}) async-start(bf16[32,48,512]{2,1,0:T(8,128)(2,1)} %bitcast.7), calls=%async_computation | async-start | bytes 3145728 | tf_op jit(solution)/shard_map/all_to_all | solution.py:194
  55.4 15.7 %collective-permute-start.1 = (bf16[1,48,1024]{2,1,0:T(8,128)(2,1)S(1)}, bf16[1,48,1024]{2,1,0:T(8,128)(2,1)S(1)}, u32[]{:S(2)}, u32[]{:S(2)}) collective-permute-start(bf16[1,48,1024]{2,1,0:T(8,128)(2,1)S(1)} %bitcast.3), channel_id=1, source_target_pairs={{0,8},{1,9},{2,10},{3,11},{4,12},{5,13},{6,14},{7,15},{8,0},{9,1},... | collective-permute-start | bytes 294920 | tf_op jit(solution)/shard_map/ppermute | solution.py:176
  58.6 12.6 %collective-permute-start = (bf16[1,48,1024]{2,1,0:T(8,128)(2,1)S(1)}, bf16[1,48,1024]{2,1,0:T(8,128)(2,1)S(1)}, u32[]{:S(2)}, u32[]{:S(2)}) collective-permute-start(bf16[1,48,1024]{2,1,0:T(8,128)(2,1)S(1)} %bitcast.4), channel_id=1, source_target_pairs={{0,16},{1,17},{2,18},{3,19},{4,20},{5,21},{6,22},{7,23},{8,24},{9,... | collective-permute-start | bytes 294920 | tf_op jit(solution)/shard_map/ppermute | solution.py:168
  64.1 43.4 %all-to-all-start.1 = ((bf16[16,2,48,512]{3,2,1,0:T(8,128)(2,1)}), bf16[16,2,48,512]{3,2,1,0:T(8,128)(2,1)}, u32[]{:S(2)}, u32[]{:S(2)}) async-start(bf16[16,2,48,512]{3,2,1,0:T(8,128)(2,1)} %shard_map.48), calls=%async_computation.1 | async-start | bytes 3145728 | tf_op jit(solution)/shard_map/all_to_all | solution.py:200
  71.2 4.2 %collective-permute-start.2 = (bf16[2,48,1024]{2,1,0:T(8,128)(2,1)S(1)}, bf16[2,48,1024]{2,1,0:T(8,128)(2,1)S(1)}, u32[]{:S(2)}, u32[]{:S(2)}) collective-permute-start(bf16[2,48,1024]{2,1,0:T(8,128)(2,1)S(1)} %pad_maximum_fusion.2), channel_id=1, source_target_pairs={{0,1},{1,0},{2,3},{3,2},{4,5},{5,4},{6,7},{7,6},{8,9},{9,8},{10,11... | collective-permute-start | bytes 589832 | tf_op jit(solution)/shard_map/ppermute | solution.py:172
  75.4 13.6 %collective-permute-start.3 = (bf16[4,48,1024]{2,1,0:T(8,128)(2,1)S(1)}, bf16[4,48,1024]{2,1,0:T(8,128)(2,1)S(1)}, u32[]{:S(2)}, u32[]{:S(2)}) collective-permute-start(bf16[4,48,1024]{2,1,0:T(8,128)(2,1)S(1)} %pad_maximum_fusion.1.refs_0_), channel_id=1, source_target_pairs={{0,2},{1,15},{2,4},{3,1},{4,6},{5,3},{6,8},{7,5},{8,10},{9,7},{10,... | collective-permute-start | bytes 1179656 | tf_op jit(solution)/shard_map/ppermute | solution.py:176
  79.1 15.2 %collective-permute-start.4 = (bf16[4,48,1024]{2,1,0:T(8,128)(2,1)S(1)}, bf16[4,48,1024]{2,1,0:T(8,128)(2,1)S(1)}, u32[]{:S(2)}, u32[]{:S(2)}) collective-permute-start(bf16[4,48,1024]{2,1,0:T(8,128)(2,1)S(1)} %pad_maximum_fusion.1.refs_0_), channel_id=1, source_target_pairs={{0,4},{1,13},{2,6},{3,15},{4,8},{5,1},{6,10},{7,3},{8,12},{9,5},{1... | collective-permute-start | bytes 1179656 | tf_op jit(solution)/shard_map/ppermute | solution.py:176
  83.8 9.3 %collective-permute-start.6 = (bf16[1,48,1024]{2,1,0:T(8,128)(2,1)S(1)}, bf16[1,48,1024]{2,1,0:T(8,128)(2,1)S(1)}, u32[]{:S(2)}, u32[]{:S(2)}) collective-permute-start(bf16[1,48,1024]{2,1,0:T(8,128)(2,1)S(1)} %collective-permute-done.1.refs_4_), channel_id=1, source_target_pairs={{0,16},{1,17},{2,18},{3,19},{4,20},{5,21},{6,22},{7,23},{8,24},{9,... | collective-permute-start | bytes 294920 | tf_op jit(solution)/shard_map/ppermute | solution.py:168
  89.1 12.6 %collective-permute-start.5 = (bf16[4,48,1024]{2,1,0:T(8,128)(2,1)S(1)}, bf16[4,48,1024]{2,1,0:T(8,128)(2,1)S(1)}, u32[]{:S(2)}, u32[]{:S(2)}) collective-permute-start(bf16[4,48,1024]{2,1,0:T(8,128)(2,1)S(1)} %collective-permute-done.3.refs_1_), channel_id=1, source_target_pairs={{0,4},{1,13},{2,6},{3,15},{4,8},{5,1},{6,10},{7,3},{8,12},{9,5},{1... | collective-permute-start | bytes 1179656 | tf_op jit(solution)/shard_map/ppermute | solution.py:176
  94.4 9.6 %collective-permute-start.8 = (bf16[6,48,1024]{2,1,0:T(8,128)(2,1)S(1)}, bf16[6,48,1024]{2,1,0:T(8,128)(2,1)S(1)}, u32[]{:S(2)}, u32[]{:S(2)}) collective-permute-start(bf16[6,48,1024]{2,1,0:T(8,128)(2,1)S(1)} %pad_maximum_fusion), channel_id=1, source_target_pairs={{0,1},{1,0},{2,3},{3,2},{4,5},{5,4},{6,7},{7,6},{8,9},{9,8},{10,11... | collective-permute-start | bytes 1769480 | tf_op jit(solution)/shard_map/ppermute | solution.py:172
  98.1 5.9 %collective-permute-start.7 = (bf16[4,48,1024]{2,1,0:T(8,128)(2,1)S(1)}, bf16[4,48,1024]{2,1,0:T(8,128)(2,1)S(1)}, u32[]{:S(2)}, u32[]{:S(2)}) collective-permute-start(bf16[4,48,1024]{2,1,0:T(8,128)(2,1)S(1)} %collective-permute-done.3.refs_1_), channel_id=1, source_target_pairs={{0,1},{1,0},{2,3},{3,2},{4,5},{5,4},{6,7},{7,6},{8,9},{9,8},{10,11... | collective-permute-start | bytes 1179656 | tf_op jit(solution)/shard_map/ppermute | solution.py:172
  101.7 3.6 %collective-permute-start.9 = (bf16[4,48,1024]{2,1,0:T(8,128)(2,1)S(1)}, bf16[4,48,1024]{2,1,0:T(8,128)(2,1)S(1)}, u32[]{:S(2)}, u32[]{:S(2)}) collective-permute-start(bf16[4,48,1024]{2,1,0:T(8,128)(2,1)S(1)} %collective-permute-done.5.refs_3_), channel_id=1, source_target_pairs={{0,1},{1,0},{2,3},{3,2},{4,5},{5,4},{6,7},{7,6},{8,9},{9,8},{10,11... | collective-permute-start | bytes 1179656 | tf_op jit(solution)/shard_map/ppermute | solution.py:172
